TPU v7x, 256 devices: a whole 4x4x8 slice. The times are simulated.
256 devices in a mesh: dp: 8 (over x, core), seq: 32 (over y, z).
Axes of the slice: x: 4, y: 4, z: 8, core: 2. Of those that a mesh axis runs over, the one named last changes fastest.
Arguments:
- xbc_in: bfloat16 [8, 8192, 2816], P('dp', 'seq'), may hold values from -4 to 4
- conv_weight: float32 [4, 2816], replicated, may hold values from -3 to 3
- conv_bias: float32 [2816], replicated, may hold values from -3 to 3
- step_sizes: float32 [8, 40, 8192], P('dp', None, 'seq'), may hold values from 0 to 1, as said below
- decay_rates: float32 [40], replicated, may hold values from 0.7 to 1.4
- skip_gain: float32 [40], replicated, may hold values from 0.5 to 1.5
- grad_out: bfloat16 [8, 8192, 2560], P('dp', 'seq'), may hold values from -0.75 to 0.75
Outputs:
- grad_xbc: bfloat16 [8, 8192, 2816], P('dp', 'seq')
- grad_steps: float32 [8, 40, 8192], P('dp', None, 'seq')
- grad_conv_weight: float32 [4, 2816], replicated
- grad_conv_bias: float32 [2816], replicated
- grad_rates: float32 [40], replicated
- grad_skip: float32 [40], replicated
Inputs may be any that keep to these rules, and one draw needn't show every extreme that they name: `step_sizes`: positive step sizes.
All inputs are finite; a program needn't handle non-finite values.
Results may differ from a plain program's by a relative error of at most 0.0056.
Values may be sent and summed in bfloat16 or wider, within the bound.
No kernel may reach another device: no remote copies, remote signals or barrier semaphores. Data moves between devices by JAX's collectives and lax.ppermute only.
A program may use at most 192 MiB of HBM per device.

v0:
```python
import jax
import jax.numpy as jnp
from jax import lax
from jax.sharding import PartitionSpec as P

HEADS = 40
HEAD_DIM = 64
STATE = 128
GROUP = 256
KCONV = 4


def shifted(array, axis, by):
    length = lax.axis_size(axis)
    pairs = [(i, i + by) for i in range(length) if 0 <= i + by < length]
    return lax.ppermute(array, axis, pairs)


def carried_in(array, axis, combine, identity, reverse):
    length, place = (lax.axis_size(axis), lax.axis_index(axis))
    everything = jax.tree.map(lambda part: lax.all_gather(part, axis), array)
    start = jax.tree.map(
        lambda part, zero: jnp.broadcast_to(jnp.asarray(zero, part.dtype), part.shape),
        array,
        identity,
    )

    def lap(k, before):
        at = length - 1 - k if reverse else k
        reached = at > place if reverse else at < place
        new = combine(before, jax.tree.map(lambda part: part[at], everything))
        return jax.tree.map(lambda a, b: jnp.where(reached, a, b), new, before)

    return lax.fori_loop(0, length, lap, start)


def silu_pair(pre_act):
    sigmoid_v = jax.nn.sigmoid(pre_act)
    return (pre_act * sigmoid_v, sigmoid_v * (1.0 + pre_act * (1.0 - sigmoid_v)))


def block_locals(z_block, dy_block, cum_log):
    x_width = HEADS * HEAD_DIM
    b_proj = z_block[:, x_width : x_width + STATE]
    c_proj = z_block[:, x_width + STATE :]
    log_end = cum_log[:, -1:]
    tail_wide = jnp.repeat(jnp.exp(log_end - cum_log).T, HEAD_DIM, axis=1)
    head_wide = jnp.repeat(jnp.exp(cum_log).T, HEAD_DIM, axis=1)
    x_weighted = (z_block[:, :x_width].astype(jnp.float32) * tail_wide).astype(jnp.bfloat16)
    dy_weighted = (dy_block.astype(jnp.float32) * head_wide).astype(jnp.bfloat16)
    contract_rows = (((0,), (0,)), ((), ()))
    s_local = lax.dot_general(x_weighted, b_proj, contract_rows, preferred_element_type=jnp.float32)
    u_local = lax.dot_general(
        dy_weighted, c_proj, contract_rows, preferred_element_type=jnp.float32
    )
    s_local = s_local.reshape(HEADS, HEAD_DIM, STATE)
    u_local = u_local.reshape(HEADS, HEAD_DIM, STATE)
    return (s_local, u_local, x_weighted, dy_weighted)


def block_grads(
    z_block, dy_block, cum_log, x_weighted, dy_weighted, start_state, end_adjoint, skip_gain
):
    x_width = HEADS * HEAD_DIM
    x_flat = z_block[:, :x_width]
    b_proj = z_block[:, x_width : x_width + STATE]
    c_proj = z_block[:, x_width + STATE :]
    log_end = cum_log[:, -1:]
    contract_last = (((1,), (1,)), ((), ()))
    gram_bc = lax.dot_general(b_proj, c_proj, contract_last, preferred_element_type=jnp.float32)
    row_index = lax.broadcasted_iota(jnp.int32, (GROUP, GROUP), 0)
    col_index = lax.broadcasted_iota(jnp.int32, (GROUP, GROUP), 1)
    causal = (row_index >= col_index)[None]
    upper = (row_index <= col_index)[None]
    log_gap = cum_log[:, :, None] - cum_log[:, None, :]
    decay_lower = jnp.where(causal, jnp.exp(jnp.where(causal, log_gap, 0.0)), 0.0)
    rise_gap = cum_log[:, None, :] - cum_log[:, :, None]
    decay_upper = jnp.where(upper, jnp.exp(jnp.where(upper, rise_gap, 0.0)), 0.0)
    x_heads = x_flat.reshape(GROUP, HEADS, HEAD_DIM)
    dy_heads = dy_block.reshape(GROUP, HEADS, HEAD_DIM)
    inner_dx = jnp.einsum("thp,shp->hts", dy_heads, x_heads, preferred_element_type=jnp.float32)
    weights = decay_lower * inner_dx
    k_matrix = (decay_upper * gram_bc[None]).astype(jnp.bfloat16)
    m_terms = weights * gram_bc.T[None]
    w_summed = jnp.sum(weights, axis=0).astype(jnp.bfloat16)
    states_low = start_state.astype(jnp.bfloat16).reshape(x_width, STATE)
    adjoint_low = end_adjoint.astype(jnp.bfloat16).reshape(x_width, STATE)
    b_adjoint = lax.dot_general(
        b_proj, adjoint_low, contract_last, preferred_element_type=jnp.float32
    )
    tail_wide = jnp.repeat(jnp.exp(log_end - cum_log).T, HEAD_DIM, axis=1)
    intra_dx = jnp.einsum("hts,shp->thp", k_matrix, dy_heads, preferred_element_type=jnp.float32)
    dx_state = intra_dx.reshape(GROUP, x_width) + tail_wide * b_adjoint
    contract_rows = (((0,), (0,)), ((), ()))
    grad_bproj = lax.dot_general(
        w_summed, c_proj, contract_rows, preferred_element_type=jnp.float32
    )
    grad_bproj = grad_bproj + jnp.dot(x_weighted, adjoint_low, preferred_element_type=jnp.float32)
    grad_cproj = jnp.dot(w_summed, b_proj, preferred_element_type=jnp.float32)
    grad_cproj = grad_cproj + jnp.dot(dy_weighted, states_low, preferred_element_type=jnp.float32)
    c_state = lax.dot_general(c_proj, states_low, contract_last, preferred_element_type=jnp.float32)
    x_float = x_flat.astype(jnp.float32)
    dy_float = dy_block.astype(jnp.float32)
    q_terms = jnp.sum((c_state * dy_float).reshape(GROUP, HEADS, HEAD_DIM), axis=2).T
    r_terms = jnp.sum((b_adjoint * x_float).reshape(GROUP, HEADS, HEAD_DIM), axis=2).T
    col_sums = jnp.sum(m_terms, axis=1)
    row_sums = jnp.sum(m_terms, axis=2)
    term_one = jnp.cumsum(col_sums - row_sums, axis=1) + row_sums
    term_two = jnp.flip(jnp.cumsum(jnp.flip(jnp.exp(cum_log) * q_terms, 1), axis=1), 1)
    term_three = jnp.cumsum(jnp.exp(log_end - cum_log) * r_terms, axis=1)
    term_four = jnp.exp(log_end) * jnp.sum(end_adjoint * start_state, axis=(1, 2))[:, None]
    own_terms = jnp.sum((x_float * dx_state).reshape(GROUP, HEADS, HEAD_DIM), axis=2).T
    grad_log = term_one + term_two + term_three + term_four - own_terms
    dx_full = dx_state + jnp.repeat(skip_gain, HEAD_DIM)[None, :] * dy_float
    grad_z = jnp.concatenate([dx_full, grad_bproj, grad_cproj], axis=1)
    return (grad_z, grad_log)


def compose(earlier, later):
    return (earlier[0] * later[0], later[0][:, :, None, None] * earlier[1] + later[1])


def shards(xbc_in, conv_weight, conv_bias, step_sizes, decay_rates, skip_gain, grad_out):
    seq_count, tokens, channels = xbc_in.shape
    rim_len = KCONV - 1
    x_width = HEADS * HEAD_DIM
    block_count = tokens // GROUP
    before = shifted(xbc_in[:, tokens - rim_len :, :], "seq", 1)
    padded_in = jnp.concatenate([before, xbc_in], axis=1)
    pre_act = jnp.zeros((seq_count, tokens, channels), jnp.float32) + conv_bias[None, None, :]
    for tap_index in range(KCONV):
        pre_act = pre_act + conv_weight[tap_index][None, None, :] * padded_in[
            :, tap_index : tap_index + tokens
        ].astype(jnp.float32)
    activated, derivative = silu_pair(pre_act)
    z_seq = activated.astype(jnp.bfloat16)
    skip_terms = (z_seq[:, :, :x_width].astype(jnp.float32) * grad_out.astype(jnp.float32)).reshape(
        seq_count, tokens, HEADS, HEAD_DIM
    )
    local_skip = jnp.sum(skip_terms, axis=(0, 1, 3))
    log_steps = -(step_sizes * decay_rates[None, :, None])
    cum_log = jnp.cumsum(log_steps.reshape(seq_count, HEADS, block_count, GROUP), axis=3)
    locals_fn = jax.vmap(block_locals)
    grads_fn = jax.vmap(block_grads, in_axes=(0, 0, 0, 0, 0, 0, 0, None))
    block_index = 0
    z_parts = [z_seq]
    dy_parts = [grad_out]
    log_parts = [cum_log[:, :, block_index]]
    local_items = [locals_fn(z_parts[block_index], dy_parts[block_index], log_parts[block_index])]
    decay_ends = [jnp.exp(log_parts[block_index][:, :, -1])]
    dev_decay = jnp.ones((seq_count, HEADS), jnp.float32)
    dev_state = jnp.zeros((seq_count, HEADS, HEAD_DIM, STATE), jnp.float32)
    dev_adjoint = jnp.zeros((seq_count, HEADS, HEAD_DIM, STATE), jnp.float32)
    block_index = 0
    dev_state = decay_ends[block_index][:, :, None, None] * dev_state + local_items[block_index][0]
    dev_decay = dev_decay * decay_ends[block_index]
    for block_index in reversed(range(block_count)):
        dev_adjoint = (
            decay_ends[block_index][:, :, None, None] * dev_adjoint + local_items[block_index][1]
        )
    identity_pair = (jnp.ones_like(dev_decay), jnp.zeros_like(dev_state))
    enter_pair = carried_in((dev_decay, dev_state), "seq", compose, identity_pair, False)
    leave_pair = carried_in((dev_decay, dev_adjoint), "seq", compose, identity_pair, True)
    entering = enter_pair[1]
    leaving = leave_pair[1]
    block_index = 0
    block_starts = [entering]
    adjoint_run = leaving
    block_ends = [adjoint_run] * block_count
    for block_index in reversed(range(block_count)):
        block_ends[block_index] = adjoint_run
        adjoint_run = (
            decay_ends[block_index][:, :, None, None] * adjoint_run + local_items[block_index][1]
        )
    block_index = 0
    grad_piece, log_piece = grads_fn(
        z_parts[block_index],
        dy_parts[block_index],
        log_parts[block_index],
        local_items[block_index][2],
        local_items[block_index][3],
        block_starts[block_index],
        block_ends[block_index],
        skip_gain,
    )
    grad_pre = grad_piece * derivative
    next_rows = shifted(grad_pre[:, :rim_len], "seq", -1)
    padded_grad = jnp.concatenate([grad_pre, next_rows], axis=1)
    grad_in = jnp.zeros((seq_count, tokens, channels), jnp.float32)
    for tap_index in range(KCONV):
        tap_start = rim_len - tap_index
        grad_in = (
            grad_in
            + conv_weight[tap_index][None, None, :] * padded_grad[:, tap_start : tap_start + tokens]
        )
    grad_taps = []
    for tap_index in range(KCONV):
        grad_taps.append(
            jnp.sum(
                grad_pre * padded_in[:, tap_index : tap_index + tokens].astype(jnp.float32),
                axis=(0, 1),
            )
        )
    local_weight = jnp.stack(grad_taps)
    local_bias = jnp.sum(grad_pre, axis=(0, 1))
    local_rates = -jnp.sum(step_sizes * log_piece, axis=(0, 2))
    grad_steps = -decay_rates[None, :, None] * log_piece
    grad_weight, grad_bias, grad_rates, grad_skip = lax.psum(
        (local_weight, local_bias, local_rates, local_skip), ("dp", "seq")
    )
    return (grad_in.astype(jnp.bfloat16), grad_steps, grad_weight, grad_bias, grad_rates, grad_skip)


def solution(mesh):
    return jax.shard_map(
        shards,
        mesh=mesh,
        in_specs=(
            P("dp", "seq", None),
            P(),
            P(),
            P("dp", None, "seq"),
            P(),
            P(),
            P("dp", "seq", None),
        ),
        out_specs=(P("dp", "seq", None), P("dp", None, "seq"), P(), P(), P(), P()),
        check_vma=False,
    )
```

profile of v0, /device:TPU:32, one launch (start us, length us, event | category | flops | bytes accessed | tf_op | source)
XLA Modules:
  0.0 851.5 jit_solution(11088155959320751652)
XLA Ops:
  8.0 3.8 collective-permute-start
  15.5 3.3 copy.237
  18.9 2.0 fusion.64
  22.6 4.4 multiply_convert_fusion.2
  33.9 3.3 copy.244
  37.2 3.2 copy.241
  40.4 40.6 %all-gather = f32[32,40,1]{1,2,0:T(1,128)S(1)} all-gather(f32[1,40,1]{1,2,0:T(1,128)S(1)} %get-tuple-element.427), channel_id=2, replica_groups=mesh['dp'=8,'seq'=32] {'seq'}, dimensions={0}, use_global_device_ids=true | all-gather | bytes 5280 | tf_op jit(solution)/shard_map/all_gather | solution.py:21
  82.3 5.4 fusion.2
  87.7 3.3 copy.242
  91.0 221.7 %all-gather.6.cloned.1.call-done = f32[1280,64,128]{2,1,0:T(8,128)} async-done(((f32[40,64,128]{2,1,0:T(8,128)}), f32[1280,64,128]{2,1,0:T(8,128)}) %all-gather.6.cloned.1.call-update) | async-done | bytes 41943056 | tf_op jit(solution)/shard_map/all_gather | solution.py:21
  312.6 53.4 %while.30 = (s32[]{:T(128)}, f32[1,40,64,128]{3,2,1,0:T(8,128)S(1)}, s32[]{:T(128)}, f32[32,1,40]{2,1,0:T(1,128)S(1)}, f32[32,1,40,64,128]{4,3,2,1,0:T(8,128)}, ...) while((s32[]{:T(128)}, f32[1,40,64,128]{3,2,1,0:T(8,128)S(1)}, s32[]{:T(128)}, ...), condition=%wide.region_3.4_spmd.clone, body=%wide.region_2.3_spmd.clone.sunk | while | flops 1310728 | bytes 3932815 | solution.py:34
  366.7 8.9 %convert_multiply_fusion.1 = (f32[1,256,2560]{2,1,0:T(8,128)}, f32[1,256,2560]{2,1,0:T(8,128)}, f32[1,256,2560]{2,1,0:T(8,128)}, f32[2560]{0:T(1024)}, bf16[2560,256]{0,1:T(8,128)(2,1)}) fusion(f32[256,2560]{1,0:T(8,128)} %copy.242, f32[256,2560]{1,0:T(8,128)} %copy.241, bf16[1,256,2816]{2,1,0:T(8,128)(2,1)} %copy-done.2, ...), kind=kOutput, calls=%fused_computation.17 | convolution fusion | flops 175633920 | bytes 20402176 | tf_op jit(solution)/shard_map/vmap()/dot_general | solution.py:88
  377.2 2.4 convolution_add_fusion
  380.9 2.5 slice.117
  383.3 2.4 copy.243
  385.7 7.2 multiply_reduce_fusion.1
  397.0 1.9 reduce-window.30
  404.5 3.2 copy.265
  407.7 2.7 reduce_sum.150
  412.6 3.3 copy.260
  415.9 2.7 reduce_sum.147
  420.2 2.6 fusion.32
  423.8 236.0 %all-gather.8.cloned.1.call-done = f32[1280,64,128]{2,1,0:T(8,128)} async-done(((f32[40,64,128]{2,1,0:T(8,128)}), f32[1280,64,128]{2,1,0:T(8,128)}) %all-gather.8.cloned.1.call-update) | async-done | bytes 41943056 | tf_op jit(solution)/shard_map/all_gather | solution.py:21
  659.8 72.8 %while.31 = (s32[]{:T(128)}, f32[1,40,64,128]{3,2,1,0:T(8,128)S(1)}, s32[]{:T(128)}, f32[32,1,40]{2,1,0:T(1,128)}, f32[32,1,40,64,128]{4,3,2,1,0:T(8,128)}, /*index=5*/s32[]{:T(128)}, s32[]{:T(128)}) while((s32[]{:T(128)}, f32[1,40,64,128]{3,2,1,0:T(8,128)S(1)}, s32[]{:T(128)}, f32[32,1,40]{2,1,0:T(1,128)}, ...), condition=%wide.region_6.7_spmd.clone, body=%wide.region_5.6_spmd.clone.sunk | while | flops 1310724 | bytes 3932753 | solution.py:34
  733.9 2.3 fusion.34
  736.2 2.9 convert_multiply_fusion.4
  739.0 3.3 copy.255
  742.4 2.1 reduce_sum.145
  747.9 5.6 fusion.13
  755.1 4.1 collective-permute-start.1
  761.7 76.1 %all-reduce = (f32[4,2816]{1,0:T(4,128)}, f32[2816]{0:T(1024)}, f32[40]{0:T(128)}, f32[40]{0:T(128)}) all-reduce(f32[4,2816]{1,0:T(4,128)S(1)} %pad_maximum_fusion.2, f32[2816]{0:T(1024)S(1)} %get-tuple-element.383, f32[40]{0:T(128)S(1)} %neg.16, f32[40]{0:T(128)S(1)} %reduce_sum.160), channel_id=1, replica_groups=mesh['dp'=8,'seq'=32] {'dp','seq'}, use_global_device_ids=true, to_apply=%region_23.24 | all-reduce | flops 14160 | bytes 113280 | tf_op jit(solution)/shard_map/psum | solution.py:208
  837.8 6.8 fusion.22
  (286 shorter events, 164.6 us)
Async XLA Ops:
  7.2 305.5 %all-gather.6.cloned.1.call-start = ((), (), s32[]{:S(2)}) async-start(), calls=%async_computation | async-start | bytes 43253760 | tf_op jit(solution)/shard_map/all_gather | solution.py:21
  8.0 14.5 %collective-permute-start = (bf16[1,3,2816]{2,1,0:T(4,128)(2,1)S(1)}, bf16[1,3,2816]{2,1,0:T(4,128)(2,1)S(1)}, u32[]{:S(2)}, u32[]{:S(2)}) collective-permute-start(bf16[1,3,2816]{2,1,0:T(4,128)(2,1)S(1)} %slice.88), channel_id=1, source_target_pairs={{0,1},{1,2},{2,3},{3,4},{4,5},{5,6},{6,7},{7,8},{8,9},{9,10},{10,1... | collective-permute-start | bytes 50696 | tf_op jit(solution)/shard_map/ppermute | solution.py:16
  15.5 3.3 copy-start
  18.9 2.0 copy-start.25
  20.9 1.6 copy-start.22
  21.1 5.9 copy-start.8
  21.1 5.9 copy-start.10
  21.1 5.9 copy-start.12
  22.6 5.5 copy-start.5
  22.6 7.1 copy-start.19
  29.7 630.0 %all-gather.8.cloned.1.call-start = ((), (), s32[]{:S(2)}) async-start(), calls=%async_computation.1 | async-start | bytes 43253760 | tf_op jit(solution)/shard_map/all_gather | solution.py:21
  32.1 5.1 copy-start.28
  81.0 6.6 copy-start.26
  82.1 5.6 copy-start.6
  312.6 54.1 %copy-start.24 = (f32[2560]{0:T(1024)S(1)}, f32[2560]{0:T(1024)}, u32[]{:S(2)}) copy-start(f32[2560]{0:T(1024)} %mul.264) | copy-start | bytes 30724
  377.2 2.5 copy-start.30
  742.3 2.3 copy-start.7
  742.3 2.3 copy-start.29
  742.3 5.5 copy-start.33
  742.3 5.5 copy-start.4
  742.3 5.5 copy-start.9
  742.3 5.5 copy-start.11
  742.3 5.5 copy-start.13
  742.3 5.5 copy-start.20
  742.4 5.5 copy-start.23
  747.9 12.2 %copy-start.21 = (f32[40,2]{1,0:T(8,128)S(1)}, f32[40,2]{1,0:T(8,128)}, u32[]{:S(2)}) copy-start(f32[40,2]{1,0:T(8,128)} %copy.254) | copy-start | bytes 964
  747.9 12.4 %copy-start.14 = (f32[1,40,256]{2,1,0:T(8,128)S(1)}, f32[1,40,256]{2,1,0:T(8,128)}, u32[]{:S(2)}) copy-start(f32[1,40,256]{2,1,0:T(8,128)} %param.14) | copy-start | bytes 122884
  747.9 12.4 %copy-start.15 = (f32[1,40,2,128]{3,2,0,1:T(2,128)S(1)}, f32[1,40,2,128]{3,2,0,1:T(2,128)}, u32[]{:S(2)}) copy-start(f32[1,40,2,128]{3,2,0,1:T(2,128)} %copy.253) | copy-start | bytes 122884
  747.9 12.4 %copy-start.17 = (f32[40,256]{1,0:T(8,128)S(1)}, f32[40,256]{1,0:T(8,128)}, u32[]{:S(2)}) copy-start(f32[40,256]{1,0:T(8,128)} %copy-done.16) | copy-start | bytes 122884
  747.9 12.4 %copy-start.18 = (f32[256,40]{0,1:T(8,128)S(1)}, f32[256,40]{0,1:T(8,128)}, u32[]{:S(2)}) copy-start(f32[256,40]{0,1:T(8,128)} %reduce_sum.150) | copy-start | bytes 122884
  747.9 13.0 %copy-start.31 = (f32[40]{0:T(128)S(1)}, f32[40]{0:T(128)}, u32[]{:S(2)}) copy-start(f32[40]{0:T(128)} %neg.15) | copy-start | bytes 484
  755.1 82.7 %collective-permute-start.1 = (f32[1,3,2816]{2,1,0:T(4,128)S(1)}, f32[1,3,2816]{2,1,0:T(4,128)S(1)}, u32[]{:S(2)}, u32[]{:S(2)}) collective-permute-start(f32[1,3,2816]{2,1,0:T(4,128)S(1)} %slice.118), channel_id=1, source_target_pairs={{1,0},{2,1},{3,2},{4,3},{5,4},{6,5},{7,6},{8,7},{9,8},{10,9},{11,1... | collective-permute-start | bytes 101384 | tf_op jit(solution)/shard_map/ppermute | solution.py:16
  (6 other events, 6.7 us)
Sparse Core Ops, SparseCore 0:
  29.8 282.7 all-gather.5
  379.8 279.8 all-gather.7
where the time goes:
time: 856 us; the launch traced here: 852 us
  waiting for transfers between devices  458 us (54%)
  other arithmetic  140 us (16%)
  blocking collectives  117 us (14%)
  local copies, waits for them, and re-layouts  75.7 us (9%)
  matrix products  36.5 us (4%)
  between operations  14.8 us (2%)
    all_gather x2, waiting for transfers between devices, carried_in(): everything = jax.tree.map(lambda part: lax.all_gather(part, axis), array)  458 us
    select_n x64, other arithmetic, lap(): return jax.tree.map(lambda a, b: jnp.where(reached, a, b), new, before)  104 us
    psum x1, blocking collectives, shards(): lax.psum((local_weight, local_bias, local_rates, local_skip), ('dp', 'seq'))  76.1 us
    all_gather x1, blocking collectives, carried_in(): everything = jax.tree.map(lambda part: lax.all_gather(part, axis), array)  40.6 us
    mul x64, local copies, waits for them, and re-layouts, compose(): later[0][:, :, None, None] * earlier[1] + later[1]  20.6 us
  transfers between devices with their start and end apart: 4, of which 2 were waited for; matrix products, arithmetic and copies ran while one was open for 9% of the time, Pallas kernels for 0%

commit v1 on v0

v1 whole, which is shorter than its diff:
```python
import functools

import jax
import jax.numpy as jnp
from jax import lax
from jax.experimental import pallas as pl
from jax.experimental.pallas import tpu as pltpu
from jax.sharding import PartitionSpec as P

HEADS = 40
HEAD_DIM = 64
STATE = 128
GROUP = 256
KCONV = 4
LANE = 128
BF16 = jnp.bfloat16
F32 = jnp.float32
X_WIDTH = HEADS * HEAD_DIM
PAIRS = HEADS // 2
TAIL_ROWS = 16
VMEM_LIMIT = 56 * 1024 * 1024
HIGH = lax.Precision.HIGHEST


def mm(a, b, ca=1, cb=0, precision=None):
    return lax.dot_general(
        a, b, (((ca,), (cb,)), ((), ())), preferred_element_type=F32, precision=precision
    )


def lanes(c):
    return pl.ds(pl.multiple_of(c * LANE, LANE), LANE)


def taps_of(x_ref, halo_ref, c):
    full = jnp.concatenate(
        [
            jnp.zeros((8 - (KCONV - 1), LANE), F32),
            halo_ref[:, lanes(c)].astype(F32),
            x_ref[:, lanes(c)].astype(F32),
        ],
        axis=0,
    )
    return [full[5 + k : 5 + k + GROUP] for k in range(KCONV)]


def front_kernel(
    x_ref, halo_ref, w_ref, bias_ref, step_ref, rate_ref, dy_ref,
    zt_ref, bc_ref, dyt_ref, deriv_ref, cum_ref, msg_ref,
    tail_ref, head_ref, *, chunks, rows,
):
    tiles = X_WIDTH // LANE + 2

    def conv(c, carry):
        taps = taps_of(x_ref, halo_ref, c)
        pre = bias_ref[:, lanes(c)]
        for k in range(KCONV):
            pre = pre + w_ref[k : k + 1, lanes(c)] * taps[k]
        sig = jax.nn.sigmoid(pre)
        deriv_ref[:, lanes(c)] = sig * (1.0 + pre * (1.0 - sig))
        z = (pre * sig).astype(BF16)
        zt_ref[lanes(c), :] = z.astype(F32).T.astype(BF16)

        @pl.when(c >= PAIRS)
        def _():
            bc_ref[:, lanes(c - PAIRS)] = z

        return carry

    lax.fori_loop(0, tiles, conv, 0)

    def turn(c, carry):
        dyt_ref[lanes(c), :] = dy_ref[:, lanes(c)].astype(F32).T.astype(BF16)
        return carry

    lax.fori_loop(0, PAIRS, turn, 0)

    logs = -(step_ref[...] * rate_ref[...])
    row = lax.broadcasted_iota(jnp.int32, (GROUP, GROUP), 0)
    col = lax.broadcasted_iota(jnp.int32, (GROUP, GROUP), 1)
    upto = jnp.where(row <= col, 1.0, 0.0).astype(F32)
    cum = mm(logs, upto, precision=HIGH)
    cum_ref[...] = cum
    log_end = cum[:, GROUP - 1 : GROUP]
    tail_ref[...] = jnp.exp(log_end - cum)
    head_ref[...] = jnp.exp(cum)

    d_end = jnp.broadcast_to(jnp.exp(log_end), (HEADS, LANE))
    part_a = d_end.astype(BF16).astype(F32)
    part_b = (d_end - part_a).astype(BF16).astype(F32)
    part_c = (d_end - part_a - part_b).astype(BF16).astype(F32)
    blank = jnp.zeros((TAIL_ROWS - 6, LANE), F32)
    for j in range(chunks):
        first = rows * j // HEAD_DIM
        last = (rows * j + rows - 1) // HEAD_DIM
        picked = [p[h : h + 1] for h in (first, last) for p in (part_a, part_b, part_c)]
        msg_ref[j, 2 * rows :, :] = jnp.concatenate(picked + [blank], axis=0).astype(BF16)

    b_proj = bc_ref[:, :STATE]
    c_proj = bc_ref[:, STATE:]
    per = 5
    span = per * HEAD_DIM
    each = span // rows

    def local(g, carry):
        for source, scale, proj, at in (
            (zt_ref, tail_ref, b_proj, 0),
            (dyt_ref, head_ref, c_proj, rows),
        ):
            parts = []
            for i in range(per):
                start = pl.multiple_of(g * span + i * HEAD_DIM, HEAD_DIM)
                wide = source[pl.ds(start, HEAD_DIM), :].astype(F32)
                parts.append((wide * scale[pl.ds(g * per + i, 1), :]).astype(BF16))
            found = mm(jnp.concatenate(parts, axis=0), proj).astype(BF16)
            for i in range(each):
                msg_ref[g * each + i, at : at + rows, :] = found[i * rows : (i + 1) * rows]
        return carry

    lax.fori_loop(0, HEADS // per, local, 0)


def within_kernel(
    zt_ref, bc_ref, dyt_ref, dy_ref, cum_ref,
    intra_ref, gbt_ref, gct_ref, col_ref, row_ref,
    column_ref, wsum_ref, cb_ref, hold_ref,
):
    hold_ref[...] = jnp.zeros_like(hold_ref)
    hold_ref[:HEADS, :] = cum_ref[...]
    turned = hold_ref[...].T
    for h in range(HEADS):
        column_ref[h] = jnp.broadcast_to(turned[:, h : h + 1], (GROUP, LANE))
    wsum_ref[...] = jnp.zeros_like(wsum_ref)
    bt = zt_ref[X_WIDTH : X_WIDTH + STATE, :]
    ct = zt_ref[X_WIDTH + STATE :, :]
    cb_ref[...] = mm(bc_ref[:, STATE:], bt)
    t_index = lax.broadcasted_iota(jnp.int32, (GROUP, GROUP), 0)
    s_index = lax.broadcasted_iota(jnp.int32, (GROUP, GROUP), 1)
    causal = t_index >= s_index

    def pair(c, carry):
        dy_pair = dy_ref[:, lanes(c)]
        xt_pair = zt_ref[lanes(c), :]
        dyt_pair = dyt_ref[lanes(c), :]
        zero = jnp.zeros((HEAD_DIM, GROUP), BF16)
        total = wsum_ref[...]
        for i in range(2):
            h = 2 * c + i
            xt = xt_pair[i * HEAD_DIM : (i + 1) * HEAD_DIM]
            dyt = dyt_pair[i * HEAD_DIM : (i + 1) * HEAD_DIM]
            wide = jnp.concatenate([xt, zero] if i == 0 else [zero, xt], axis=0)
            inner = mm(dy_pair, wide)
            column = column_ref[h]
            column = jnp.concatenate([column, column], axis=1)
            gap = column - cum_ref[pl.ds(h, 1), :]
            decay = jnp.exp(jnp.where(causal, gap, -jnp.inf))
            total = total + decay * inner
            kt = (decay * cb_ref[...]).astype(BF16)
            intra = mm(dyt, kt)
            forth = mm(xt, kt, 1, 1)
            intra_ref[pl.ds(pl.multiple_of(h * HEAD_DIM, HEAD_DIM), HEAD_DIM), :] = intra
            col_ref[pl.ds(h, 1), :] = jnp.sum(intra * xt.astype(F32), axis=0, keepdims=True)
            row_ref[pl.ds(h, 1), :] = jnp.sum(forth * dyt.astype(F32), axis=0, keepdims=True)
        wsum_ref[...] = total
        return carry

    lax.fori_loop(0, PAIRS, pair, 0)
    w_summed = wsum_ref[...].astype(BF16)
    gbt_ref[...] = mm(ct, w_summed)
    gct_ref[...] = mm(bt, w_summed, 1, 1)


def chain_kernel(got_ref, out_ref, *, chunks, rows):
    j = lax.axis_index("seq")
    split = HEAD_DIM - lax.rem(rows * j, HEAD_DIM)
    ahead = lax.broadcasted_iota(jnp.int32, (rows, LANE), 0) < split

    def decay_of(i):
        ends = got_ref[i, 2 * rows :, :].astype(F32)
        one = ends[0:1] + ends[1:2] + ends[2:3]
        two = ends[3:4] + ends[4:5] + ends[5:6]
        return jnp.where(ahead, one, two)

    def step(k, carry):
        state, adjoint = carry
        out_ref[k, :rows, :] = state.astype(BF16)
        state = decay_of(k) * state + got_ref[k, :rows, :].astype(F32)
        m = chunks - 1 - k
        out_ref[m, rows:, :] = adjoint.astype(BF16)
        adjoint = decay_of(m) * adjoint + got_ref[m, rows : 2 * rows, :].astype(F32)
        return state, adjoint

    zero = jnp.zeros((rows, LANE), F32)
    lax.fori_loop(0, chunks, step, (zero, zero))


def back_kernel(
    back_ref, zt_ref, dyt_ref, cum_ref, intra_ref, gbt_ref, gct_ref, colin_ref, row_ref,
    deriv_ref, x_ref, halo_ref, step_ref, rate_ref, skip_ref,
    gpre_ref, edge_ref, gsteps_ref, params_ref,
    st_ref, ad_ref, tail_ref, head_ref, q_ref, r_ref, skiprow_ref, four_ref, gb_ref, gc_ref, sums_ref, flip_ref,
    *, chunks, rows,
):
    for j in range(chunks):
        st_ref[j * rows : (j + 1) * rows, :] = back_ref[j, :rows, :]
        ad_ref[j * rows : (j + 1) * rows, :] = back_ref[j, rows:, :]
    cum = cum_ref[...]
    log_end = cum[:, GROUP - 1 : GROUP]
    tail_ref[...] = jnp.exp(log_end - cum)
    head_ref[...] = jnp.exp(cum)
    bt = zt_ref[X_WIDTH : X_WIDTH + STATE, :]
    ct = zt_ref[X_WIDTH + STATE :, :]
    gb_ref[...] = gbt_ref[...]
    gc_ref[...] = gct_ref[...]

    def finish(c, grad_t):
        grad = grad_t.T * deriv_ref[:, lanes(c)]
        gpre_ref[:, lanes(c)] = grad
        edge_ref[:, lanes(c)] = grad[:8]
        taps = taps_of(x_ref, halo_ref, c)
        found = [jnp.sum(grad * tap, axis=0, keepdims=True) for tap in taps]
        found.append(jnp.sum(grad, axis=0, keepdims=True))
        found.append(jnp.zeros((8 - len(found), LANE), F32))
        sums_ref[c] = jnp.concatenate(found, axis=0)

    def pair(c, carry):
        xt = zt_ref[lanes(c), :]
        dyt = dyt_ref[lanes(c), :]
        xf = xt.astype(F32)
        dyf = dyt.astype(F32)
        states = st_ref[lanes(c), :]
        adjoint = ad_ref[lanes(c), :]
        c_state = mm(states, ct)
        b_adj = mm(adjoint, bt)
        both = states.astype(F32) * adjoint.astype(F32)
        tails, heads, skips = [], [], []
        for i in range(2):
            h = 2 * c + i
            part = slice(i * HEAD_DIM, (i + 1) * HEAD_DIM)
            at = pl.ds(h, 1)
            tails.append(jnp.broadcast_to(tail_ref[at, :], (HEAD_DIM, GROUP)))
            heads.append(jnp.broadcast_to(head_ref[at, :], (HEAD_DIM, GROUP)))
            skips.append(jnp.full((HEAD_DIM, GROUP), skip_ref[h], F32))
            q_ref[at, :] = jnp.sum((c_state * dyf)[part], axis=0, keepdims=True)
            r_ref[at, :] = jnp.sum((b_adj * xf)[part], axis=0, keepdims=True)
            skiprow_ref[at, :] = jnp.sum((xf * dyf)[part], axis=0, keepdims=True)
            four_ref[at, :] = jnp.sum(both[part], axis=0, keepdims=True)
        tail = jnp.concatenate(tails, axis=0)
        head = jnp.concatenate(heads, axis=0)
        skip = jnp.concatenate(skips, axis=0)
        gb_ref[...] += mm(adjoint, (xf * tail).astype(BF16), 0, 0)
        gc_ref[...] += mm(states, (dyf * head).astype(BF16), 0, 0)
        finish(c, intra_ref[lanes(c), :] + tail * b_adj + skip * dyf)
        return carry

    lax.fori_loop(0, PAIRS, pair, 0)
    finish(PAIRS, gb_ref[...])
    finish(PAIRS + 1, gc_ref[...])

    row_i = lax.broadcasted_iota(jnp.int32, (GROUP, GROUP), 0)
    col_i = lax.broadcasted_iota(jnp.int32, (GROUP, GROUP), 1)
    upto = jnp.where(row_i <= col_i, 1.0, 0.0).astype(F32)
    since = jnp.where(row_i >= col_i, 1.0, 0.0).astype(F32)
    col_sums = colin_ref[...]
    row_sums = row_ref[...]
    tail_r = tail_ref[...] * r_ref[...]
    running = mm(col_sums - row_sums + tail_r, upto, precision=HIGH)
    ending = mm(head_ref[...] * q_ref[...], since, precision=HIGH)
    four = jnp.exp(log_end) * jnp.sum(four_ref[...], axis=1, keepdims=True)
    grad_log = running + row_sums + ending + four - col_sums - tail_r
    gsteps_ref[...] = -rate_ref[...] * grad_log
    rates = -jnp.sum(step_ref[...] * grad_log, axis=1, keepdims=True)
    skips = jnp.sum(skiprow_ref[...], axis=1, keepdims=True)
    flip_ref[...] = jnp.zeros_like(flip_ref)
    lane = lax.broadcasted_iota(jnp.int32, (HEADS, LANE), 1)
    flip_ref[:HEADS, :] = jnp.where(lane == 0, rates, 0.0) + jnp.where(lane == 1, skips, 0.0)
    tiles = PAIRS + 2
    for c in range(tiles):
        sums = sums_ref[c]
        for k in range(KCONV + 1):
            at = k * tiles + c
            params_ref[at : at + 1, :] = sums[k : k + 1]
    at = (KCONV + 1) * tiles
    params_ref[at : at + 2, :] = flip_ref[...].T[:2]


def spread_kernel(gpre_ref, next_ref, w_ref, out_ref):
    rim = KCONV - 1

    def tile(c, carry):
        full = jnp.concatenate(
            [gpre_ref[:, lanes(c)], next_ref[:, lanes(c)]], axis=0
        )
        total = w_ref[rim : rim + 1, lanes(c)] * full[:GROUP]
        for k in range(rim):
            start = rim - k
            total = total + w_ref[k : k + 1, lanes(c)] * full[start : start + GROUP]
        out_ref[:, lanes(c)] = total.astype(BF16)
        return carry

    lax.fori_loop(0, X_WIDTH // LANE + 2, tile, 0)


def call(kernel, outs, scratch, *operands, in_specs=None):
    extra = {} if in_specs is None else {"in_specs": in_specs}
    return pl.pallas_call(
        kernel,
        out_shape=[jax.ShapeDtypeStruct(shape, dtype) for shape, dtype in outs],
        scratch_shapes=[pltpu.VMEM(shape, dtype) for shape, dtype in scratch],
        compiler_params=pltpu.CompilerParams(vmem_limit_bytes=VMEM_LIMIT),
        **extra,
    )(*operands)


def shifted(array, axis, by):
    length = lax.axis_size(axis)
    pairs = [(i, i + by) for i in range(length) if 0 <= i + by < length]
    return lax.ppermute(array, axis, pairs)


def total_over_devices(array):
    for axis in ("dp", "seq"):
        length = lax.axis_size(axis)
        bit = 1
        while bit < length:
            array = array + lax.ppermute(array, axis, [(i, i ^ bit) for i in range(length)])
            bit *= 2
    return array


def shards(xbc_in, conv_weight, conv_bias, step_sizes, decay_rates, skip_gain, grad_out):
    channels = xbc_in.shape[2]
    rim = KCONV - 1
    chunks = lax.axis_size("seq")
    rows = X_WIDTH // chunks
    x_in = xbc_in[0]
    dy = grad_out[0]
    steps = step_sizes[0]
    rates = decay_rates.reshape(HEADS, 1)
    halo = shifted(x_in[GROUP - rim :], "seq", 1)
    wide_heads = (HEADS, GROUP)
    zt, bc, dyt, deriv, cum, msg = call(
        functools.partial(front_kernel, chunks=chunks, rows=rows),
        [
            ((channels, GROUP), BF16),
            ((GROUP, 2 * STATE), BF16),
            ((X_WIDTH, GROUP), BF16),
            ((GROUP, channels), F32),
            (wide_heads, F32),
            ((chunks, 2 * rows + TAIL_ROWS, LANE), BF16),
        ],
        [(wide_heads, F32), (wide_heads, F32)],
        x_in, halo, conv_weight, conv_bias.reshape(1, channels), steps, rates, dy,
    )
    got = lax.all_to_all(msg, "seq", 0, 0, tiled=True)
    intra, gbt, gct, col_sums, row_sums = call(
        within_kernel,
        [
            ((X_WIDTH, GROUP), F32),
            ((STATE, GROUP), F32),
            ((STATE, GROUP), F32),
            (wide_heads, F32),
            (wide_heads, F32),
        ],
        [
            ((HEADS, GROUP, LANE), F32),
            ((GROUP, GROUP), F32),
            ((GROUP, GROUP), F32),
            ((LANE, GROUP), F32),
        ],
        zt, bc, dyt, dy, cum,
    )
    (turned,) = call(
        functools.partial(chain_kernel, chunks=chunks, rows=rows),
        [((chunks, 2 * rows, LANE), BF16)],
        [],
        got,
    )
    back = lax.all_to_all(turned, "seq", 0, 0, tiled=True)
    vmem = pl.BlockSpec(memory_space=pltpu.VMEM)
    gpre, edge, gsteps, params = call(
        functools.partial(back_kernel, chunks=chunks, rows=rows),
        [
            ((GROUP, channels), F32),
            ((8, channels), F32),
            (wide_heads, F32),
            (((KCONV + 1) * (PAIRS + 2) + 2, LANE), F32),
        ],
        [
            ((X_WIDTH, STATE), BF16),
            ((X_WIDTH, STATE), BF16),
            (wide_heads, F32),
            (wide_heads, F32),
            (wide_heads, F32),
            (wide_heads, F32),
            (wide_heads, F32),
            ((HEADS, LANE), F32),
            ((STATE, GROUP), F32),
            ((STATE, GROUP), F32),
            ((PAIRS + 2, 8, LANE), F32),
            ((LANE, LANE), F32),
        ],
        back, zt, dyt, cum, intra, gbt, gct, col_sums, row_sums,
        deriv, x_in, halo, steps, rates, skip_gain,
        in_specs=[vmem] * 14 + [pl.BlockSpec(memory_space=pltpu.SMEM)],
    )
    next_rows = shifted(edge, "seq", -1)
    (grad_in,) = call(
        spread_kernel, [((GROUP, channels), BF16)], [], gpre, next_rows, conv_weight
    )
    sums = total_over_devices(params)
    tiles = PAIRS + 2
    grad_weight = sums[: KCONV * tiles].reshape(KCONV, channels)
    grad_bias = sums[KCONV * tiles : (KCONV + 1) * tiles].reshape(channels)
    grad_rates = sums[(KCONV + 1) * tiles, :HEADS]
    grad_skip = sums[(KCONV + 1) * tiles + 1, :HEADS]
    return (grad_in[None], gsteps[None], grad_weight, grad_bias, grad_rates, grad_skip)


def solution(mesh):
    return jax.shard_map(
        shards,
        mesh=mesh,
        in_specs=(
            P("dp", "seq", None),
            P(),
            P(),
            P("dp", None, "seq"),
            P(),
            P(),
            P("dp", "seq", None),
        ),
        out_specs=(P("dp", "seq", None), P("dp", None, "seq"), P(), P(), P(), P()),
        check_vma=False,
    )
```

time: 856 us -> 170 us (0.20)
  waiting for transfers between devices: 458 us -> 47.3 us
  other arithmetic: 140 us -> 0.89 us
  blocking collectives: 117 us -> 48.2 us
  local copies, waits for them, and re-layouts: 75.7 us -> 7.52 us
  Pallas kernels: 0 us -> 44.9 us
  matrix products: 36.5 us -> 0 us
  between operations: 14.8 us -> 0.7 us
  starting transfers between devices: 8.03 us -> 19.7 us
    all_gather x2 -> x0, waiting for transfers between devices: 458 us -> none  [carried_in(): everything = jax.tree.map(lambda part: lax.all_gather(part, axis), array)]
    select_n x64 -> x0, other arithmetic: 104 us -> none  [lap(): return jax.tree.map(lambda a, b: jnp.where(reached, a, b), new, before)]
    psum x1 -> x0, blocking collectives: 76.1 us -> none  [shards(): lax.psum((local_weight, local_bias, local_rates, local_skip), ('dp', 'seq'))]
    all_to_all x0 -> x1, blocking collectives: none -> 48.2 us  [shards(): got = lax.all_to_all(msg, 'seq', 0, 0, tiled=True)]
    pallas_call x0 -> x5, Pallas kernels: none -> 44.9 us  [call(): pl.pallas_call(kernel, out_shape=[jax.ShapeDtypeStruct(shape, dtype) for...]
    all_gather x1 -> x0, blocking collectives: 40.6 us -> none  [carried_in(): everything = jax.tree.map(lambda part: lax.all_gather(part, axis), array)]
    dot_general x11 -> x0, matrix products: 36.5 us -> none  [the longest x1 8.93 us: block_grads(): lax.dot_general(b_proj, adjoint_low, contract_last, preferred_element_typ...]
    mul x68 -> x0, local copies, waits for them, and re-layouts: 31.1 us -> none  [the longest x64 20.6 us: compose(): later[0][:, :, None, None] * earlier[1] + later[1]]
  transfers between devices with their start and end apart: 4 -> 11, of which waited for: 2 -> 9; matrix products, arithmetic and copies ran while one was open for 9% -> 2% of each run, Pallas kernels for 0% -> 9%
where the time goes in v1:
time: 170 us; the launch traced here: 169 us
  blocking collectives  48.2 us (28%)
  waiting for transfers between devices  47.3 us (28%)
  Pallas kernels  44.9 us (26%)
  starting transfers between devices  19.7 us (12%)
  local copies, waits for them, and re-layouts  7.52 us (4%)
    all_to_all x1, blocking collectives, shards(): got = lax.all_to_all(msg, 'seq', 0, 0, tiled=True)  48.2 us
    pallas_call x5, Pallas kernels, call(): pl.pallas_call(kernel, out_shape=[jax.ShapeDtypeStruct(shape, dtype) for...  44.9 us
    ppermute x8, waiting for transfers between devices, total_over_devices(): lax.ppermute(array, axis, [(i, i ^ bit) for i in range(length)])  24.3 us
    all_to_all x1, waiting for transfers between devices, shards(): back = lax.all_to_all(turned, 'seq', 0, 0, tiled=True)  21.4 us
    ppermute x8, starting transfers between devices, total_over_devices(): lax.ppermute(array, axis, [(i, i ^ bit) for i in range(length)])  9.27 us
    ppermute x2, starting transfers between devices, shifted(): return lax.ppermute(array, axis, pairs)  5.73 us
    all_to_all x1, starting transfers between devices, shards(): back = lax.all_to_all(turned, 'seq', 0, 0, tiled=True)  4.7 us
  transfers between devices with their start and end apart: 11, of which 9 were waited for; matrix products, arithmetic and copies ran while one was open for 2% of the time, Pallas kernels for 9%

profile of v1, /device:TPU:32, one launch (start us, length us, event | category | flops | bytes accessed | tf_op | source)
XLA Modules:
  0.0 169.2 jit_solution(1968279435314453228)
XLA Ops:
  0.6 0.8 slice_bitcast_fusion
  1.4 3.8 %collective-permute-start = (bf16[3,2816]{1,0:T(4,128)(2,1)S(1)}, bf16[3,2816]{1,0:T(4,128)(2,1)S(1)}, u32[]{:S(2)}, u32[]{:S(2)}) collective-permute-start(bf16[3,2816]{1,0:T(4,128)(2,1)S(1)} %slice_bitcast_fusion), channel_id=1, source_target_pairs={{0,1},{1,2},{2,3},{3,4},{4,5},{5,6},{6,7},{7,8},{8,9},{9,10},{10,1... | collective-permute-start | bytes 50696 | tf_op jit(solution)/shard_map/ppermute | solution.py:318
  5.3 1.3 reshape.25.bias_ref
  6.6 1.3 copy.13.rate_ref
  7.9 0.6 copy-done.2
  8.5 13.5 %shard_map.118 = (bf16[2816,256]{1,0:T(8,128)(2,1)}, bf16[256,256]{1,0:T(8,128)(2,1)}, bf16[2560,256]{1,0:T(8,128)(2,1)}, f32[256,2816]{1,0:T(8,128)}, f32[40,256]{1,0:T(8,128)}, /*index=5*/bf16[32,176,128]{2,1,0:T(8,128)(2,1)}) custom-call(bf16[256,2816]{1,0:T(8,128)(2,1)} %bitcast.14, bf16[3,2816]{1,0:T(4,128)(2,1)} %copy-done.2, f32[4,2816]{1,0:T(4,128)} %w_ref.3, ...), custom_call_target="tpu_custom_call" | custom-call | tf_op jit(solution)/shard_map/pallas_call | solution.py:306
  22.1 48.2 %all_to_all.10.got_ref = bf16[32,176,128]{2,1,0:T(8,128)(2,1)} all-to-all(bf16[32,176,128]{2,1,0:T(8,128)(2,1)} %get-tuple-element.21), channel_id=1, replica_groups=mesh['dp'=8,'seq'=32] {'seq'}, dimensions={0} | all-to-all | bytes 2883584 | tf_op jit(solution)/shard_map/all_to_all | solution.py:355
  70.2 3.1 %shard_map.119 = bf16[32,160,128]{2,1,0:T(8,128)(2,1)} custom-call(bf16[32,176,128]{2,1,0:T(8,128)(2,1)} %all_to_all.10.got_ref), custom_call_target="tpu_custom_call" | custom-call | tf_op jit(solution)/shard_map/pallas_call | solution.py:306
  73.3 4.7 %all-to-all-start.1 = ((bf16[32,160,128]{2,1,0:T(8,128)(2,1)}), bf16[32,160,128]{2,1,0:T(8,128)(2,1)S(1)}, u32[]{:S(2)}, u32[]{:S(2)}) async-start(bf16[32,160,128]{2,1,0:T(8,128)(2,1)} %shard_map.119), calls=%async_computation.1 | async-start | bytes 2621440 | tf_op jit(solution)/shard_map/all_to_all | solution.py:379
  78.0 11.3 %shard_map.120 = (f32[2560,256]{1,0:T(8,128)}, f32[128,256]{1,0:T(8,128)}, f32[128,256]{1,0:T(8,128)}, f32[40,256]{1,0:T(8,128)}, f32[40,256]{1,0:T(8,128)}) custom-call(bf16[2816,256]{1,0:T(8,128)(2,1)} %get-tuple-element.22.zt_ref, bf16[256,256]{1,0:T(8,128)(2,1)} %get-tuple-element.25.bc_ref, bf16[2560,256]{1,0:T(8,128)(2,1)} %get-tuple-element.23.dyt_ref, ...), custom_call_target="tpu_custom_call" | custom-call | tf_op jit(solution)/shard_map/pallas_call | solution.py:306
  89.3 21.4 %all-to-all-done.1.back_ref = bf16[32,160,128]{2,1,0:T(8,128)(2,1)S(1)} async-done(((bf16[32,160,128]{2,1,0:T(8,128)(2,1)}), bf16[32,160,128]{2,1,0:T(8,128)(2,1)S(1)}, u32[]{:S(2)}, u32[]{:S(2)}) %all-to-all-start.1) | async-done | bytes 1310752 | tf_op jit(solution)/shard_map/all_to_all | solution.py:379
  110.8 1.1 copy-done
  111.8 12.6 %shard_map.121 = (f32[256,2816]{1,0:T(8,128)}, f32[8,2816]{1,0:T(8,128)}, f32[40,256]{1,0:T(8,128)}, f32[112,128]{1,0:T(8,128)}) custom-call(bf16[32,160,128]{2,1,0:T(8,128)(2,1)} %copy-done, bf16[2816,256]{1,0:T(8,128)(2,1)} %get-tuple-element.22.zt_ref, bf16[2560,256]{1,0:T(8,128)(2,1)} %get-tuple-element.23.dyt_ref, f32[40,256]{1,0:T(8,128)} %get-tuple-element.24.cum_ref, ...), custom_call_target="tpu_custom_call" | custom-call | tf_op jit(solution)/shard_map/pallas_call | solution.py:306
  124.5 1.4 collective-permute-done.2
  125.9 0.8 add.24
  126.8 1.5 collective-permute-start.3
  128.2 2.7 %collective-permute-done.3 = f32[112,128]{1,0:T(8,128)S(1)} collective-permute-done((f32[112,128]{1,0:T(8,128)S(1)}, f32[112,128]{1,0:T(8,128)S(1)}, u32[]{:S(2)}, u32[]{:S(2)}) %collective-permute-start.3) | collective-permute-done | bytes 57376 | tf_op jit(solution)/shard_map/ppermute | solution.py:326
  130.9 3.1 %collective-permute-start.4 = (f32[112,128]{1,0:T(8,128)S(1)}, f32[112,128]{1,0:T(8,128)S(1)}, u32[]{:S(2)}, u32[]{:S(2)}) collective-permute-start(f32[112,128]{1,0:T(8,128)S(1)} %add.25), channel_id=1, source_target_pairs={{0,128},{32,160},{64,192},{96,224},{128,0},{160,32},{192,64},{224,... | collective-permute-start | bytes 172040 | tf_op jit(solution)/shard_map/ppermute | solution.py:326
  134.0 2.7 %collective-permute-done.4 = f32[112,128]{1,0:T(8,128)S(1)} collective-permute-done((f32[112,128]{1,0:T(8,128)S(1)}, f32[112,128]{1,0:T(8,128)S(1)}, u32[]{:S(2)}, u32[]{:S(2)}) %collective-permute-start.4) | collective-permute-done | bytes 57376 | tf_op jit(solution)/shard_map/ppermute | solution.py:326
  137.3 4.1 %collective-permute-done.5 = f32[112,128]{1,0:T(8,128)S(1)} collective-permute-done((f32[112,128]{1,0:T(8,128)S(1)}, f32[112,128]{1,0:T(8,128)S(1)}, u32[]{:S(2)}, u32[]{:S(2)}) %collective-permute-start.5) | collective-permute-done | bytes 57376 | tf_op jit(solution)/shard_map/ppermute | solution.py:326
  141.4 1.2 collective-permute-start.6
  142.6 4.1 %collective-permute-done.6 = f32[112,128]{1,0:T(8,128)S(1)} collective-permute-done((f32[112,128]{1,0:T(8,128)S(1)}, f32[112,128]{1,0:T(8,128)S(1)}, u32[]{:S(2)}, u32[]{:S(2)}) %collective-permute-start.6) | collective-permute-done | bytes 57376 | tf_op jit(solution)/shard_map/ppermute | solution.py:326
  147.1 7.8 %collective-permute-done.7 = f32[112,128]{1,0:T(8,128)S(1)} collective-permute-done((f32[112,128]{1,0:T(8,128)S(1)}, f32[112,128]{1,0:T(8,128)S(1)}, u32[]{:S(2)}, u32[]{:S(2)}) %collective-permute-start.7) | collective-permute-done | bytes 57376 | tf_op jit(solution)/shard_map/ppermute | solution.py:326
  154.9 0.8 collective-permute-start.8
  155.7 1.9 %collective-permute-start.1 = (f32[8,2816]{1,0:T(8,128)}, f32[8,2816]{1,0:T(8,128)S(1)}, u32[]{:S(2)}, u32[]{:S(2)}) collective-permute-start(f32[8,2816]{1,0:T(8,128)} %get-tuple-element.33), channel_id=1, source_target_pairs={{1,0},{2,1},{3,2},{4,3},{5,4},{6,5},{7,6},{8,7},{9,8},{10,9},{11,1... | collective-permute-start | bytes 270344 | tf_op jit(solution)/shard_map/ppermute | solution.py:318
  157.6 1.6 collective-permute-done.8
  159.2 1.6 collective-permute-start.9
  160.8 1.6 collective-permute-done.1.next_ref
  162.3 0.6 copy-done.1
  163.0 4.4 %shard_map.122 = bf16[256,2816]{1,0:T(8,128)(2,1)} custom-call(f32[256,2816]{1,0:T(8,128)} %get-tuple-element.32.gpre_ref, f32[8,2816]{1,0:T(8,128)} %copy-done.1, f32[4,2816]{1,0:T(4,128)} %w_ref.3), custom_call_target="tpu_custom_call" | custom-call | tf_op jit(solution)/shard_map/pallas_call | solution.py:306
  167.9 0.6 slice_bitcast_fusion.1
  168.6 0.6 reshape.27
  (17 shorter events, 1.7 us)
Async XLA Ops:
  1.4 6.5 %collective-permute-start = (bf16[3,2816]{1,0:T(4,128)(2,1)S(1)}, bf16[3,2816]{1,0:T(4,128)(2,1)S(1)}, u32[]{:S(2)}, u32[]{:S(2)}) collective-permute-start(bf16[3,2816]{1,0:T(4,128)(2,1)S(1)} %slice_bitcast_fusion), channel_id=1, source_target_pairs={{0,1},{1,2},{2,3},{3,4},{4,5},{5,6},{6,7},{7,8},{8,9},{9,10},{10,1... | collective-permute-start | bytes 50696 | tf_op jit(solution)/shard_map/ppermute | solution.py:318
  7.9 0.6 copy-start.2
  73.3 37.4 %all-to-all-start.1 = ((bf16[32,160,128]{2,1,0:T(8,128)(2,1)}), bf16[32,160,128]{2,1,0:T(8,128)(2,1)S(1)}, u32[]{:S(2)}, u32[]{:S(2)}) async-start(bf16[32,160,128]{2,1,0:T(8,128)(2,1)} %shard_map.119), calls=%async_computation.1 | async-start | bytes 2621440 | tf_op jit(solution)/shard_map/all_to_all | solution.py:379
  110.8 1.1 copy-start
  124.4 1.5 collective-permute-start.2
  126.8 4.2 %collective-permute-start.3 = (f32[112,128]{1,0:T(8,128)S(1)}, f32[112,128]{1,0:T(8,128)S(1)}, u32[]{:S(2)}, u32[]{:S(2)}) collective-permute-start(f32[112,128]{1,0:T(8,128)S(1)} %add.24), channel_id=1, source_target_pairs={{0,64},{32,96},{64,0},{96,32},{128,192},{160,224},{192,128},{224,1... | collective-permute-start | bytes 172040 | tf_op jit(solution)/shard_map/ppermute | solution.py:326
  130.9 5.8 %collective-permute-start.4 = (f32[112,128]{1,0:T(8,128)S(1)}, f32[112,128]{1,0:T(8,128)S(1)}, u32[]{:S(2)}, u32[]{:S(2)}) collective-permute-start(f32[112,128]{1,0:T(8,128)S(1)} %add.25), channel_id=1, source_target_pairs={{0,128},{32,160},{64,192},{96,224},{128,0},{160,32},{192,64},{224,... | collective-permute-start | bytes 172040 | tf_op jit(solution)/shard_map/ppermute | solution.py:326
  136.7 4.6 %collective-permute-start.5 = (f32[112,128]{1,0:T(8,128)S(1)}, f32[112,128]{1,0:T(8,128)S(1)}, u32[]{:S(2)}, u32[]{:S(2)}) collective-permute-start(f32[112,128]{1,0:T(8,128)S(1)} %add.26), channel_id=1, source_target_pairs={{0,1},{1,0},{2,3},{3,2},{4,5},{5,4},{6,7},{7,6},{8,9},{9,8},{10,11... | collective-permute-start | bytes 172040 | tf_op jit(solution)/shard_map/ppermute | solution.py:326
  141.4 5.3 %collective-permute-start.6 = (f32[112,128]{1,0:T(8,128)S(1)}, f32[112,128]{1,0:T(8,128)S(1)}, u32[]{:S(2)}, u32[]{:S(2)}) collective-permute-start(f32[112,128]{1,0:T(8,128)S(1)} %add.27), channel_id=1, source_target_pairs={{0,2},{1,3},{2,0},{3,1},{4,6},{5,7},{6,4},{7,5},{8,10},{9,11},{10,... | collective-permute-start | bytes 172040 | tf_op jit(solution)/shard_map/ppermute | solution.py:326
  146.6 8.3 %collective-permute-start.7 = (f32[112,128]{1,0:T(8,128)S(1)}, f32[112,128]{1,0:T(8,128)S(1)}, u32[]{:S(2)}, u32[]{:S(2)}) collective-permute-start(f32[112,128]{1,0:T(8,128)S(1)} %add.28), channel_id=1, source_target_pairs={{0,4},{1,5},{2,6},{3,7},{4,0},{5,1},{6,2},{7,3},{8,12},{9,13},{10,... | collective-permute-start | bytes 172040 | tf_op jit(solution)/shard_map/ppermute | solution.py:326
  154.9 4.3 %collective-permute-start.8 = (f32[112,128]{1,0:T(8,128)S(1)}, f32[112,128]{1,0:T(8,128)S(1)}, u32[]{:S(2)}, u32[]{:S(2)}) collective-permute-start(f32[112,128]{1,0:T(8,128)S(1)} %add.29), channel_id=1, source_target_pairs={{0,8},{1,9},{2,10},{3,11},{4,12},{5,13},{6,14},{7,15},{8,0},{9,1},... | collective-permute-start | bytes 172040 | tf_op jit(solution)/shard_map/ppermute | solution.py:326
  155.7 6.6 %collective-permute-start.1 = (f32[8,2816]{1,0:T(8,128)}, f32[8,2816]{1,0:T(8,128)S(1)}, u32[]{:S(2)}, u32[]{:S(2)}) collective-permute-start(f32[8,2816]{1,0:T(8,128)} %get-tuple-element.33), channel_id=1, source_target_pairs={{1,0},{2,1},{3,2},{4,3},{5,4},{6,5},{7,6},{8,7},{9,8},{10,9},{11,1... | collective-permute-start | bytes 270344 | tf_op jit(solution)/shard_map/ppermute | solution.py:318
  159.2 8.2 %collective-permute-start.9 = (f32[112,128]{1,0:T(8,128)S(1)}, f32[112,128]{1,0:T(8,128)S(1)}, u32[]{:S(2)}, u32[]{:S(2)}) collective-permute-start(f32[112,128]{1,0:T(8,128)S(1)} %add.30), channel_id=1, source_target_pairs={{0,16},{1,17},{2,18},{3,19},{4,20},{5,21},{6,22},{7,23},{8,24},{9,... | collective-permute-start | bytes 172040 | tf_op jit(solution)/shard_map/ppermute | solution.py:326
  162.3 0.6 copy-start.1

commit v2 on v1

v2 whole, which is shorter than its diff:
```python
import functools

import jax
import jax.numpy as jnp
from jax import lax
from jax.experimental import pallas as pl
from jax.experimental.pallas import tpu as pltpu
from jax.sharding import PartitionSpec as P

HEADS = 40
HEAD_DIM = 64
STATE = 128
GROUP = 256
KCONV = 4
LANE = 128
BF16 = jnp.bfloat16
F32 = jnp.float32
X_WIDTH = HEADS * HEAD_DIM
PAIRS = HEADS // 2
TAIL_ROWS = 16
VMEM_LIMIT = 24 * 1024 * 1024
HIGH = lax.Precision.HIGHEST


def mm(a, b, ca=1, cb=0, precision=None):
    return lax.dot_general(
        a, b, (((ca,), (cb,)), ((), ())), preferred_element_type=F32, precision=precision
    )


def lanes(c):
    return pl.ds(pl.multiple_of(c * LANE, LANE), LANE)


def taps_of(x_ref, halo_ref, c):
    full = jnp.concatenate(
        [
            jnp.zeros((8 - (KCONV - 1), LANE), F32),
            halo_ref[:, lanes(c)].astype(F32),
            x_ref[:, lanes(c)].astype(F32),
        ],
        axis=0,
    )
    return [full[5 + k : 5 + k + GROUP] for k in range(KCONV)]


def triangle(lower):
    row = lax.broadcasted_iota(jnp.int32, (GROUP, GROUP), 0)
    col = lax.broadcasted_iota(jnp.int32, (GROUP, GROUP), 1)
    return jnp.where(row >= col if lower else row <= col, 1.0, 0.0).astype(F32)


def head_column(scalar_ref):
    head = lax.broadcasted_iota(jnp.int32, (HEADS, GROUP), 0)
    found = jnp.zeros((HEADS, GROUP), F32)
    for h in range(HEADS):
        found = jnp.where(head == h, scalar_ref[h], found)
    return found


def pre_act_of(taps, w_ref, bias_ref, c):
    pre = bias_ref[lanes(c)].reshape(1, LANE)
    for k in range(KCONV):
        pre = pre + w_ref[k : k + 1, lanes(c)] * taps[k]
    return pre


def pair_rows(ref, c):
    return jnp.concatenate(
        [jnp.broadcast_to(ref[pl.ds(2 * c + i, 1), :], (HEAD_DIM, GROUP)) for i in range(2)], axis=0
    )


def decay_kernel(step_ref, rate_ref, dy_ref, dyt_ref, cum_ref, tail_ref, head_ref):
    logs = -(step_ref[...] * head_column(rate_ref))
    cum = mm(logs, triangle(False), precision=HIGH)
    cum_ref[...] = cum
    tail_ref[...] = jnp.exp(cum[:, GROUP - 1 :] - cum)
    head_ref[...] = jnp.exp(cum)

    def turn(c, carry):
        dyt_ref[lanes(c), :] = dy_ref[:, lanes(c)].T
        return carry

    lax.fori_loop(0, PAIRS, turn, 0)


def front_kernel(
    x_ref, halo_ref, w_ref, bias_ref, dyt_ref, tail_ref, head_ref,
    zt_ref, bc_ref, msg_ref, *, chunks, rows,
):
    def conv(c, carry):
        pre = pre_act_of(taps_of(x_ref, halo_ref, c), w_ref, bias_ref, c)
        z = (pre * jax.nn.sigmoid(pre)).astype(BF16)
        zt_ref[lanes(c), :] = z.T

        @pl.when(c >= PAIRS)
        def _():
            bc_ref[:, lanes(c - PAIRS)] = z

        return carry

    lax.fori_loop(0, PAIRS + 2, conv, 0)

    d_end = jnp.broadcast_to(head_ref[:, GROUP - 1 :], (HEADS, LANE))
    part_a = d_end.astype(BF16).astype(F32)
    part_b = (d_end - part_a).astype(BF16).astype(F32)
    part_c = (d_end - part_a - part_b).astype(BF16).astype(F32)
    blank = jnp.zeros((TAIL_ROWS - 6, LANE), F32)
    for j in range(chunks):
        first = rows * j // HEAD_DIM
        last = (rows * j + rows - 1) // HEAD_DIM
        picked = [p[h : h + 1] for h in (first, last) for p in (part_a, part_b, part_c)]
        msg_ref[j, 2 * rows :, :] = jnp.concatenate(picked + [blank], axis=0).astype(BF16)

    b_proj = bc_ref[:, :STATE]
    c_proj = bc_ref[:, STATE:]
    per = 5
    span = per * HEAD_DIM
    each = span // rows

    def local(g, carry):
        for source, scale, proj, at in (
            (zt_ref, tail_ref, b_proj, 0),
            (dyt_ref, head_ref, c_proj, rows),
        ):
            parts = []
            for i in range(per):
                start = pl.multiple_of(g * span + i * HEAD_DIM, HEAD_DIM)
                wide = source[pl.ds(start, HEAD_DIM), :].astype(F32)
                parts.append((wide * scale[pl.ds(g * per + i, 1), :]).astype(BF16))
            found = mm(jnp.concatenate(parts, axis=0), proj).astype(BF16)
            for i in range(each):
                msg_ref[g * each + i, at : at + rows, :] = found[i * rows : (i + 1) * rows]
        return carry

    lax.fori_loop(0, HEADS // per, local, 0)


def within_kernel(
    zt_ref, bc_ref, dyt_ref, dy_ref, cum_ref, skip_ref,
    base_ref, gb_ref, gc_ref, col_ref, row_ref, skiprow_ref,
    column_ref, wsum_ref, cb_ref, hold_ref,
):
    hold_ref[...] = jnp.zeros_like(hold_ref)
    hold_ref[:HEADS, :] = cum_ref[...]
    turned = hold_ref[...].T
    for h in range(HEADS):
        column_ref[h] = jnp.broadcast_to(turned[:, h : h + 1], (GROUP, LANE))
    wsum_ref[...] = jnp.zeros_like(wsum_ref)
    bt = zt_ref[X_WIDTH : X_WIDTH + STATE, :]
    cb_ref[...] = mm(bc_ref[:, STATE:], bt)
    t_index = lax.broadcasted_iota(jnp.int32, (GROUP, GROUP), 0)
    s_index = lax.broadcasted_iota(jnp.int32, (GROUP, GROUP), 1)
    causal = t_index >= s_index

    def pair(c, carry):
        dy_pair = dy_ref[:, lanes(c)]
        xt_pair = zt_ref[lanes(c), :]
        dyt_pair = dyt_ref[lanes(c), :]
        zero = jnp.zeros((HEAD_DIM, GROUP), BF16)
        total = wsum_ref[...]
        for i in range(2):
            h = 2 * c + i
            at = pl.ds(h, 1)
            xt = xt_pair[i * HEAD_DIM : (i + 1) * HEAD_DIM]
            dyt = dyt_pair[i * HEAD_DIM : (i + 1) * HEAD_DIM]
            wide = jnp.concatenate([xt, zero] if i == 0 else [zero, xt], axis=0)
            inner = mm(dy_pair, wide)
            column = column_ref[h]
            column = jnp.concatenate([column, column], axis=1)
            gap = column - cum_ref[at, :]
            decay = jnp.exp(jnp.where(causal, gap, -jnp.inf))
            total = total + decay * inner
            kt = (decay * cb_ref[...]).astype(BF16)
            intra = mm(dyt, kt)
            forth = mm(xt, kt, 1, 1)
            xf = xt.astype(F32)
            dyf = dyt.astype(F32)
            base_ref[pl.ds(pl.multiple_of(h * HEAD_DIM, HEAD_DIM), HEAD_DIM), :] = (
                intra + skip_ref[h] * dyf
            )
            col_ref[at, :] = jnp.sum(intra * xf, axis=0, keepdims=True)
            row_ref[at, :] = jnp.sum(forth * dyf, axis=0, keepdims=True)
            skiprow_ref[at, :] = jnp.sum(xf * dyf, axis=0, keepdims=True)
        wsum_ref[...] = total
        return carry

    lax.fori_loop(0, PAIRS, pair, 0)
    w_summed = wsum_ref[...].astype(BF16)
    gb_ref[...] = mm(w_summed, bc_ref[:, STATE:], 0, 0)
    gc_ref[...] = mm(w_summed, bc_ref[:, :STATE])


def ready_kernel(
    x_ref, halo_ref, w_ref, bias_ref, dy_ref, tail_ref, head_ref, base_ref,
    own_ref, scale_ref, xw_ref, dyw_ref,
):
    def slopes(c):
        pre = pre_act_of(taps_of(x_ref, halo_ref, c), w_ref, bias_ref, c)
        sig = jax.nn.sigmoid(pre)
        return pre * sig, sig * (1.0 + pre * (1.0 - sig))

    def pair(c, carry):
        act, slope = slopes(c)
        tail = pair_rows(tail_ref, c).T
        head = pair_rows(head_ref, c).T
        own_ref[:, lanes(c)] = base_ref[lanes(c), :].T * slope
        scale_ref[:, lanes(c)] = tail * slope
        xw_ref[:, lanes(c)] = (act.astype(BF16).astype(F32) * tail).astype(BF16)
        dyw_ref[:, lanes(c)] = (dy_ref[:, lanes(c)].astype(F32) * head).astype(BF16)
        return carry

    lax.fori_loop(0, PAIRS, pair, 0)
    for c in (PAIRS, PAIRS + 1):
        scale_ref[:, lanes(c)] = slopes(c)[1]


def chain_kernel(got_ref, out_ref, *, chunks, rows):
    j = lax.axis_index("seq")
    split = HEAD_DIM - lax.rem(rows * j, HEAD_DIM)
    ahead = lax.broadcasted_iota(jnp.int32, (rows, LANE), 0) < split

    def decay_of(i):
        ends = got_ref[i, 2 * rows :, :].astype(F32)
        one = ends[0:1] + ends[1:2] + ends[2:3]
        two = ends[3:4] + ends[4:5] + ends[5:6]
        return jnp.where(ahead, one, two)

    def step(k, carry):
        state, adjoint = carry
        out_ref[k, :rows, :] = state.astype(BF16)
        state = decay_of(k) * state + got_ref[k, :rows, :].astype(F32)
        m = chunks - 1 - k
        out_ref[m, rows:, :] = adjoint.astype(BF16)
        adjoint = decay_of(m) * adjoint + got_ref[m, rows : 2 * rows, :].astype(F32)
        return state, adjoint

    zero = jnp.zeros((rows, LANE), F32)
    lax.fori_loop(0, chunks, step, (zero, zero))


def back_kernel(
    back_ref, zt_ref, bc_ref, dyt_ref, tail_ref, head_ref, own_ref, scale_ref, xw_ref, dyw_ref,
    gbin_ref, gcin_ref, colin_ref, row_ref, skiprow_ref,
    x_ref, halo_ref, w_ref, step_ref, rate_ref,
    gin_ref, last_ref, edge_ref, gsteps_ref, params_ref,
    st_ref, ad_ref, q_ref, r_ref, four_ref, gb_ref, gc_ref, sums_ref, flip_ref,
    *, chunks, rows,
):
    rim = KCONV - 1
    for j in range(chunks):
        st_ref[j * rows : (j + 1) * rows, :] = back_ref[j, :rows, :]
        ad_ref[j * rows : (j + 1) * rows, :] = back_ref[j, rows:, :]
    gb_ref[...] = gbin_ref[...]
    gc_ref[...] = gcin_ref[...]

    def finish(c, grad):
        edge_ref[:, lanes(c)] = grad[:rim]
        found = [
            jnp.sum(grad * tap, axis=0, keepdims=True) for tap in taps_of(x_ref, halo_ref, c)
        ]
        found.append(jnp.sum(grad, axis=0, keepdims=True))
        found.append(jnp.zeros((8 - len(found), LANE), F32))
        sums_ref[c] = jnp.concatenate(found, axis=0)
        full = jnp.concatenate([grad, jnp.zeros((8, LANE), F32)], axis=0)
        spread = w_ref[rim : rim + 1, lanes(c)] * grad
        for k in range(rim):
            spread = spread + w_ref[k : k + 1, lanes(c)] * full[rim - k : rim - k + GROUP]
        gin_ref[:, lanes(c)] = spread.astype(BF16)
        last_ref[:, lanes(c)] = spread[GROUP - 16 :]

    def pair(c, carry):
        bt = zt_ref[X_WIDTH : X_WIDTH + STATE, :]
        ct = zt_ref[X_WIDTH + STATE :, :]
        states = st_ref[lanes(c), :]
        adjoint = ad_ref[lanes(c), :]
        c_dot = mm(states, ct) * dyt_ref[lanes(c), :].astype(F32)
        b_dot = mm(adjoint, bt) * zt_ref[lanes(c), :].astype(F32)
        both = states.astype(F32) * adjoint.astype(F32)
        for i in range(2):
            part = slice(i * HEAD_DIM, (i + 1) * HEAD_DIM)
            at = pl.ds(2 * c + i, 1)
            q_ref[at, :] = jnp.sum(c_dot[part], axis=0, keepdims=True)
            r_ref[at, :] = jnp.sum(b_dot[part], axis=0, keepdims=True)
            four_ref[at, :] = jnp.sum(both[part], axis=0, keepdims=True)
        gb_ref[...] += mm(xw_ref[:, lanes(c)], adjoint)
        gc_ref[...] += mm(dyw_ref[:, lanes(c)], states)
        finish(c, own_ref[:, lanes(c)] + scale_ref[:, lanes(c)] * mm(bc_ref[:, :STATE], adjoint, 1, 1))
        return carry

    lax.fori_loop(0, PAIRS, pair, 0)
    finish(PAIRS, gb_ref[...] * scale_ref[:, lanes(PAIRS)])
    finish(PAIRS + 1, gc_ref[...] * scale_ref[:, lanes(PAIRS + 1)])

    col_sums = colin_ref[...]
    row_sums = row_ref[...]
    tail_r = tail_ref[...] * r_ref[...]
    running = mm(col_sums - row_sums + tail_r, triangle(False), precision=HIGH)
    ending = mm(head_ref[...] * q_ref[...], triangle(True), precision=HIGH)
    four = head_ref[:, GROUP - 1 :] * jnp.sum(four_ref[...], axis=1, keepdims=True)
    grad_log = running + row_sums + ending + four - col_sums - tail_r
    gsteps_ref[...] = -head_column(rate_ref) * grad_log
    rates = -jnp.sum(step_ref[...] * grad_log, axis=1, keepdims=True)
    skips = jnp.sum(skiprow_ref[...], axis=1, keepdims=True)
    flip_ref[...] = jnp.zeros_like(flip_ref)
    lane = lax.broadcasted_iota(jnp.int32, (HEADS, LANE), 1)
    flip_ref[:HEADS, :] = jnp.where(lane == 0, rates, 0.0) + jnp.where(lane == 1, skips, 0.0)
    tiles = PAIRS + 2
    for c in range(tiles):
        sums = sums_ref[c]
        for k in range(KCONV + 1):
            at = k * tiles + c
            params_ref[at : at + 1, :] = sums[k : k + 1]
    at = (KCONV + 1) * tiles
    params_ref[at : at + 2, :] = flip_ref[...].T[:2]


def call(kernel, outs, scratch, *operands, scalars=0):
    vmem = pl.BlockSpec(memory_space=pltpu.VMEM)
    smem = pl.BlockSpec(memory_space=pltpu.SMEM)
    return pl.pallas_call(
        kernel,
        out_shape=[jax.ShapeDtypeStruct(shape, dtype) for shape, dtype in outs],
        in_specs=[vmem] * (len(operands) - scalars) + [smem] * scalars,
        scratch_shapes=[pltpu.VMEM(shape, dtype) for shape, dtype in scratch],
        compiler_params=pltpu.CompilerParams(vmem_limit_bytes=VMEM_LIMIT),
    )(*operands)


def shifted(array, axis, by):
    length = lax.axis_size(axis)
    pairs = [(i, i + by) for i in range(length) if 0 <= i + by < length]
    return lax.ppermute(array, axis, pairs)


def flipped(array, axis, bits):
    return lax.ppermute(array, axis, [(i, i ^ bits) for i in range(lax.axis_size(axis))])


def total_over_devices(array):
    for axis in ("dp", "seq"):
        length = lax.axis_size(axis)
        bit = 1
        if length.bit_length() % 2 == 0:
            array = array + flipped(array, axis, 1)
            bit = 2
        while bit < length:
            near = flipped(array, axis, bit)
            far = flipped(array, axis, 2 * bit)
            both = flipped(array, axis, 3 * bit)
            array = (array + near) + (far + both)
            bit *= 4
    return array


def shards(xbc_in, conv_weight, conv_bias, step_sizes, decay_rates, skip_gain, grad_out):
    channels = xbc_in.shape[2]
    rim = KCONV - 1
    chunks = lax.axis_size("seq")
    rows = X_WIDTH // chunks
    x_in = xbc_in[0]
    dy = grad_out[0]
    steps = step_sizes[0]
    wide_heads = ((HEADS, GROUP), F32)
    by_head = ((X_WIDTH, GROUP), F32)
    by_token = ((GROUP, STATE), F32)
    halo = shifted(x_in[GROUP - rim :], "seq", 1)
    dyt, cum, tail, head = call(
        lambda steps, dy, rates, *outs: decay_kernel(steps, rates, dy, *outs),
        [((X_WIDTH, GROUP), BF16), wide_heads, wide_heads, wide_heads],
        [],
        steps, dy, decay_rates, scalars=1,
    )
    zt, bc, msg = call(
        functools.partial(front_kernel, chunks=chunks, rows=rows),
        [
            ((channels, GROUP), BF16),
            ((GROUP, 2 * STATE), BF16),
            ((chunks, 2 * rows + TAIL_ROWS, LANE), BF16),
        ],
        [],
        x_in, halo, conv_weight, conv_bias, dyt, tail, head,
    )
    got = lax.all_to_all(msg, "seq", 0, 0, tiled=True)
    base, gb, gc, col_sums, row_sums, skip_rows = call(
        within_kernel,
        [by_head, by_token, by_token, wide_heads, wide_heads, wide_heads],
        [
            ((HEADS, GROUP, LANE), F32),
            ((GROUP, GROUP), F32),
            ((GROUP, GROUP), F32),
            ((LANE, GROUP), F32),
        ],
        zt, bc, dyt, dy, cum, skip_gain, scalars=1,
    )
    got, base = lax.optimization_barrier((got, base))
    (turned,) = call(
        functools.partial(chain_kernel, chunks=chunks, rows=rows),
        [((chunks, 2 * rows, LANE), BF16)],
        [],
        got,
    )
    back = lax.all_to_all(turned, "seq", 0, 0, tiled=True)
    own, scale, xw, dyw = call(
        ready_kernel,
        [
            ((GROUP, X_WIDTH), F32),
            ((GROUP, channels), F32),
            ((GROUP, X_WIDTH), BF16),
            ((GROUP, X_WIDTH), BF16),
        ],
        [],
        x_in, halo, conv_weight, conv_bias, dy, tail, head, base,
    )
    grad_in, last, edge, gsteps, params = call(
        functools.partial(back_kernel, chunks=chunks, rows=rows),
        [
            ((GROUP, channels), BF16),
            ((16, channels), F32),
            ((rim, channels), F32),
            wide_heads,
            (((KCONV + 1) * (PAIRS + 2) + 2, LANE), F32),
        ],
        [
            ((X_WIDTH, STATE), BF16),
            ((X_WIDTH, STATE), BF16),
            wide_heads,
            wide_heads,
            ((HEADS, LANE), F32),
            by_token,
            by_token,
            ((PAIRS + 2, 8, LANE), F32),
            ((LANE, LANE), F32),
        ],
        back, zt, bc, dyt, tail, head, own, scale, xw, dyw,
        gb, gc, col_sums, row_sums, skip_rows,
        x_in, halo, conv_weight, steps, decay_rates, scalars=1,
    )
    next_rows = shifted(edge, "seq", -1)
    ahead = jnp.concatenate([jnp.zeros_like(next_rows), next_rows], axis=0)
    added = last[16 - rim :]
    for k in range(rim):
        added = added + conv_weight[k][None] * ahead[rim - k : 2 * rim - k]
    ending = jnp.concatenate([last[: 16 - rim], added], axis=0).astype(BF16)
    grad_in = lax.dynamic_update_slice(grad_in, ending, (GROUP - 16, 0))
    sums = total_over_devices(params)
    tiles = PAIRS + 2
    grad_weight = sums[: KCONV * tiles].reshape(KCONV, channels)
    grad_bias = sums[KCONV * tiles : (KCONV + 1) * tiles].reshape(channels)
    grad_rates = sums[(KCONV + 1) * tiles, :HEADS]
    grad_skip = sums[(KCONV + 1) * tiles + 1, :HEADS]
    return (grad_in[None], gsteps[None], grad_weight, grad_bias, grad_rates, grad_skip)


def solution(mesh):
    return jax.shard_map(
        shards,
        mesh=mesh,
        in_specs=(
            P("dp", "seq", None),
            P(),
            P(),
            P("dp", None, "seq"),
            P(),
            P(),
            P("dp", "seq", None),
        ),
        out_specs=(P("dp", "seq", None), P("dp", None, "seq"), P(), P(), P(), P()),
        check_vma=False,
    )
```

time: 170 us -> 166 us (0.976)
  blocking collectives: 48.2 us -> 0 us
  local copies, waits for them, and re-layouts: 7.52 us -> 30.6 us
  starting transfers between devices: 19.7 us -> 37.4 us
  waiting for transfers between devices: 47.3 us -> 61.7 us
  Pallas kernels: 44.9 us -> 33.2 us
    all_to_all x1 -> x0, blocking collectives: 48.2 us -> none  [shards(): got = lax.all_to_all(msg, 'seq', 0, 0, tiled=True)]
    unnamed x6 -> x60, local copies, waits for them, and re-layouts: 2.3 us -> 28 us
    all_to_all x0 -> x1, waiting for transfers between devices: none -> 25.5 us  [shards(): got = lax.all_to_all(msg, 'seq', 0, 0, tiled=True)]
    pallas_call x5 -> x6, Pallas kernels: 44.9 us -> 33.2 us  [call(): pl.pallas_call(kernel, out_shape=[jax.ShapeDtypeStruct(shape, dtype) for...]
    all_to_all x0 -> x1, starting transfers between devices: none -> 10.6 us  [shards(): got = lax.all_to_all(msg, 'seq', 0, 0, tiled=True)]
    ppermute x8 -> x11, waiting for transfers between devices: 24.3 us -> 14.2 us  [flipped(): lax.ppermute(array, axis, [(i, i ^ bits) for i in range(lax.axis_size(axi...]
    ppermute x8 -> x11, starting transfers between devices: 9.27 us -> 15 us  [flipped(): lax.ppermute(array, axis, [(i, i ^ bits) for i in range(lax.axis_size(axi...]
    reshape x2 -> x0, local copies, waits for them, and re-layouts: 2.65 us -> none  [the longest x1 1.33 us: shards(): rates = decay_rates.reshape(HEADS, 1)]
  transfers between devices with their start and end apart: 11 -> 15, of which waited for: 9 -> 10; matrix products, arithmetic and copies ran while one was open for 2% -> 1% of each run, Pallas kernels for 9% -> 9%
where the time goes in v2:
time: 166 us; the launch traced here: 165 us
  waiting for transfers between devices  61.7 us (37%)
  starting transfers between devices  37.4 us (23%)
  Pallas kernels  33.2 us (20%)
  local copies, waits for them, and re-layouts  30.6 us (18%)
    pallas_call x6, Pallas kernels, call(): pl.pallas_call(kernel, out_shape=[jax.ShapeDtypeStruct(shape, dtype) for...  33.2 us
    unnamed x60, local copies, waits for them, and re-layouts  28 us
    all_to_all x1, waiting for transfers between devices, shards(): got = lax.all_to_all(msg, 'seq', 0, 0, tiled=True)  25.5 us
    all_to_all x1, waiting for transfers between devices, shards(): back = lax.all_to_all(turned, 'seq', 0, 0, tiled=True)  22 us
    ppermute x11, starting transfers between devices, flipped(): lax.ppermute(array, axis, [(i, i ^ bits) for i in range(lax.axis_size(axi...  15 us
    ppermute x11, waiting for transfers between devices, flipped(): lax.ppermute(array, axis, [(i, i ^ bits) for i in range(lax.axis_size(axi...  14.2 us
    all_to_all x1, starting transfers between devices, shards(): got = lax.all_to_all(msg, 'seq', 0, 0, tiled=True)  10.6 us
    ppermute x2, starting transfers between devices, shifted(): return lax.ppermute(array, axis, pairs)  6.24 us
  transfers between devices with their start and end apart: 15, of which 10 were waited for; matrix products, arithmetic and copies ran while one was open for 1% of the time, Pallas kernels for 9%

profile of v2, /device:TPU:32, one launch (start us, length us, event | category | flops | bytes accessed | tf_op | source)
XLA Modules:
  0.0 164.6 jit_solution(8704219592990422527)
XLA Ops:
  1.4 3.8 %collective-permute-start = (bf16[3,2816]{1,0:T(4,128)(2,1)S(1)}, bf16[3,2816]{1,0:T(4,128)(2,1)S(1)}, u32[]{:S(2)}, u32[]{:S(2)}) collective-permute-start(bf16[3,2816]{1,0:T(4,128)(2,1)S(1)} %slice_bitcast_fusion), channel_id=1, source_target_pairs={{0,1},{1,2},{2,3},{3,4},{4,5},{5,6},{6,7},{7,8},{8,9},{9,10},{10,1... | collective-permute-start | bytes 50696 | tf_op jit(solution)/shard_map/ppermute | solution.py:334
  8.0 2.3 %shard_map.118 = (bf16[2560,256]{1,0:T(8,128)(2,1)S(1)}, f32[40,256]{1,0:T(8,128)S(1)}, f32[40,256]{1,0:T(8,128)S(1)}, f32[40,256]{1,0:T(8,128)S(1)}) custom-call(f32[40,256]{1,0:T(8,128)S(1)} %bitcast.23, bf16[256,2560]{1,0:T(8,128)(2,1)S(1)} %bitcast.20, f32[40]{0:T(128)S(1)} %copy-done.27), custom_call_target="tpu_custom_call" | custom-call | tf_op jit(solution)/shard_map/pallas_call | solution.py:322
  10.3 1.8 %copy-done = bf16[1,256,2816]{2,1,0:T(8,128)(2,1)S(1)} copy-done((bf16[1,256,2816]{2,1,0:T(8,128)(2,1)S(1)}, bf16[1,256,2816]{2,1,0:T(8,128)(2,1)}, u32[]{:S(2)}) %copy-start) | copy-done | bytes 1441816
  13.7 5.8 %shard_map.119 = (bf16[2816,256]{1,0:T(8,128)(2,1)S(1)}, bf16[256,256]{1,0:T(8,128)(2,1)S(1)}, bf16[32,176,128]{2,1,0:T(8,128)(2,1)S(1)}) custom-call(bf16[256,2816]{1,0:T(8,128)(2,1)S(1)} %bitcast.17, bf16[3,2816]{1,0:T(4,128)(2,1)S(1)} %collective-permute-done.halo_ref, f32[4,2816]{1,0:T(4,128)S(1)} %copy-done.21, f32[2816]{0:T(1024)S(1)} %copy-done.25, ...), custom_call_target="tpu_custom_call" | custom-call | tf_op jit(solution)/shard_map/pallas_call | solution.py:322
  21.7 10.6 %all-to-all-start = ((bf16[32,176,128]{2,1,0:T(8,128)(2,1)}), bf16[32,176,128]{2,1,0:T(8,128)(2,1)}, u32[]{:S(2)}, u32[]{:S(2)}) async-start(bf16[32,176,128]{2,1,0:T(8,128)(2,1)} %copy-done.16), calls=%async_computation | async-start | bytes 2883584 | tf_op jit(solution)/shard_map/all_to_all | solution.py:385
  32.4 1.4 copy-done.7
  33.8 8.2 %shard_map.120 = (f32[2560,256]{1,0:T(8,128)S(1)}, f32[256,128]{1,0:T(8,128)S(1)}, f32[256,128]{1,0:T(8,128)S(1)}, f32[40,256]{1,0:T(8,128)S(1)}, f32[40,256]{1,0:T(8,128)S(1)}, /*index=5*/f32[40,256]{1,0:T(8,128)S(1)}) custom-call(bf16[2816,256]{1,0:T(8,128)(2,1)S(1)} %copy-done.7, bf16[256,256]{1,0:T(8,128)(2,1)S(1)} %get-tuple-element.35.bc_ref, ...), custom_call_target="tpu_custom_call" | custom-call | tf_op jit(solution)/shard_map/pallas_call | solution.py:322
  42.0 1.5 copy-done.12
  43.5 25.5 %all-to-all-done.got_ref = bf16[32,176,128]{2,1,0:T(8,128)(2,1)} async-done(((bf16[32,176,128]{2,1,0:T(8,128)(2,1)}), bf16[32,176,128]{2,1,0:T(8,128)(2,1)}, u32[]{:S(2)}, u32[]{:S(2)}) %all-to-all-start) | async-done | bytes 1441824 | tf_op jit(solution)/shard_map/all_to_all | solution.py:385
  69.0 2.0 %shard_map.121 = bf16[32,160,128]{2,1,0:T(8,128)(2,1)S(1)} custom-call(bf16[32,176,128]{2,1,0:T(8,128)(2,1)} %all-to-all-done.got_ref), custom_call_target="tpu_custom_call" | custom-call | tf_op jit(solution)/shard_map/pallas_call | solution.py:322
  72.0 5.5 %all-to-all-start.1 = ((bf16[32,160,128]{2,1,0:T(8,128)(2,1)}), bf16[32,160,128]{2,1,0:T(8,128)(2,1)}, u32[]{:S(2)}, u32[]{:S(2)}) async-start(bf16[32,160,128]{2,1,0:T(8,128)(2,1)} %copy-done.9), calls=%async_computation.1 | async-start | bytes 2621440 | tf_op jit(solution)/shard_map/all_to_all | solution.py:404
  77.6 1.7 %copy-done.13 = f32[2560,256]{1,0:T(8,128)S(1)} copy-done((f32[2560,256]{1,0:T(8,128)S(1)}, f32[2560,256]{1,0:T(8,128)}, u32[]{:S(2)}) %copy-start.13) | copy-done | bytes 2621464
  79.3 4.5 %shard_map.122 = (f32[256,2560]{1,0:T(8,128)S(1)}, f32[256,2816]{1,0:T(8,128)S(1)}, bf16[256,2560]{1,0:T(8,128)(2,1)S(1)}, bf16[256,2560]{1,0:T(8,128)(2,1)S(1)}) custom-call(bf16[256,2816]{1,0:T(8,128)(2,1)S(1)} %bitcast.18, bf16[3,2816]{1,0:T(4,128)(2,1)S(1)} %collective-permute-done.halo_ref, f32[4,2816]{1,0:T(4,128)S(1)} %copy-done.22, ...), custom_call_target="tpu_custom_call" | custom-call | tf_op jit(solution)/shard_map/pallas_call | solution.py:322
  83.8 1.5 copy-done.10
  85.4 1.5 copy-done.14
  89.0 22.0 %all-to-all-done.1.back_ref = bf16[32,160,128]{2,1,0:T(8,128)(2,1)} async-done(((bf16[32,160,128]{2,1,0:T(8,128)(2,1)}), bf16[32,160,128]{2,1,0:T(8,128)(2,1)}, u32[]{:S(2)}, u32[]{:S(2)}) %all-to-all-start.1) | async-done | bytes 1310752 | tf_op jit(solution)/shard_map/all_to_all | solution.py:404
  112.3 1.4 copy-done.8
  113.7 1.8 %copy-done.11 = f32[256,2816]{1,0:T(8,128)S(1)} copy-done((f32[256,2816]{1,0:T(8,128)S(1)}, f32[256,2816]{1,0:T(8,128)}, u32[]{:S(2)}) %copy-start.11) | copy-done | bytes 2883608
  115.5 1.7 %copy-done.15 = f32[256,2560]{1,0:T(8,128)S(1)} copy-done((f32[256,2560]{1,0:T(8,128)S(1)}, f32[256,2560]{1,0:T(8,128)}, u32[]{:S(2)}) %copy-start.15) | copy-done | bytes 2621464
  119.8 10.4 %shard_map.123 = (bf16[256,2816]{1,0:T(8,128)(2,1)}, f32[16,2816]{1,0:T(8,128)S(1)}, f32[3,2816]{1,0:T(4,128)S(1)}, f32[40,256]{1,0:T(8,128)}, f32[112,128]{1,0:T(8,128)S(1)}) custom-call(bf16[32,160,128]{2,1,0:T(8,128)(2,1)} %all-to-all-done.1.back_ref, bf16[2816,256]{1,0:T(8,128)(2,1)S(1)} %copy-done.8, bf16[256,256]{1,0:T(8,128)(2,1)S(1)} %get-tuple-element.35.bc_ref, ...), custom_call_target="tpu_custom_call" | custom-call | tf_op jit(solution)/shard_map/pallas_call | solution.py:322
  131.5 3.1 %collective-permute-start.4 = (f32[112,128]{1,0:T(8,128)S(1)}, f32[112,128]{1,0:T(8,128)S(1)}, u32[]{:S(2)}, u32[]{:S(2)}) collective-permute-start(f32[112,128]{1,0:T(8,128)S(1)} %add.47), channel_id=1, source_target_pairs={{0,128},{32,160},{64,192},{96,224},{128,0},{160,32},{192,64},{224,... | collective-permute-start | bytes 172040 | tf_op jit(solution)/shard_map/ppermute | solution.py:338
  135.8 2.4 %collective-permute-start.1 = (f32[3,2816]{1,0:T(4,128)S(1)}, f32[3,2816]{1,0:T(4,128)S(1)}, u32[]{:S(2)}, u32[]{:S(2)}) collective-permute-start(f32[3,2816]{1,0:T(4,128)S(1)} %get-tuple-element.51), channel_id=1, source_target_pairs={{1,0},{2,1},{3,2},{4,3},{5,4},{6,5},{7,6},{8,7},{9,8},{10,9},{11,1... | collective-permute-start | bytes 101384 | tf_op jit(solution)/shard_map/ppermute | solution.py:334
  138.3 1.7 %collective-permute-done.5 = f32[112,128]{1,0:T(8,128)S(1)} collective-permute-done((f32[112,128]{1,0:T(8,128)S(1)}, f32[112,128]{1,0:T(8,128)S(1)}, u32[]{:S(2)}, u32[]{:S(2)}) %collective-permute-start.5) | collective-permute-done | bytes 57376 | tf_op jit(solution)/shard_map/ppermute | solution.py:338
  140.6 3.7 %collective-permute-done.6 = f32[112,128]{1,0:T(8,128)S(1)} collective-permute-done((f32[112,128]{1,0:T(8,128)S(1)}, f32[112,128]{1,0:T(8,128)S(1)}, u32[]{:S(2)}, u32[]{:S(2)}) %collective-permute-start.6) | collective-permute-done | bytes 57376 | tf_op jit(solution)/shard_map/ppermute | solution.py:338
  144.3 1.5 collective-permute-start.8
  145.8 3.7 %collective-permute-start.9 = (f32[112,128]{1,0:T(8,128)S(1)}, f32[112,128]{1,0:T(8,128)S(1)}, u32[]{:S(2)}, u32[]{:S(2)}) collective-permute-start(f32[112,128]{1,0:T(8,128)S(1)} %add.51), channel_id=1, source_target_pairs={{0,6},{1,7},{2,4},{3,5},{4,2},{5,3},{6,0},{7,1},{8,14},{9,15},{10,... | collective-permute-start | bytes 172040 | tf_op jit(solution)/shard_map/ppermute | solution.py:338
  149.4 1.4 collective-permute-start.7
  150.9 2.3 %collective-permute-done.8 = f32[112,128]{1,0:T(8,128)S(1)} collective-permute-done((f32[112,128]{1,0:T(8,128)S(1)}, f32[112,128]{1,0:T(8,128)S(1)}, u32[]{:S(2)}, u32[]{:S(2)}) %collective-permute-start.8) | collective-permute-done | bytes 57376 | tf_op jit(solution)/shard_map/ppermute | solution.py:338
  153.2 1.8 %collective-permute-done.7 = f32[112,128]{1,0:T(8,128)S(1)} collective-permute-done((f32[112,128]{1,0:T(8,128)S(1)}, f32[112,128]{1,0:T(8,128)S(1)}, u32[]{:S(2)}, u32[]{:S(2)}) %collective-permute-start.7) | collective-permute-done | bytes 57376 | tf_op jit(solution)/shard_map/ppermute | solution.py:338
  155.0 1.5 collective-permute-start.11
  156.6 2.1 %collective-permute-start.12 = (f32[112,128]{1,0:T(8,128)S(1)}, f32[112,128]{1,0:T(8,128)S(1)}, u32[]{:S(2)}, u32[]{:S(2)}) collective-permute-start(f32[112,128]{1,0:T(8,128)S(1)} %add_add_fusion.1), channel_id=1, source_target_pairs={{0,24},{1,25},{2,26},{3,27},{4,28},{5,29},{6,30},{7,31},{8,16},{9,... | collective-permute-start | bytes 172040 | tf_op jit(solution)/shard_map/ppermute | solution.py:338
  159.3 1.5 collective-permute-done.11
  (78 shorter events, 22.1 us)
Async XLA Ops:
  1.4 8.9 %collective-permute-start = (bf16[3,2816]{1,0:T(4,128)(2,1)S(1)}, bf16[3,2816]{1,0:T(4,128)(2,1)S(1)}, u32[]{:S(2)}, u32[]{:S(2)}) collective-permute-start(bf16[3,2816]{1,0:T(4,128)(2,1)S(1)} %slice_bitcast_fusion), channel_id=1, source_target_pairs={{0,1},{1,2},{2,3},{3,4},{4,5},{5,6},{6,7},{7,8},{8,9},{9,10},{10,1... | collective-permute-start | bytes 50696 | tf_op jit(solution)/shard_map/ppermute | solution.py:334
  10.3 22.1 %copy-start.4 = (bf16[2560,256]{1,0:T(8,128)(2,1)}, bf16[2560,256]{1,0:T(8,128)(2,1)S(1)}, u32[]{:S(2)}) copy-start(bf16[2560,256]{1,0:T(8,128)(2,1)S(1)} %get-tuple-element.30.dyt_ref) | copy-start | bytes 3932164
  10.3 1.8 %copy-start = (bf16[1,256,2816]{2,1,0:T(8,128)(2,1)S(1)}, bf16[1,256,2816]{2,1,0:T(8,128)(2,1)}, u32[]{:S(2)}) copy-start(bf16[1,256,2816]{2,1,0:T(8,128)(2,1)} %param.7) | copy-start | bytes 4325380
  21.7 10.7 %copy-start.3 = (bf16[1,256,2560]{2,1,0:T(8,128)(2,1)S(1)}, bf16[1,256,2560]{2,1,0:T(8,128)(2,1)}, u32[]{:S(2)}) copy-start(bf16[1,256,2560]{2,1,0:T(8,128)(2,1)} %param.13) | copy-start | bytes 3932164
  21.7 10.7 %copy-start.29 = (f32[40]{0:T(128)S(1)}, f32[40]{0:T(128)}, u32[]{:S(2)}) copy-start(f32[40]{0:T(128)} %skip_ref.1) | copy-start | bytes 484
  21.7 47.2 %all-to-all-start = ((bf16[32,176,128]{2,1,0:T(8,128)(2,1)}), bf16[32,176,128]{2,1,0:T(8,128)(2,1)}, u32[]{:S(2)}, u32[]{:S(2)}) async-start(bf16[32,176,128]{2,1,0:T(8,128)(2,1)} %copy-done.16), calls=%async_computation | async-start | bytes 2883584 | tf_op jit(solution)/shard_map/all_to_all | solution.py:385
  32.4 1.4 copy-start.7
  42.0 1.5 copy-start.12
  72.0 5.5 %copy-start.1 = (bf16[1,256,2816]{2,1,0:T(8,128)(2,1)S(1)}, bf16[1,256,2816]{2,1,0:T(8,128)(2,1)}, u32[]{:S(2)}) copy-start(bf16[1,256,2816]{2,1,0:T(8,128)(2,1)} %param.7) | copy-start | bytes 4325380
  72.0 5.5 %copy-start.22 = (f32[4,2816]{1,0:T(4,128)S(1)}, f32[4,2816]{1,0:T(4,128)}, u32[]{:S(2)}) copy-start(f32[4,2816]{1,0:T(4,128)} %w_ref.5) | copy-start | bytes 135172
  72.0 5.6 %copy-start.26 = (f32[2816]{0:T(1024)S(1)}, f32[2816]{0:T(1024)}, u32[]{:S(2)}) copy-start(f32[2816]{0:T(1024)} %bias_ref.3) | copy-start | bytes 33796
  72.0 39.0 %all-to-all-start.1 = ((bf16[32,160,128]{2,1,0:T(8,128)(2,1)}), bf16[32,160,128]{2,1,0:T(8,128)(2,1)}, u32[]{:S(2)}, u32[]{:S(2)}) async-start(bf16[32,160,128]{2,1,0:T(8,128)(2,1)} %copy-done.9), calls=%async_computation.1 | async-start | bytes 2621440 | tf_op jit(solution)/shard_map/all_to_all | solution.py:404
  77.6 1.7 %copy-start.13 = (f32[2560,256]{1,0:T(8,128)S(1)}, f32[2560,256]{1,0:T(8,128)}, u32[]{:S(2)}) copy-start(f32[2560,256]{1,0:T(8,128)} %copy-done.12) | copy-start | bytes 7864324
  79.3 31.7 %copy-start.24 = (f32[1,40,256]{2,1,0:T(8,128)S(1)}, f32[1,40,256]{2,1,0:T(8,128)}, u32[]{:S(2)}) copy-start(f32[1,40,256]{2,1,0:T(8,128)} %param.10) | copy-start | bytes 122884
  79.3 31.7 %copy-start.28 = (f32[40]{0:T(128)S(1)}, f32[40]{0:T(128)}, u32[]{:S(2)}) copy-start(f32[40]{0:T(128)} %rate_ref.1) | copy-start | bytes 484
  83.8 1.6 copy-start.10
  85.4 1.5 copy-start.14
  112.3 1.4 copy-start.8
  113.7 1.8 %copy-start.11 = (f32[256,2816]{1,0:T(8,128)S(1)}, f32[256,2816]{1,0:T(8,128)}, u32[]{:S(2)}) copy-start(f32[256,2816]{1,0:T(8,128)} %copy-done.10) | copy-start | bytes 8650756
  115.5 1.7 %copy-start.15 = (f32[256,2560]{1,0:T(8,128)S(1)}, f32[256,2560]{1,0:T(8,128)}, u32[]{:S(2)}) copy-start(f32[256,2560]{1,0:T(8,128)} %copy-done.14) | copy-start | bytes 7864324
  130.2 1.2 collective-permute-start.2
  131.5 6.8 %collective-permute-start.4 = (f32[112,128]{1,0:T(8,128)S(1)}, f32[112,128]{1,0:T(8,128)S(1)}, u32[]{:S(2)}, u32[]{:S(2)}) collective-permute-start(f32[112,128]{1,0:T(8,128)S(1)} %add.47), channel_id=1, source_target_pairs={{0,128},{32,160},{64,192},{96,224},{128,0},{160,32},{192,64},{224,... | collective-permute-start | bytes 172040 | tf_op jit(solution)/shard_map/ppermute | solution.py:338
  134.6 5.4 %collective-permute-start.5 = (f32[112,128]{1,0:T(8,128)S(1)}, f32[112,128]{1,0:T(8,128)S(1)}, u32[]{:S(2)}, u32[]{:S(2)}) collective-permute-start(f32[112,128]{1,0:T(8,128)S(1)} %add.47), channel_id=1, source_target_pairs={{0,192},{32,224},{64,128},{96,160},{128,64},{160,96},{192,0},{224,... | collective-permute-start | bytes 172040 | tf_op jit(solution)/shard_map/ppermute | solution.py:338
  135.7 4.2 %collective-permute-start.3 = (f32[112,128]{1,0:T(8,128)S(1)}, f32[112,128]{1,0:T(8,128)S(1)}, u32[]{:S(2)}, u32[]{:S(2)}) collective-permute-start(f32[112,128]{1,0:T(8,128)S(1)} %add.47), channel_id=1, source_target_pairs={{0,64},{32,96},{64,0},{96,32},{128,192},{160,224},{192,128},{224,1... | collective-permute-start | bytes 172040 | tf_op jit(solution)/shard_map/ppermute | solution.py:338
  135.8 15.0 %collective-permute-start.1 = (f32[3,2816]{1,0:T(4,128)S(1)}, f32[3,2816]{1,0:T(4,128)S(1)}, u32[]{:S(2)}, u32[]{:S(2)}) collective-permute-start(f32[3,2816]{1,0:T(4,128)S(1)} %get-tuple-element.51), channel_id=1, source_target_pairs={{1,0},{2,1},{3,2},{4,3},{5,4},{6,5},{7,6},{8,7},{9,8},{10,9},{11,1... | collective-permute-start | bytes 101384 | tf_op jit(solution)/shard_map/ppermute | solution.py:334
  140.0 4.3 %collective-permute-start.6 = (f32[112,128]{1,0:T(8,128)S(1)}, f32[112,128]{1,0:T(8,128)S(1)}, u32[]{:S(2)}, u32[]{:S(2)}) collective-permute-start(f32[112,128]{1,0:T(8,128)S(1)} %add_add_fusion.2), channel_id=1, source_target_pairs={{0,1},{1,0},{2,3},{3,2},{4,5},{5,4},{6,7},{7,6},{8,9},{9,8},{10,11... | collective-permute-start | bytes 172040 | tf_op jit(solution)/shard_map/ppermute | solution.py:338
  144.3 8.9 %collective-permute-start.8 = (f32[112,128]{1,0:T(8,128)S(1)}, f32[112,128]{1,0:T(8,128)S(1)}, u32[]{:S(2)}, u32[]{:S(2)}) collective-permute-start(f32[112,128]{1,0:T(8,128)S(1)} %add.51), channel_id=1, source_target_pairs={{0,4},{1,5},{2,6},{3,7},{4,0},{5,1},{6,2},{7,3},{8,12},{9,13},{10,... | collective-permute-start | bytes 172040 | tf_op jit(solution)/shard_map/ppermute | solution.py:338
  145.8 7.4 %collective-permute-start.9 = (f32[112,128]{1,0:T(8,128)S(1)}, f32[112,128]{1,0:T(8,128)S(1)}, u32[]{:S(2)}, u32[]{:S(2)}) collective-permute-start(f32[112,128]{1,0:T(8,128)S(1)} %add.51), channel_id=1, source_target_pairs={{0,6},{1,7},{2,4},{3,5},{4,2},{5,3},{6,0},{7,1},{8,14},{9,15},{10,... | collective-permute-start | bytes 172040 | tf_op jit(solution)/shard_map/ppermute | solution.py:338
  149.4 5.6 %collective-permute-start.7 = (f32[112,128]{1,0:T(8,128)S(1)}, f32[112,128]{1,0:T(8,128)S(1)}, u32[]{:S(2)}, u32[]{:S(2)}) collective-permute-start(f32[112,128]{1,0:T(8,128)S(1)} %add.51), channel_id=1, source_target_pairs={{0,2},{1,3},{2,0},{3,1},{4,6},{5,7},{6,4},{7,5},{8,10},{9,11},{10,... | collective-permute-start | bytes 172040 | tf_op jit(solution)/shard_map/ppermute | solution.py:338
  155.0 5.8 %collective-permute-start.11 = (f32[112,128]{1,0:T(8,128)S(1)}, f32[112,128]{1,0:T(8,128)S(1)}, u32[]{:S(2)}, u32[]{:S(2)}) collective-permute-start(f32[112,128]{1,0:T(8,128)S(1)} %add_add_fusion.1), channel_id=1, source_target_pairs={{0,16},{1,17},{2,18},{3,19},{4,20},{5,21},{6,22},{7,23},{8,24},{9,... | collective-permute-start | bytes 172040 | tf_op jit(solution)/shard_map/ppermute | solution.py:338
  156.6 5.4 %collective-permute-start.12 = (f32[112,128]{1,0:T(8,128)S(1)}, f32[112,128]{1,0:T(8,128)S(1)}, u32[]{:S(2)}, u32[]{:S(2)}) collective-permute-start(f32[112,128]{1,0:T(8,128)S(1)} %add_add_fusion.1), channel_id=1, source_target_pairs={{0,24},{1,25},{2,26},{3,27},{4,28},{5,29},{6,30},{7,31},{8,16},{9,... | collective-permute-start | bytes 172040 | tf_op jit(solution)/shard_map/ppermute | solution.py:338
  158.6 4.2 %collective-permute-start.10 = (f32[112,128]{1,0:T(8,128)S(1)}, f32[112,128]{1,0:T(8,128)S(1)}, u32[]{:S(2)}, u32[]{:S(2)}) collective-permute-start(f32[112,128]{1,0:T(8,128)S(1)} %add_add_fusion.1), channel_id=1, source_target_pairs={{0,8},{1,9},{2,10},{3,11},{4,12},{5,13},{6,14},{7,15},{8,0},{9,1},... | collective-permute-start | bytes 172040 | tf_op jit(solution)/shard_map/ppermute | solution.py:338
  (13 other events, 13.6 us)

commit v3 on v2

v3 whole, which is shorter than its diff:
```python
import functools

import jax
import jax.numpy as jnp
from jax import lax
from jax.experimental import pallas as pl
from jax.experimental.pallas import tpu as pltpu
from jax.sharding import PartitionSpec as P

HEADS = 40
HEAD_DIM = 64
STATE = 128
GROUP = 256
KCONV = 4
LANE = 128
BF16 = jnp.bfloat16
F32 = jnp.float32
X_WIDTH = HEADS * HEAD_DIM
PAIRS = HEADS // 2
TAIL_ROWS = 16
VMEM_LIMIT = 56 * 1024 * 1024
SMALL_LIMIT = 24 * 1024 * 1024
PARTS = 4
HIGH = lax.Precision.HIGHEST


def mm(a, b, ca=1, cb=0, precision=None):
    return lax.dot_general(
        a, b, (((ca,), (cb,)), ((), ())), preferred_element_type=F32, precision=precision
    )


def lanes(c):
    return pl.ds(pl.multiple_of(c * LANE, LANE), LANE)


def taps_of(x_ref, halo_ref, c):
    full = jnp.concatenate(
        [
            jnp.zeros((8 - (KCONV - 1), LANE), F32),
            halo_ref[:, lanes(c)].astype(F32),
            x_ref[:, lanes(c)].astype(F32),
        ],
        axis=0,
    )
    return [full[5 + k : 5 + k + GROUP] for k in range(KCONV)]


def triangle(lower):
    row = lax.broadcasted_iota(jnp.int32, (GROUP, GROUP), 0)
    col = lax.broadcasted_iota(jnp.int32, (GROUP, GROUP), 1)
    return jnp.where(row >= col if lower else row <= col, 1.0, 0.0).astype(F32)


def head_column(scalar_ref):
    head = lax.broadcasted_iota(jnp.int32, (HEADS, GROUP), 0)
    found = jnp.zeros((HEADS, GROUP), F32)
    for h in range(HEADS):
        found = jnp.where(head == h, scalar_ref[h], found)
    return found


def pre_act_of(taps, w_ref, bias_ref, c):
    pre = bias_ref[lanes(c)].reshape(1, LANE)
    for k in range(KCONV):
        pre = pre + w_ref[k : k + 1, lanes(c)] * taps[k]
    return pre


def pair_rows(ref, c):
    return jnp.concatenate(
        [jnp.broadcast_to(ref[pl.ds(2 * c + i, 1), :], (HEAD_DIM, GROUP)) for i in range(2)], axis=0
    )


def started(sem, *pairs):
    made = [pltpu.make_async_copy(a, b, sem.at[i]) for i, (a, b) in enumerate(pairs)]
    for copy in made:
        copy.start()
    return made


def decay_kernel(
    step_hbm, rate_hbm, dy_hbm,
    dywt_ref, cum_ref, tail_ref, head_ref,
    step_ref, rate_ref, dy_ref, few_sem, dy_sem,
):
    span = X_WIDTH // PARTS
    few = started(few_sem, (step_hbm, step_ref), (rate_hbm, rate_ref))
    cuts = [slice(g * span, (g + 1) * span) for g in range(PARTS)]
    many = started(dy_sem, *[(dy_hbm.at[:, cut], dy_ref.at[:, cut]) for cut in cuts])
    for copy in few:
        copy.wait()
    logs = -(step_ref[...] * head_column(rate_ref))
    cum = mm(logs, triangle(False), precision=HIGH)
    cum_ref[...] = cum
    tail_ref[...] = jnp.exp(cum[:, GROUP - 1 :] - cum)
    head_ref[...] = jnp.exp(cum)

    def turn(c, carry):
        head = pair_rows(head_ref, c)
        dywt_ref[lanes(c), :] = (dy_ref[:, lanes(c)].T.astype(F32) * head).astype(BF16)
        return carry

    per = PAIRS // PARTS
    for g in range(PARTS):
        many[g].wait()
        lax.fori_loop(g * per, (g + 1) * per, turn, 0)


def front_kernel(
    halo_ref, dywt_ref, tail_ref, head_ref,
    x_hbm, w_hbm, bias_hbm,
    msg_hbm,
    x_ref, w_ref, bias_ref, msg_ref, bc_ref, xwt_ref, few_sem, x_sem, msg_sem,
    *, chunks, rows,
):
    per = PAIRS // PARTS
    span = per * LANE
    held = chunks // PARTS
    few = started(
        few_sem, (w_hbm, w_ref), (bias_hbm, bias_ref), (x_hbm.at[:, X_WIDTH:], x_ref.at[:, X_WIDTH:])
    )
    cuts = [slice(g * span, (g + 1) * span) for g in range(PARTS)]
    many = started(x_sem, *[(x_hbm.at[:, cut], x_ref.at[:, cut]) for cut in cuts])

    d_end = jnp.broadcast_to(head_ref[:, GROUP - 1 :], (HEADS, LANE))
    part_a = d_end.astype(BF16).astype(F32)
    part_b = (d_end - part_a).astype(BF16).astype(F32)
    part_c = (d_end - part_a - part_b).astype(BF16).astype(F32)
    blank = jnp.zeros((TAIL_ROWS - 6, LANE), F32)
    for j in range(chunks):
        first = rows * j // HEAD_DIM
        last = (rows * j + rows - 1) // HEAD_DIM
        picked = [p[h : h + 1] for h in (first, last) for p in (part_a, part_b, part_c)]
        msg_ref[j, 2 * rows :, :] = jnp.concatenate(picked + [blank], axis=0).astype(BF16)

    def active(c):
        pre = pre_act_of(taps_of(x_ref, halo_ref, c), w_ref, bias_ref, c)
        return (pre * jax.nn.sigmoid(pre)).astype(BF16)

    for copy in few:
        copy.wait()
    bc_ref[:, :STATE] = active(PAIRS)
    bc_ref[:, STATE:] = active(PAIRS + 1)
    sent = []
    for g in range(PARTS):
        many[g].wait()

        def conv(p, carry, g=g):
            c = g * per + p
            tail = pair_rows(tail_ref, c)
            xwt_ref[lanes(p), :] = (active(c).T.astype(F32) * tail).astype(BF16)
            return carry

        lax.fori_loop(0, per, conv, 0, unroll=True)
        s_local = mm(xwt_ref[...], bc_ref[:, :STATE]).astype(BF16)
        u_local = mm(dywt_ref[cuts[g], :], bc_ref[:, STATE:]).astype(BF16)
        for i in range(held):
            at = slice(i * rows, (i + 1) * rows)
            msg_ref[g * held + i, :rows, :] = s_local[at]
            msg_ref[g * held + i, rows : 2 * rows, :] = u_local[at]
        block = slice(g * held, (g + 1) * held)
        sent.append(pltpu.make_async_copy(msg_ref.at[block], msg_hbm.at[block], msg_sem.at[g]))
        sent[-1].start()
    for copy in sent:
        copy.wait()


def within_kernel(
    x_ref, halo_ref, w_ref, bias_ref, dy_ref, cum_ref, tail_ref, head_ref, skip_ref,
    own_ref, scale_ref, xwt_ref, dywt_ref, bc_ref, bct_ref, slope_ref,
    gb_ref, gc_ref, col_ref, row_ref, skiprow_ref,
    column_ref, wsum_ref, cb_ref, hold_ref, base_ref,
):
    def conv(c):
        pre = pre_act_of(taps_of(x_ref, halo_ref, c), w_ref, bias_ref, c)
        sig = jax.nn.sigmoid(pre)
        return (pre * sig).astype(BF16), sig * (1.0 + pre * (1.0 - sig))

    for i in range(2):
        at = slice(i * STATE, (i + 1) * STATE)
        z, slope_ref[:, at] = conv(PAIRS + i)
        bc_ref[:, at] = z
        bct_ref[at, :] = z.T
    hold_ref[...] = jnp.zeros_like(hold_ref)
    hold_ref[:HEADS, :] = cum_ref[...]
    turned = hold_ref[...].T
    for h in range(HEADS):
        column_ref[h] = jnp.broadcast_to(turned[:, h : h + 1], (GROUP, LANE))
    wsum_ref[...] = jnp.zeros_like(wsum_ref)
    cb_ref[...] = mm(bc_ref[:, STATE:], bct_ref[:STATE, :])
    t_index = lax.broadcasted_iota(jnp.int32, (GROUP, GROUP), 0)
    s_index = lax.broadcasted_iota(jnp.int32, (GROUP, GROUP), 1)
    causal = t_index >= s_index

    def pair(c, carry):
        z, slope = conv(c)
        xt_pair = z.T
        dy_pair = dy_ref[:, lanes(c)]
        dyt_pair = dy_pair.T
        tail = pair_rows(tail_ref, c)
        head = pair_rows(head_ref, c)
        xwt_ref[lanes(c), :] = (xt_pair.astype(F32) * tail).astype(BF16)
        dywt_ref[lanes(c), :] = (dyt_pair.astype(F32) * head).astype(BF16)
        scale_ref[:, lanes(c)] = (tail.T * slope).astype(BF16)
        zero = jnp.zeros((HEAD_DIM, GROUP), BF16)
        total = wsum_ref[...]
        for i in range(2):
            h = 2 * c + i
            at = pl.ds(h, 1)
            part = slice(i * HEAD_DIM, (i + 1) * HEAD_DIM)
            xt = xt_pair[part]
            dyt = dyt_pair[part]
            wide = jnp.concatenate([xt, zero] if i == 0 else [zero, xt], axis=0)
            inner = mm(dy_pair, wide)
            column = column_ref[h]
            column = jnp.concatenate([column, column], axis=1)
            gap = column - cum_ref[at, :]
            decay = jnp.exp(jnp.where(causal, gap, -jnp.inf))
            total = total + decay * inner
            kt = (decay * cb_ref[...]).astype(BF16)
            intra = mm(dyt, kt)
            forth = mm(xt, kt, 1, 1)
            xf = xt.astype(F32)
            dyf = dyt.astype(F32)
            base_ref[part, :] = intra + skip_ref[h] * dyf
            col_ref[at, :] = jnp.sum(intra * xf, axis=0, keepdims=True)
            row_ref[at, :] = jnp.sum(forth * dyf, axis=0, keepdims=True)
            skiprow_ref[at, :] = jnp.sum(xf * dyf, axis=0, keepdims=True)
        wsum_ref[...] = total
        own_ref[:, lanes(c)] = base_ref[...].T * slope
        return carry

    lax.fori_loop(0, PAIRS, pair, 0)
    w_summed = wsum_ref[...].astype(BF16)
    gb_ref[...] = mm(bct_ref[STATE:, :], w_summed)
    gc_ref[...] = mm(bct_ref[:STATE, :], w_summed, 1, 1)


def chain_kernel(got_ref, out_hbm, out_ref, sem, *, chunks, rows):
    j = lax.axis_index("seq")
    split = HEAD_DIM - lax.rem(rows * j, HEAD_DIM)
    ahead = lax.broadcasted_iota(jnp.int32, (rows, LANE), 0) < split

    def decay_of(i):
        ends = got_ref[i, 2 * rows :, :].astype(F32)
        one = ends[0:1] + ends[1:2] + ends[2:3]
        two = ends[3:4] + ends[4:5] + ends[5:6]
        return jnp.where(ahead, one, two)

    def step(k, carry):
        state, adjoint = carry
        out_ref[k, :rows, :] = state.astype(BF16)
        state = decay_of(k) * state + got_ref[k, :rows, :].astype(F32)
        m = chunks - 1 - k
        out_ref[m, rows:, :] = adjoint.astype(BF16)
        adjoint = decay_of(m) * adjoint + got_ref[m, rows : 2 * rows, :].astype(F32)
        return state, adjoint

    carry = (jnp.zeros((rows, LANE), F32), jnp.zeros((rows, LANE), F32))
    half = chunks // 2
    sent = []
    for g in range(2):
        carry = lax.fori_loop(g * half, (g + 1) * half, step, carry, unroll=4)
        fore = (slice(g * half, (g + 1) * half), slice(0, rows))
        rear = (slice((1 - g) * half, (2 - g) * half), slice(rows, 2 * rows))
        for i, at in enumerate((fore, rear)):
            sent.append(pltpu.make_async_copy(out_ref.at[at], out_hbm.at[at], sem.at[2 * g + i]))
            sent[-1].start()
    for copy in sent:
        copy.wait()


def back_kernel(
    back_ref, bc_ref, bct_ref, slope_ref,
    gbin_ref, gcin_ref, colin_ref, row_ref, skiprow_ref,
    halo_ref, w_ref, step_ref, head_ref,
    own_hbm, scale_hbm, xwt_hbm, dywt_hbm, x_hbm,
    rate_ref,
    gin_ref, last_ref, edge_ref, gsteps_ref, params_ref,
    own_ref, scale_ref, xwt_ref, dywt_ref, x_ref,
    cdot_ref, bdot_ref, btok_ref, q_ref, r_ref, four_ref, grad_ref, sums_ref, flip_ref, part_sem,
    *, chunks, rows,
):
    rim = KCONV - 1
    per = PAIRS // PARTS
    span = per * LANE
    held = chunks // PARTS

    def finish(c, grad):
        edge_ref[:, lanes(c)] = grad[:rim]
        x = x_ref[:, lanes(c)].astype(F32)
        halo = halo_ref[:, lanes(c)].astype(F32)
        full = jnp.concatenate([grad, jnp.zeros((8, LANE), F32)], axis=0)
        spread = w_ref[rim : rim + 1, lanes(c)] * grad
        found = []
        for k in range(rim):
            moved = full[rim - k : rim - k + GROUP]
            spread = spread + w_ref[k : k + 1, lanes(c)] * moved
            entering = jnp.sum(grad[: rim - k] * halo[k:], axis=0, keepdims=True)
            found.append(jnp.sum(moved * x, axis=0, keepdims=True) + entering)
        found.append(jnp.sum(grad * x, axis=0, keepdims=True))
        found.append(jnp.sum(grad, axis=0, keepdims=True))
        found.append(jnp.zeros((8 - len(found), LANE), F32))
        sums_ref[c] = jnp.concatenate(found, axis=0)
        gin_ref[:, lanes(c)] = spread.astype(BF16)
        last_ref[:, lanes(c)] = spread[GROUP - 16 :]

    def begin(g):
        if g == PARTS:
            return started(part_sem.at[g], (x_hbm.at[:, X_WIDTH:], x_ref.at[:, X_WIDTH:]))
        at = slice(g * span, (g + 1) * span)
        return started(
            part_sem.at[g],
            (xwt_hbm.at[at], xwt_ref.at[at]),
            (dywt_hbm.at[at], dywt_ref.at[at]),
            (own_hbm.at[:, at], own_ref.at[:, at]),
            (scale_hbm.at[:, at], scale_ref.at[:, at]),
            (x_hbm.at[:, at], x_ref.at[:, at]),
        )

    coming = [begin(0), begin(1)]
    b_proj = bc_ref[:, :STATE]
    gb = gbin_ref[...]
    gc = gcin_ref[...]
    for g in range(PARTS):
        at = slice(g * span, (g + 1) * span)
        states = back_ref[g * held : (g + 1) * held, :rows, :].reshape(span, STATE)
        adjoint = back_ref[g * held : (g + 1) * held, rows:, :].reshape(span, STATE)
        cdot_ref[...] = mm(states, bct_ref[STATE:, :])
        bdot_ref[...] = mm(adjoint, bct_ref[:STATE, :])
        btok_ref[...] = mm(b_proj, adjoint, 1, 1)
        both = states.astype(F32) * adjoint.astype(F32)
        for i in range(2 * per):
            h = 2 * per * g + i
            product = both[i * HEAD_DIM : (i + 1) * HEAD_DIM]
            four_ref[h : h + 1, :] = jnp.sum(product, axis=0, keepdims=True)
        for copy in coming[g]:
            copy.wait()
        if g + 2 <= PARTS:
            coming.append(begin(g + 2))
        gb = gb + mm(adjoint, xwt_ref[at, :], 0, 0)
        gc = gc + mm(states, dywt_ref[at, :], 0, 0)

        def pair(p, carry, g=g):
            c = g * per + p
            c_dot = cdot_ref[lanes(p), :] * dywt_ref[lanes(c), :].astype(F32)
            b_dot = bdot_ref[lanes(p), :] * xwt_ref[lanes(c), :].astype(F32)
            for i in range(2):
                part = slice(i * HEAD_DIM, (i + 1) * HEAD_DIM)
                h = pl.ds(2 * c + i, 1)
                q_ref[h, :] = jnp.sum(c_dot[part], axis=0, keepdims=True)
                r_ref[h, :] = jnp.sum(b_dot[part], axis=0, keepdims=True)
            state_part = scale_ref[:, lanes(c)].astype(F32) * btok_ref[:, lanes(p)]
            finish(c, own_ref[:, lanes(c)] + state_part)
            return carry

        lax.fori_loop(0, per, pair, 0, unroll=True)
    for copy in coming[PARTS]:
        copy.wait()
    for i, total in enumerate((gb, gc)):
        grad_ref[...] = total
        finish(PAIRS + i, grad_ref[...].T * slope_ref[:, i * STATE : (i + 1) * STATE])

    col_sums = colin_ref[...]
    row_sums = row_ref[...]
    tail_r = r_ref[...]
    running = mm(col_sums - row_sums + tail_r, triangle(False), precision=HIGH)
    ending = mm(q_ref[...], triangle(True), precision=HIGH)
    four = head_ref[:, GROUP - 1 :] * jnp.sum(four_ref[...], axis=1, keepdims=True)
    grad_log = running + row_sums + ending + four - col_sums - tail_r
    gsteps_ref[...] = -head_column(rate_ref) * grad_log
    rates = -jnp.sum(step_ref[...] * grad_log, axis=1, keepdims=True)
    skips = jnp.sum(skiprow_ref[...], axis=1, keepdims=True)
    flip_ref[...] = jnp.zeros_like(flip_ref)
    lane = lax.broadcasted_iota(jnp.int32, (HEADS, LANE), 1)
    flip_ref[:HEADS, :] = jnp.where(lane == 0, rates, 0.0) + jnp.where(lane == 1, skips, 0.0)
    tiles = PAIRS + 2
    for c in range(tiles):
        sums = sums_ref[c]
        for k in range(KCONV + 1):
            at = k * tiles + c
            params_ref[at : at + 1, :] = sums[k : k + 1]
    at = (KCONV + 1) * tiles
    params_ref[at : at + 2, :] = flip_ref[...].T[:2]


def call(
    kernel, outs, scratch, *operands, large=0, scalars=0, kept=(), large_out=False, limit=VMEM_LIMIT
):
    small = len(operands) - large - scalars
    spaces = [pltpu.VMEM] * small + [pltpu.HBM] * large + [pltpu.SMEM] * scalars
    operands = [
        pltpu.with_memory_space_constraint(operand, pltpu.HBM)
        if space == pltpu.HBM
        else operand
        for operand, space in zip(operands, spaces)
    ]
    out_space = pltpu.HBM if large_out else pltpu.VMEM
    return pl.pallas_call(
        kernel,
        out_shape=[
            out_space(*out) if large_out or i in kept else jax.ShapeDtypeStruct(*out)
            for i, out in enumerate(outs)
        ],
        in_specs=[pl.BlockSpec(memory_space=space) for space in spaces],
        out_specs=[pl.BlockSpec(memory_space=out_space)] * len(outs),
        scratch_shapes=[pltpu.VMEM(*item) if isinstance(item, tuple) else item for item in scratch],
        compiler_params=pltpu.CompilerParams(vmem_limit_bytes=limit),
    )(*operands)


def shifted(array, axis, by):
    length = lax.axis_size(axis)
    pairs = [(i, i + by) for i in range(length) if 0 <= i + by < length]
    return lax.ppermute(array, axis, pairs)


def flipped(array, axis, bits):
    return lax.ppermute(array, axis, [(i, i ^ bits) for i in range(lax.axis_size(axis))])


def total_over_devices(array):
    for axis in ("dp", "seq"):
        length = lax.axis_size(axis)
        bit = 1
        if length.bit_length() % 2 == 0:
            array = array + flipped(array, axis, 1)
            bit = 2
        while bit < length:
            near = flipped(array, axis, bit)
            far = flipped(array, axis, 2 * bit)
            both = flipped(array, axis, 3 * bit)
            array = (array + near) + (far + both)
            bit *= 4
    return array


def shards(xbc_in, conv_weight, conv_bias, step_sizes, decay_rates, skip_gain, grad_out):
    channels = xbc_in.shape[2]
    rim = KCONV - 1
    chunks = lax.axis_size("seq")
    rows = X_WIDTH // chunks
    x_in = xbc_in[0]
    dy = grad_out[0]
    steps = step_sizes[0]
    wide_heads = ((HEADS, GROUP), F32)
    by_head = ((X_WIDTH, GROUP), BF16)
    halo = shifted(x_in[GROUP - rim :], "seq", 1)
    dma = pltpu.SemaphoreType.DMA
    dywt, cum, tail, head = call(
        decay_kernel,
        [((X_WIDTH, GROUP), BF16), wide_heads, wide_heads, wide_heads],
        [wide_heads, pltpu.SMEM((HEADS,), F32), ((GROUP, X_WIDTH), BF16), dma((2,)), dma((PARTS,))],
        steps, decay_rates, dy, large=3, kept=(0,), limit=SMALL_LIMIT,
    )
    (msg,) = call(
        functools.partial(front_kernel, chunks=chunks, rows=rows),
        [((chunks, 2 * rows + TAIL_ROWS, LANE), BF16)],
        [
            ((GROUP, channels), BF16),
            ((KCONV, channels), F32),
            ((channels,), F32),
            ((chunks, 2 * rows + TAIL_ROWS, LANE), BF16),
            ((GROUP, 2 * STATE), BF16),
            ((X_WIDTH // PARTS, GROUP), BF16),
            dma((3,)),
            dma((PARTS,)),
            dma((PARTS,)),
        ],
        halo, dywt, tail, head, x_in, conv_weight, conv_bias,
        large=3, large_out=True, limit=SMALL_LIMIT,
    )
    got = lax.all_to_all(msg, "seq", 0, 0, tiled=True)
    own, scale, xwt, dywt, bc, bct, slope, gb, gc, col_sums, row_sums, skip_rows = call(
        within_kernel,
        [
            ((GROUP, X_WIDTH), F32),
            ((GROUP, X_WIDTH), BF16),
            by_head,
            by_head,
            ((GROUP, 2 * STATE), BF16),
            ((2 * STATE, GROUP), BF16),
            ((GROUP, 2 * STATE), F32),
            ((STATE, GROUP), F32),
            ((STATE, GROUP), F32),
            wide_heads,
            wide_heads,
            wide_heads,
        ],
        [
            ((HEADS, GROUP, LANE), F32),
            ((GROUP, GROUP), F32),
            ((GROUP, GROUP), F32),
            ((LANE, GROUP), F32),
            ((LANE, GROUP), F32),
        ],
        x_in, halo, conv_weight, conv_bias, dy, cum, tail, head, skip_gain, scalars=1,
    )
    got, own = lax.optimization_barrier((got, own))
    (turned,) = call(
        functools.partial(chain_kernel, chunks=chunks, rows=rows),
        [((chunks, 2 * rows, LANE), BF16)],
        [((chunks, 2 * rows, LANE), BF16), dma((4,))],
        got, large_out=True, limit=SMALL_LIMIT,
    )
    back = lax.all_to_all(turned, "seq", 0, 0, tiled=True)
    grad_in, last, edge, gsteps, params = call(
        functools.partial(back_kernel, chunks=chunks, rows=rows),
        [
            ((GROUP, channels), BF16),
            ((16, channels), F32),
            ((rim, channels), F32),
            wide_heads,
            (((KCONV + 1) * (PAIRS + 2) + 2, LANE), F32),
        ],
        [
            ((GROUP, X_WIDTH), F32),
            ((GROUP, X_WIDTH), BF16),
            by_head,
            by_head,
            ((GROUP, channels), BF16),
            ((X_WIDTH // PARTS, GROUP), F32),
            ((X_WIDTH // PARTS, GROUP), F32),
            ((GROUP, X_WIDTH // PARTS), F32),
            wide_heads,
            wide_heads,
            ((HEADS, LANE), F32),
            ((STATE, GROUP), F32),
            ((PAIRS + 2, 8, LANE), F32),
            ((LANE, LANE), F32),
            dma((PARTS + 1, 5)),
        ],
        back, bc, bct, slope, gb, gc, col_sums, row_sums, skip_rows,
        halo, conv_weight, steps, head,
        own, scale, xwt, dywt, x_in, decay_rates,
        large=5, scalars=1, limit=SMALL_LIMIT,
    )
    next_rows = shifted(edge, "seq", -1)
    ahead = jnp.concatenate([jnp.zeros_like(next_rows), next_rows], axis=0)
    added = last[16 - rim :]
    for k in range(rim):
        added = added + conv_weight[k][None] * ahead[rim - k : 2 * rim - k]
    ending = jnp.concatenate([last[: 16 - rim], added], axis=0).astype(BF16)
    grad_in = lax.dynamic_update_slice(grad_in, ending, (GROUP - 16, 0))
    sums = total_over_devices(params)
    tiles = PAIRS + 2
    grad_weight = sums[: KCONV * tiles].reshape(KCONV, channels)
    grad_bias = sums[KCONV * tiles : (KCONV + 1) * tiles].reshape(channels)
    grad_rates = sums[(KCONV + 1) * tiles, :HEADS]
    grad_skip = sums[(KCONV + 1) * tiles + 1, :HEADS]
    return (grad_in[None], gsteps[None], grad_weight, grad_bias, grad_rates, grad_skip)


def solution(mesh):
    return jax.shard_map(
        shards,
        mesh=mesh,
        in_specs=(
            P("dp", "seq", None),
            P(),
            P(),
            P("dp", None, "seq"),
            P(),
            P(),
            P("dp", "seq", None),
        ),
        out_specs=(P("dp", "seq", None), P("dp", None, "seq"), P(), P(), P(), P()),
        check_vma=False,
    )
```

time: 166 us -> 149 us (0.90)
  blocking collectives: 0 us -> 40 us
  waiting for transfers between devices: 61.7 us -> 31.8 us
  local copies, waits for them, and re-layouts: 30.6 us -> 3.35 us
  starting transfers between devices: 37.4 us -> 34.4 us
  Pallas kernels: 33.2 us -> 36 us
    all_to_all x0 -> x1, blocking collectives: none -> 40 us  [shards(): back = lax.all_to_all(turned, 'seq', 0, 0, tiled=True)]
    unnamed x60 -> x34, local copies, waits for them, and re-layouts: 28 us -> 0.68 us
    all_to_all x1 -> x0, waiting for transfers between devices: 22 us -> none  [shards(): back = lax.all_to_all(turned, 'seq', 0, 0, tiled=True)]
    all_to_all x1, waiting for transfers between devices: 25.5 us -> 19.1 us  [shards(): got = lax.all_to_all(msg, 'seq', 0, 0, tiled=True)]
    all_to_all x1 -> x0, starting transfers between devices: 5.52 us -> none  [shards(): back = lax.all_to_all(turned, 'seq', 0, 0, tiled=True)]
    pallas_call x6 -> x5, Pallas kernels: 33.2 us -> 36 us  [call(): pl.pallas_call(kernel, out_shape=[out_space(*out) if large_out or i in ke...]
    ppermute x11, starting transfers between devices: 15 us -> 17 us  [flipped(): lax.ppermute(array, axis, [(i, i ^ bits) for i in range(lax.axis_size(axi...]
  transfers between devices with their start and end apart: 15 -> 14, of which waited for: 10 -> 8; matrix products, arithmetic and copies ran while one was open for 1% -> 1% of each run, Pallas kernels for 9% -> 13%
where the time goes in v3:
time: 149 us; the launch traced here: 147 us
  blocking collectives  40 us (27%)
  Pallas kernels  36 us (24%)
  starting transfers between devices  34.4 us (23%)
  waiting for transfers between devices  31.8 us (21%)
  local copies, waits for them, and re-layouts  3.35 us (2%)
    all_to_all x1, blocking collectives, shards(): back = lax.all_to_all(turned, 'seq', 0, 0, tiled=True)  40 us
    pallas_call x5, Pallas kernels, call(): pl.pallas_call(kernel, out_shape=[out_space(*out) if large_out or i in ke...  36 us
    all_to_all x1, waiting for transfers between devices, shards(): got = lax.all_to_all(msg, 'seq', 0, 0, tiled=True)  19.1 us
    ppermute x11, starting transfers between devices, flipped(): lax.ppermute(array, axis, [(i, i ^ bits) for i in range(lax.axis_size(axi...  17 us
    ppermute x11, waiting for transfers between devices, flipped(): lax.ppermute(array, axis, [(i, i ^ bits) for i in range(lax.axis_size(axi...  12.7 us
    all_to_all x1, starting transfers between devices, shards(): got = lax.all_to_all(msg, 'seq', 0, 0, tiled=True)  10.9 us
    ppermute x2, starting transfers between devices, shifted(): return lax.ppermute(array, axis, pairs)  6.41 us
  transfers between devices with their start and end apart: 14, of which 8 were waited for; matrix products, arithmetic and copies ran while one was open for 1% of the time, Pallas kernels for 13%

profile of v3, /device:TPU:32, one launch (start us, length us, event | category | flops | bytes accessed | tf_op | source)
XLA Modules:
  0.0 147.2 jit_solution(14195956947416033801)
XLA Ops:
  0.6 0.8 slice_bitcast_fusion
  1.4 3.8 %collective-permute-start = (bf16[3,2816]{1,0:T(4,128)(2,1)S(1)}, bf16[3,2816]{1,0:T(4,128)(2,1)S(1)}, u32[]{:S(2)}, u32[]{:S(2)}) collective-permute-start(bf16[3,2816]{1,0:T(4,128)(2,1)S(1)} %slice_bitcast_fusion), channel_id=1, source_target_pairs={{0,1},{1,2},{2,3},{3,4},{4,5},{5,6},{6,7},{7,8},{8,9},{9,10},{10,1... | collective-permute-start | bytes 50696 | tf_op jit(solution)/shard_map/ppermute | solution.py:417
  5.3 2.8 %shard_map.118 = (bf16[2560,256]{1,0:T(8,128)(2,1)S(1)}, f32[40,256]{1,0:T(8,128)S(1)}, f32[40,256]{1,0:T(8,128)S(1)}, f32[40,256]{1,0:T(8,128)S(1)}) custom-call(f32[40,256]{1,0:T(8,128)} %bitcast.17, f32[40]{0:T(128)} %rate_ref.1, bf16[256,2560]{1,0:T(8,128)(2,1)} %bitcast.22), custom_call_target="tpu_custom_call" | custom-call | tf_op jit(solution)/shard_map/pallas_call | solution.py:401
  8.1 0.6 copy-done.15
  8.7 5.0 %shard_map.119 = bf16[32,176,128]{2,1,0:T(8,128)(2,1)} custom-call(bf16[3,2816]{1,0:T(4,128)(2,1)S(1)} %collective-permute-done.halo_ref, bf16[2560,256]{1,0:T(8,128)(2,1)S(1)} %get-tuple-element.29.dywt_ref, f32[40,256]{1,0:T(8,128)S(1)} %get-tuple-element.30.tail_ref, f32[40,256]{1,0:T(8,128)S(1)} %get-tuple-element.31.head_ref, ...), custom_call_target="tpu_custom_call" | custom-call | tf_op jit(solution)/shard_map/pallas_call | solution.py:401
  13.7 10.9 %all-to-all-start = ((bf16[32,176,128]{2,1,0:T(8,128)(2,1)}), bf16[32,176,128]{2,1,0:T(8,128)(2,1)S(1)}, u32[]{:S(2)}, u32[]{:S(2)}) async-start(bf16[32,176,128]{2,1,0:T(8,128)(2,1)} %shard_map.119), calls=%async_computation | async-start | bytes 2883584 | tf_op jit(solution)/shard_map/all_to_all | solution.py:475
  24.7 16.7 %shard_map.120 = (f32[256,2560]{1,0:T(8,128)}, bf16[256,2560]{1,0:T(8,128)(2,1)}, bf16[2560,256]{1,0:T(8,128)(2,1)}, bf16[2560,256]{1,0:T(8,128)(2,1)}, bf16[256...) custom-call(bf16[256,2816]{1,0:T(8,128)(2,1)} %bitcast.20, ...), custom_call_target="tpu_custom_call" | custom-call | tf_op jit(solution)/shard_map/pallas_call | solution.py:401
  41.4 19.1 %all-to-all-done.got_ref = bf16[32,176,128]{2,1,0:T(8,128)(2,1)S(1)} async-done(((bf16[32,176,128]{2,1,0:T(8,128)(2,1)}), bf16[32,176,128]{2,1,0:T(8,128)(2,1)S(1)}, u32[]{:S(2)}, u32[]{:S(2)}) %all-to-all-start) | async-done | bytes 1441824 | tf_op jit(solution)/shard_map/all_to_all | solution.py:475
  60.4 1.4 shard_map.121
  62.0 40.0 %all_to_all.10.back_ref = bf16[32,160,128]{2,1,0:T(8,128)(2,1)S(1)} all-to-all(bf16[32,160,128]{2,1,0:T(8,128)(2,1)} %shard_map.121), channel_id=1, replica_groups=mesh['dp'=8,'seq'=32] {'seq'}, dimensions={0} | all-to-all | bytes 2621440 | tf_op jit(solution)/shard_map/all_to_all | solution.py:508
  102.1 10.1 %shard_map.122 = (bf16[256,2816]{1,0:T(8,128)(2,1)}, f32[16,2816]{1,0:T(8,128)S(1)}, f32[3,2816]{1,0:T(4,128)S(1)}, f32[40,256]{1,0:T(8,128)}, f32[112,128]{1,0:T(8,128)S(1)}) custom-call(bf16[32,160,128]{2,1,0:T(8,128)(2,1)S(1)} %all_to_all.10.back_ref, bf16[256,256]{1,0:T(8,128)(2,1)S(1)} %copy-done.8, bf16[256,256]{1,0:T(8,128)(2,1)S(1)} %copy-done.9, ...), custom_call_target="tpu_custom_call" | custom-call | tf_op jit(solution)/shard_map/pallas_call | solution.py:401
  112.3 1.2 collective-permute-done.2
  113.5 1.6 %collective-permute-start.3 = (f32[112,128]{1,0:T(8,128)S(1)}, f32[112,128]{1,0:T(8,128)S(1)}, u32[]{:S(2)}, u32[]{:S(2)}) collective-permute-start(f32[112,128]{1,0:T(8,128)S(1)} %add.47), channel_id=1, source_target_pairs={{0,64},{32,96},{64,0},{96,32},{128,192},{160,224},{192,128},{224,1... | collective-permute-start | bytes 172040 | tf_op jit(solution)/shard_map/ppermute | solution.py:421
  115.1 2.7 %collective-permute-start.4 = (f32[112,128]{1,0:T(8,128)S(1)}, f32[112,128]{1,0:T(8,128)S(1)}, u32[]{:S(2)}, u32[]{:S(2)}) collective-permute-start(f32[112,128]{1,0:T(8,128)S(1)} %add.47), channel_id=1, source_target_pairs={{0,128},{32,160},{64,192},{96,224},{128,0},{160,32},{192,64},{224,... | collective-permute-start | bytes 172040 | tf_op jit(solution)/shard_map/ppermute | solution.py:421
  117.9 0.5 collective-permute-start.5
  118.4 2.6 %collective-permute-start.1 = (f32[3,2816]{1,0:T(4,128)S(1)}, f32[3,2816]{1,0:T(4,128)S(1)}, u32[]{:S(2)}, u32[]{:S(2)}) collective-permute-start(f32[3,2816]{1,0:T(4,128)S(1)} %get-tuple-element.49), channel_id=1, source_target_pairs={{1,0},{2,1},{3,2},{4,3},{5,4},{6,5},{7,6},{8,7},{9,8},{10,9},{11,1... | collective-permute-start | bytes 101384 | tf_op jit(solution)/shard_map/ppermute | solution.py:417
  121.0 2.2 %collective-permute-done.5 = f32[112,128]{1,0:T(8,128)S(1)} collective-permute-done((f32[112,128]{1,0:T(8,128)S(1)}, f32[112,128]{1,0:T(8,128)S(1)}, u32[]{:S(2)}, u32[]{:S(2)}) %collective-permute-start.5) | collective-permute-done | bytes 57376 | tf_op jit(solution)/shard_map/ppermute | solution.py:421
  123.3 0.8 collective-permute-start.6
  124.0 3.5 %collective-permute-done.6 = f32[112,128]{1,0:T(8,128)S(1)} collective-permute-done((f32[112,128]{1,0:T(8,128)S(1)}, f32[112,128]{1,0:T(8,128)S(1)}, u32[]{:S(2)}, u32[]{:S(2)}) %collective-permute-start.6) | collective-permute-done | bytes 57376 | tf_op jit(solution)/shard_map/ppermute | solution.py:421
  127.5 1.0 collective-permute-start.7
  128.5 1.6 %collective-permute-start.8 = (f32[112,128]{1,0:T(8,128)S(1)}, f32[112,128]{1,0:T(8,128)S(1)}, u32[]{:S(2)}, u32[]{:S(2)}) collective-permute-start(f32[112,128]{1,0:T(8,128)S(1)} %add.51), channel_id=1, source_target_pairs={{0,4},{1,5},{2,6},{3,7},{4,0},{5,1},{6,2},{7,3},{8,12},{9,13},{10,... | collective-permute-start | bytes 172040 | tf_op jit(solution)/shard_map/ppermute | solution.py:421
  130.1 4.0 %collective-permute-start.9 = (f32[112,128]{1,0:T(8,128)S(1)}, f32[112,128]{1,0:T(8,128)S(1)}, u32[]{:S(2)}, u32[]{:S(2)}) collective-permute-start(f32[112,128]{1,0:T(8,128)S(1)} %add.51), channel_id=1, source_target_pairs={{0,6},{1,7},{2,4},{3,5},{4,2},{5,3},{6,0},{7,1},{8,14},{9,15},{10,... | collective-permute-start | bytes 172040 | tf_op jit(solution)/shard_map/ppermute | solution.py:421
  134.2 2.4 %collective-permute-done.8 = f32[112,128]{1,0:T(8,128)S(1)} collective-permute-done((f32[112,128]{1,0:T(8,128)S(1)}, f32[112,128]{1,0:T(8,128)S(1)}, u32[]{:S(2)}, u32[]{:S(2)}) %collective-permute-start.8) | collective-permute-done | bytes 57376 | tf_op jit(solution)/shard_map/ppermute | solution.py:421
  137.0 0.7 collective-permute-start.10
  137.7 2.3 %collective-permute-start.11 = (f32[112,128]{1,0:T(8,128)S(1)}, f32[112,128]{1,0:T(8,128)S(1)}, u32[]{:S(2)}, u32[]{:S(2)}) collective-permute-start(f32[112,128]{1,0:T(8,128)S(1)} %add_add_fusion.1), channel_id=1, source_target_pairs={{0,16},{1,17},{2,18},{3,19},{4,20},{5,21},{6,22},{7,23},{8,24},{9,... | collective-permute-start | bytes 172040 | tf_op jit(solution)/shard_map/ppermute | solution.py:421
  140.0 1.8 %collective-permute-start.12 = (f32[112,128]{1,0:T(8,128)S(1)}, f32[112,128]{1,0:T(8,128)S(1)}, u32[]{:S(2)}, u32[]{:S(2)}) collective-permute-start(f32[112,128]{1,0:T(8,128)S(1)} %add_add_fusion.1), channel_id=1, source_target_pairs={{0,24},{1,25},{2,26},{3,27},{4,28},{5,29},{6,30},{7,31},{8,16},{9,... | collective-permute-start | bytes 172040 | tf_op jit(solution)/shard_map/ppermute | solution.py:421
  141.8 0.7 maximum_dynamic-update-slice_fusion
  142.5 0.9 collective-permute-done.11
  143.4 2.0 %collective-permute-done.12 = f32[112,128]{1,0:T(8,128)S(1)} collective-permute-done((f32[112,128]{1,0:T(8,128)S(1)}, f32[112,128]{1,0:T(8,128)S(1)}, u32[]{:S(2)}, u32[]{:S(2)}) %collective-permute-start.12) | collective-permute-done | bytes 57376 | tf_op jit(solution)/shard_map/ppermute | solution.py:421
  145.5 0.6 slice_bitcast_fusion.1
  146.1 0.5 slice_bitcast_fusion.2
  146.6 0.6 reshape.52
  (50 shorter events, 0.8 us)
Async XLA Ops:
  1.4 7.3 %collective-permute-start = (bf16[3,2816]{1,0:T(4,128)(2,1)S(1)}, bf16[3,2816]{1,0:T(4,128)(2,1)S(1)}, u32[]{:S(2)}, u32[]{:S(2)}) collective-permute-start(bf16[3,2816]{1,0:T(4,128)(2,1)S(1)} %slice_bitcast_fusion), channel_id=1, source_target_pairs={{0,1},{1,2},{2,3},{3,4},{4,5},{5,6},{6,7},{7,8},{8,9},{9,10},{10,1... | collective-permute-start | bytes 50696 | tf_op jit(solution)/shard_map/ppermute | solution.py:417
  8.1 0.6 copy-start.15
  8.7 5.0 %copy-start.1 = (f32[40,256]{1,0:T(8,128)}, f32[40,256]{1,0:T(8,128)S(1)}, u32[]{:S(2)}) copy-start(f32[40,256]{1,0:T(8,128)S(1)} %get-tuple-element.31.head_ref) | copy-start | bytes 122884
  8.7 5.0 %copy-start.7 = (f32[40,256]{1,0:T(8,128)}, f32[40,256]{1,0:T(8,128)S(1)}, u32[]{:S(2)}) copy-start(f32[40,256]{1,0:T(8,128)S(1)} %get-tuple-element.30.tail_ref) | copy-start | bytes 122884
  8.7 5.0 %copy-start.4 = (bf16[3,2816]{1,0:T(4,128)(2,1)}, bf16[3,2816]{1,0:T(4,128)(2,1)S(1)}, u32[]{:S(2)}) copy-start(bf16[3,2816]{1,0:T(4,128)(2,1)S(1)} %collective-permute-done.halo_ref) | copy-start | bytes 50692
  13.7 46.7 %all-to-all-start = ((bf16[32,176,128]{2,1,0:T(8,128)(2,1)}), bf16[32,176,128]{2,1,0:T(8,128)(2,1)S(1)}, u32[]{:S(2)}, u32[]{:S(2)}) async-start(bf16[32,176,128]{2,1,0:T(8,128)(2,1)} %shard_map.119), calls=%async_computation | async-start | bytes 2883584 | tf_op jit(solution)/shard_map/all_to_all | solution.py:475
  61.8 40.1 %copy-start = (f32[4,2816]{1,0:T(4,128)S(1)}, f32[4,2816]{1,0:T(4,128)}, u32[]{:S(2)}) copy-start(f32[4,2816]{1,0:T(4,128)} %w_ref.3) | copy-start | bytes 135172
  61.8 40.1 %copy-start.2 = (f32[40,256]{1,0:T(8,128)S(1)}, f32[40,256]{1,0:T(8,128)}, u32[]{:S(2)}) copy-start(f32[40,256]{1,0:T(8,128)} %copy-done.1) | copy-start | bytes 122884
  61.8 40.1 %copy-start.3 = (f32[256,256]{1,0:T(8,128)S(1)}, f32[256,256]{1,0:T(8,128)}, u32[]{:S(2)}) copy-start(f32[256,256]{1,0:T(8,128)} %get-tuple-element.37.slope_ref) | copy-start | bytes 786436
  61.9 40.1 %copy-start.5 = (bf16[3,2816]{1,0:T(4,128)(2,1)S(1)}, bf16[3,2816]{1,0:T(4,128)(2,1)}, u32[]{:S(2)}) copy-start(bf16[3,2816]{1,0:T(4,128)(2,1)} %copy-done.4) | copy-start | bytes 50692
  61.9 40.1 %copy-start.6 = (f32[1,40,256]{2,1,0:T(8,128)S(1)}, f32[1,40,256]{2,1,0:T(8,128)}, u32[]{:S(2)}) copy-start(f32[1,40,256]{2,1,0:T(8,128)} %param.10) | copy-start | bytes 122884
  61.9 40.1 %copy-start.8 = (bf16[256,256]{1,0:T(8,128)(2,1)S(1)}, bf16[256,256]{1,0:T(8,128)(2,1)}, u32[]{:S(2)}) copy-start(bf16[256,256]{1,0:T(8,128)(2,1)} %get-tuple-element.35.bc_ref) | copy-start | bytes 393220
  61.9 40.1 %copy-start.9 = (bf16[256,256]{1,0:T(8,128)(2,1)S(1)}, bf16[256,256]{1,0:T(8,128)(2,1)}, u32[]{:S(2)}) copy-start(bf16[256,256]{1,0:T(8,128)(2,1)} %get-tuple-element.36.bct_ref) | copy-start | bytes 393220
  61.9 40.1 %copy-start.10 = (f32[128,256]{1,0:T(8,128)S(1)}, f32[128,256]{1,0:T(8,128)}, u32[]{:S(2)}) copy-start(f32[128,256]{1,0:T(8,128)} %get-tuple-element.38.gbin_ref) | copy-start | bytes 393220
  61.9 40.1 %copy-start.11 = (f32[128,256]{1,0:T(8,128)S(1)}, f32[128,256]{1,0:T(8,128)}, u32[]{:S(2)}) copy-start(f32[128,256]{1,0:T(8,128)} %get-tuple-element.39.gcin_ref) | copy-start | bytes 393220
  61.9 40.1 %copy-start.12 = (f32[40,256]{1,0:T(8,128)S(1)}, f32[40,256]{1,0:T(8,128)}, u32[]{:S(2)}) copy-start(f32[40,256]{1,0:T(8,128)} %get-tuple-element.40.colin_ref) | copy-start | bytes 122884
  61.9 40.1 %copy-start.13 = (f32[40,256]{1,0:T(8,128)S(1)}, f32[40,256]{1,0:T(8,128)}, u32[]{:S(2)}) copy-start(f32[40,256]{1,0:T(8,128)} %get-tuple-element.41.row_ref) | copy-start | bytes 122884
  61.9 40.1 %copy-start.14 = (f32[40,256]{1,0:T(8,128)S(1)}, f32[40,256]{1,0:T(8,128)}, u32[]{:S(2)}) copy-start(f32[40,256]{1,0:T(8,128)} %get-tuple-element.42.skiprow_ref) | copy-start | bytes 122884
  61.9 40.1 %copy-start.16 = (f32[40]{0:T(128)S(1)}, f32[40]{0:T(128)}, u32[]{:S(2)}) copy-start(f32[40]{0:T(128)} %rate_ref.1) | copy-start | bytes 484
  112.2 1.3 collective-permute-start.2
  113.5 7.5 %collective-permute-start.3 = (f32[112,128]{1,0:T(8,128)S(1)}, f32[112,128]{1,0:T(8,128)S(1)}, u32[]{:S(2)}, u32[]{:S(2)}) collective-permute-start(f32[112,128]{1,0:T(8,128)S(1)} %add.47), channel_id=1, source_target_pairs={{0,64},{32,96},{64,0},{96,32},{128,192},{160,224},{192,128},{224,1... | collective-permute-start | bytes 172040 | tf_op jit(solution)/shard_map/ppermute | solution.py:421
  115.1 5.9 %collective-permute-start.4 = (f32[112,128]{1,0:T(8,128)S(1)}, f32[112,128]{1,0:T(8,128)S(1)}, u32[]{:S(2)}, u32[]{:S(2)}) collective-permute-start(f32[112,128]{1,0:T(8,128)S(1)} %add.47), channel_id=1, source_target_pairs={{0,128},{32,160},{64,192},{96,224},{128,0},{160,32},{192,64},{224,... | collective-permute-start | bytes 172040 | tf_op jit(solution)/shard_map/ppermute | solution.py:421
  117.9 5.4 %collective-permute-start.5 = (f32[112,128]{1,0:T(8,128)S(1)}, f32[112,128]{1,0:T(8,128)S(1)}, u32[]{:S(2)}, u32[]{:S(2)}) collective-permute-start(f32[112,128]{1,0:T(8,128)S(1)} %add.47), channel_id=1, source_target_pairs={{0,192},{32,224},{64,128},{96,160},{128,64},{160,96},{192,0},{224,... | collective-permute-start | bytes 172040 | tf_op jit(solution)/shard_map/ppermute | solution.py:421
  118.4 15.7 %collective-permute-start.1 = (f32[3,2816]{1,0:T(4,128)S(1)}, f32[3,2816]{1,0:T(4,128)S(1)}, u32[]{:S(2)}, u32[]{:S(2)}) collective-permute-start(f32[3,2816]{1,0:T(4,128)S(1)} %get-tuple-element.49), channel_id=1, source_target_pairs={{1,0},{2,1},{3,2},{4,3},{5,4},{6,5},{7,6},{8,7},{9,8},{10,9},{11,1... | collective-permute-start | bytes 101384 | tf_op jit(solution)/shard_map/ppermute | solution.py:417
  123.3 4.3 %collective-permute-start.6 = (f32[112,128]{1,0:T(8,128)S(1)}, f32[112,128]{1,0:T(8,128)S(1)}, u32[]{:S(2)}, u32[]{:S(2)}) collective-permute-start(f32[112,128]{1,0:T(8,128)S(1)} %add_add_fusion.2), channel_id=1, source_target_pairs={{0,1},{1,0},{2,3},{3,2},{4,5},{5,4},{6,7},{7,6},{8,9},{9,8},{10,11... | collective-permute-start | bytes 172040 | tf_op jit(solution)/shard_map/ppermute | solution.py:421
  127.5 6.6 %collective-permute-start.7 = (f32[112,128]{1,0:T(8,128)S(1)}, f32[112,128]{1,0:T(8,128)S(1)}, u32[]{:S(2)}, u32[]{:S(2)}) collective-permute-start(f32[112,128]{1,0:T(8,128)S(1)} %add.51), channel_id=1, source_target_pairs={{0,2},{1,3},{2,0},{3,1},{4,6},{5,7},{6,4},{7,5},{8,10},{9,11},{10,... | collective-permute-start | bytes 172040 | tf_op jit(solution)/shard_map/ppermute | solution.py:421
  128.5 8.1 %collective-permute-start.8 = (f32[112,128]{1,0:T(8,128)S(1)}, f32[112,128]{1,0:T(8,128)S(1)}, u32[]{:S(2)}, u32[]{:S(2)}) collective-permute-start(f32[112,128]{1,0:T(8,128)S(1)} %add.51), channel_id=1, source_target_pairs={{0,4},{1,5},{2,6},{3,7},{4,0},{5,1},{6,2},{7,3},{8,12},{9,13},{10,... | collective-permute-start | bytes 172040 | tf_op jit(solution)/shard_map/ppermute | solution.py:421
  130.1 6.9 %collective-permute-start.9 = (f32[112,128]{1,0:T(8,128)S(1)}, f32[112,128]{1,0:T(8,128)S(1)}, u32[]{:S(2)}, u32[]{:S(2)}) collective-permute-start(f32[112,128]{1,0:T(8,128)S(1)} %add.51), channel_id=1, source_target_pairs={{0,6},{1,7},{2,4},{3,5},{4,2},{5,3},{6,0},{7,1},{8,14},{9,15},{10,... | collective-permute-start | bytes 172040 | tf_op jit(solution)/shard_map/ppermute | solution.py:421
  137.0 5.5 %collective-permute-start.10 = (f32[112,128]{1,0:T(8,128)S(1)}, f32[112,128]{1,0:T(8,128)S(1)}, u32[]{:S(2)}, u32[]{:S(2)}) collective-permute-start(f32[112,128]{1,0:T(8,128)S(1)} %add_add_fusion.1), channel_id=1, source_target_pairs={{0,8},{1,9},{2,10},{3,11},{4,12},{5,13},{6,14},{7,15},{8,0},{9,1},... | collective-permute-start | bytes 172040 | tf_op jit(solution)/shard_map/ppermute | solution.py:421
  137.7 5.7 %collective-permute-start.11 = (f32[112,128]{1,0:T(8,128)S(1)}, f32[112,128]{1,0:T(8,128)S(1)}, u32[]{:S(2)}, u32[]{:S(2)}) collective-permute-start(f32[112,128]{1,0:T(8,128)S(1)} %add_add_fusion.1), channel_id=1, source_target_pairs={{0,16},{1,17},{2,18},{3,19},{4,20},{5,21},{6,22},{7,23},{8,24},{9,... | collective-permute-start | bytes 172040 | tf_op jit(solution)/shard_map/ppermute | solution.py:421
  140.0 5.4 %collective-permute-start.12 = (f32[112,128]{1,0:T(8,128)S(1)}, f32[112,128]{1,0:T(8,128)S(1)}, u32[]{:S(2)}, u32[]{:S(2)}) collective-permute-start(f32[112,128]{1,0:T(8,128)S(1)} %add_add_fusion.1), channel_id=1, source_target_pairs={{0,24},{1,25},{2,26},{3,27},{4,28},{5,29},{6,30},{7,31},{8,16},{9,... | collective-permute-start | bytes 172040 | tf_op jit(solution)/shard_map/ppermute | solution.py:421

commit v4 on v3

--- a/solution.py
+++ b/solution.py
@@ -80,20 +80,25 @@
     return made
 
 
+def logs_of(step_ref, rate_ref):
+    return mm(-(step_ref[...] * head_column(rate_ref)), triangle(False), precision=HIGH)
+
+
 def decay_kernel(
-    step_hbm, rate_hbm, dy_hbm,
-    dywt_ref, cum_ref, tail_ref, head_ref,
-    step_ref, rate_ref, dy_ref, few_sem, dy_sem,
+    step_hbm, rate_hbm, dy_hbm, x_hbm,
+    dywt_ref, tail_ref, head_ref, rim_ref,
+    step_ref, rate_ref, dy_ref, last_ref, few_sem, dy_sem,
 ):
     span = X_WIDTH // PARTS
-    few = started(few_sem, (step_hbm, step_ref), (rate_hbm, rate_ref))
+    few = started(
+        few_sem, (step_hbm, step_ref), (rate_hbm, rate_ref), (x_hbm.at[GROUP - 16 :], last_ref)
+    )
     cuts = [slice(g * span, (g + 1) * span) for g in range(PARTS)]
     many = started(dy_sem, *[(dy_hbm.at[:, cut], dy_ref.at[:, cut]) for cut in cuts])
     for copy in few:
         copy.wait()
-    logs = -(step_ref[...] * head_column(rate_ref))
-    cum = mm(logs, triangle(False), precision=HIGH)
-    cum_ref[...] = cum
+    rim_ref[...] = last_ref[...].astype(F32)[16 - (KCONV - 1) :].astype(BF16)
+    cum = logs_of(step_ref, rate_ref)
     tail_ref[...] = jnp.exp(cum[:, GROUP - 1 :] - cum)
     head_ref[...] = jnp.exp(cum)
 
@@ -105,7 +110,7 @@
     per = PAIRS // PARTS
     for g in range(PARTS):
         many[g].wait()
-        lax.fori_loop(g * per, (g + 1) * per, turn, 0)
+        lax.fori_loop(g * per, (g + 1) * per, turn, 0, unroll=True)
 
 
 def front_kernel(
@@ -168,11 +173,18 @@
 
 
 def within_kernel(
-    x_ref, halo_ref, w_ref, bias_ref, dy_ref, cum_ref, tail_ref, head_ref, skip_ref,
+    x_ref, halo_ref, w_ref, bias_ref, dy_ref, step_ref, rate_ref, skip_ref,
     own_ref, scale_ref, xwt_ref, dywt_ref, bc_ref, bct_ref, slope_ref,
-    gb_ref, gc_ref, col_ref, row_ref, skiprow_ref,
-    column_ref, wsum_ref, cb_ref, hold_ref, base_ref,
+    gb_ref, gc_ref, col_ref, row_ref, skiprow_ref, sofar_ref, end_ref,
+    column_ref, wsum_ref, cb_ref, hold_ref, base_ref, cum_ref, tail_ref, head_ref,
 ):
+    cum = logs_of(step_ref, rate_ref)
+    cum_ref[...] = cum
+    tail_ref[...] = jnp.exp(cum[:, GROUP - 1 :] - cum)
+    head_ref[...] = jnp.exp(cum)
+    end_ref[...] = jnp.broadcast_to(jnp.exp(cum[:, GROUP - 1 :]), (HEADS, LANE))
+    sofar_ref[...] = mm(step_ref[...], triangle(False), precision=HIGH)
+
     def conv(c):
         pre = pre_act_of(taps_of(x_ref, halo_ref, c), w_ref, bias_ref, c)
         sig = jax.nn.sigmoid(pre)
@@ -275,12 +287,11 @@
 def back_kernel(
     back_ref, bc_ref, bct_ref, slope_ref,
     gbin_ref, gcin_ref, colin_ref, row_ref, skiprow_ref,
-    halo_ref, w_ref, step_ref, head_ref,
+    halo_ref, w_ref, step_ref, sofar_ref, end_ref,
     own_hbm, scale_hbm, xwt_hbm, dywt_hbm, x_hbm,
-    rate_ref,
-    gin_ref, last_ref, edge_ref, gsteps_ref, params_ref,
+    gin_ref, last_ref, edge_ref, q_ref, r_ref, four_ref, params_ref,
     own_ref, scale_ref, xwt_ref, dywt_ref, x_ref,
-    cdot_ref, bdot_ref, btok_ref, q_ref, r_ref, four_ref, grad_ref, sums_ref, flip_ref, part_sem,
+    cdot_ref, bdot_ref, btok_ref, product_ref, grad_ref, sums_ref, flip_ref, part_sem,
     *, chunks, rows,
 ):
     rim = KCONV - 1
@@ -335,7 +346,7 @@
         for i in range(2 * per):
             h = 2 * per * g + i
             product = both[i * HEAD_DIM : (i + 1) * HEAD_DIM]
-            four_ref[h : h + 1, :] = jnp.sum(product, axis=0, keepdims=True)
+            product_ref[h : h + 1, :] = jnp.sum(product, axis=0, keepdims=True)
         for copy in coming[g]:
             copy.wait()
         if g + 2 <= PARTS:
@@ -363,15 +374,14 @@
         grad_ref[...] = total
         finish(PAIRS + i, grad_ref[...].T * slope_ref[:, i * STATE : (i + 1) * STATE])
 
-    col_sums = colin_ref[...]
-    row_sums = row_ref[...]
-    tail_r = r_ref[...]
-    running = mm(col_sums - row_sums + tail_r, triangle(False), precision=HIGH)
-    ending = mm(q_ref[...], triangle(True), precision=HIGH)
-    four = head_ref[:, GROUP - 1 :] * jnp.sum(four_ref[...], axis=1, keepdims=True)
-    grad_log = running + row_sums + ending + four - col_sums - tail_r
-    gsteps_ref[...] = -head_column(rate_ref) * grad_log
-    rates = -jnp.sum(step_ref[...] * grad_log, axis=1, keepdims=True)
+    four = end_ref[...] * jnp.sum(product_ref[...], axis=1, keepdims=True)
+    four_ref[...] = four
+    steps = step_ref[...]
+    sofar = sofar_ref[...]
+    every = sofar[:, GROUP - 1 :]
+    own = row_ref[...] - colin_ref[...] - r_ref[...]
+    met = steps * own - (every - sofar + steps) * own + sofar * q_ref[...]
+    rates = -(jnp.sum(met, axis=1, keepdims=True) + four[:, :1] * every)
     skips = jnp.sum(skiprow_ref[...], axis=1, keepdims=True)
     flip_ref[...] = jnp.zeros_like(flip_ref)
     lane = lax.broadcasted_iota(jnp.int32, (HEADS, LANE), 1)
@@ -384,6 +394,27 @@
             params_ref[at : at + 1, :] = sums[k : k + 1]
     at = (KCONV + 1) * tiles
     params_ref[at : at + 2, :] = flip_ref[...].T[:2]
+
+
+def log_kernel(q_ref, r_ref, four_ref, col_ref, row_ref, rate_ref, gsteps_ref):
+    own = row_ref[...] - col_ref[...] - r_ref[...]
+    running = mm(own, triangle(False), precision=HIGH)
+    ending = mm(q_ref[...], triangle(True), precision=HIGH)
+    grad_log = own - running + ending + four_ref[:, :1]
+    gsteps_ref[...] = -head_column(rate_ref) * grad_log
+
+
+def unpack_kernel(near_ref, far_ref, weight_ref, bias_ref, rates_ref, skip_ref, sum_ref):
+    sum_ref[...] = near_ref[...] + far_ref[...]
+    tiles = PAIRS + 2
+    for c in range(tiles):
+        at = slice(c * LANE, (c + 1) * LANE)
+        for k in range(KCONV):
+            weight_ref[k : k + 1, at] = sum_ref[k * tiles + c : k * tiles + c + 1, :]
+        bias_ref[at] = sum_ref[KCONV * tiles + c, :]
+    at = (KCONV + 1) * tiles
+    rates_ref[...] = sum_ref[at, :HEADS]
+    skip_ref[...] = sum_ref[at + 1, :HEADS]
 
 
 def call(
@@ -421,20 +452,11 @@
     return lax.ppermute(array, axis, [(i, i ^ bits) for i in range(lax.axis_size(axis))])
 
 
-def total_over_devices(array):
-    for axis in ("dp", "seq"):
-        length = lax.axis_size(axis)
-        bit = 1
-        if length.bit_length() % 2 == 0:
-            array = array + flipped(array, axis, 1)
-            bit = 2
-        while bit < length:
-            near = flipped(array, axis, bit)
-            far = flipped(array, axis, 2 * bit)
-            both = flipped(array, axis, 3 * bit)
-            array = (array + near) + (far + both)
-            bit *= 4
-    return array
+def four_summed(array, axis, bit):
+    near = flipped(array, axis, bit)
+    far = flipped(array, axis, 2 * bit)
+    both = flipped(array, axis, 3 * bit)
+    return (array + near) + (far + both)
 
 
 def shards(xbc_in, conv_weight, conv_bias, step_sizes, decay_rates, skip_gain, grad_out):
@@ -447,14 +469,21 @@
     steps = step_sizes[0]
     wide_heads = ((HEADS, GROUP), F32)
     by_head = ((X_WIDTH, GROUP), BF16)
-    halo = shifted(x_in[GROUP - rim :], "seq", 1)
     dma = pltpu.SemaphoreType.DMA
-    dywt, cum, tail, head = call(
+    dywt, tail, head, x_rim = call(
         decay_kernel,
-        [((X_WIDTH, GROUP), BF16), wide_heads, wide_heads, wide_heads],
-        [wide_heads, pltpu.SMEM((HEADS,), F32), ((GROUP, X_WIDTH), BF16), dma((2,)), dma((PARTS,))],
-        steps, decay_rates, dy, large=3, kept=(0,), limit=SMALL_LIMIT,
-    )
+        [((X_WIDTH, GROUP), BF16), wide_heads, wide_heads, ((rim, channels), BF16)],
+        [
+            wide_heads,
+            pltpu.SMEM((HEADS,), F32),
+            ((GROUP, X_WIDTH), BF16),
+            ((16, channels), BF16),
+            dma((3,)),
+            dma((PARTS,)),
+        ],
+        steps, decay_rates, dy, x_in, large=4, kept=(0,), limit=SMALL_LIMIT,
+    )
+    halo = shifted(x_rim, "seq", 1)
     (msg,) = call(
         functools.partial(front_kernel, chunks=chunks, rows=rows),
         [((chunks, 2 * rows + TAIL_ROWS, LANE), BF16)],
@@ -473,7 +502,7 @@
         large=3, large_out=True, limit=SMALL_LIMIT,
     )
     got = lax.all_to_all(msg, "seq", 0, 0, tiled=True)
-    own, scale, xwt, dywt, bc, bct, slope, gb, gc, col_sums, row_sums, skip_rows = call(
+    (own, scale, xwt, dywt, bc, bct, slope, gb, gc, col_sums, row_sums, skip_rows, sofar, d_end) = call(
         within_kernel,
         [
             ((GROUP, X_WIDTH), F32),
@@ -488,6 +517,8 @@
             wide_heads,
             wide_heads,
             wide_heads,
+            wide_heads,
+            ((HEADS, LANE), F32),
         ],
         [
             ((HEADS, GROUP, LANE), F32),
@@ -495,8 +526,11 @@
             ((GROUP, GROUP), F32),
             ((LANE, GROUP), F32),
             ((LANE, GROUP), F32),
-        ],
-        x_in, halo, conv_weight, conv_bias, dy, cum, tail, head, skip_gain, scalars=1,
+            wide_heads,
+            wide_heads,
+            wide_heads,
+        ],
+        x_in, halo, conv_weight, conv_bias, dy, steps, decay_rates, skip_gain, scalars=2,
     )
     got, own = lax.optimization_barrier((got, own))
     (turned,) = call(
@@ -506,13 +540,15 @@
         got, large_out=True, limit=SMALL_LIMIT,
     )
     back = lax.all_to_all(turned, "seq", 0, 0, tiled=True)
-    grad_in, last, edge, gsteps, params = call(
+    grad_in, last, edge, q_rows, r_rows, four, params = call(
         functools.partial(back_kernel, chunks=chunks, rows=rows),
         [
             ((GROUP, channels), BF16),
             ((16, channels), F32),
             ((rim, channels), F32),
             wide_heads,
+            wide_heads,
+            ((HEADS, LANE), F32),
             (((KCONV + 1) * (PAIRS + 2) + 2, LANE), F32),
         ],
         [
@@ -524,8 +560,6 @@
             ((X_WIDTH // PARTS, GROUP), F32),
             ((X_WIDTH // PARTS, GROUP), F32),
             ((GROUP, X_WIDTH // PARTS), F32),
-            wide_heads,
-            wide_heads,
             ((HEADS, LANE), F32),
             ((STATE, GROUP), F32),
             ((PAIRS + 2, 8, LANE), F32),
@@ -533,23 +567,33 @@
             dma((PARTS + 1, 5)),
         ],
         back, bc, bct, slope, gb, gc, col_sums, row_sums, skip_rows,
-        halo, conv_weight, steps, head,
-        own, scale, xwt, dywt, x_in, decay_rates,
-        large=5, scalars=1, limit=SMALL_LIMIT,
-    )
+        halo, conv_weight, steps, sofar, d_end,
+        own, scale, xwt, dywt, x_in,
+        large=5, limit=SMALL_LIMIT,
+    )
+    sums = params + flipped(params, "dp", 1)
+    sums = four_summed(sums, "dp", 2)
+    sums = four_summed(sums, "seq", 8)
+    sums = four_summed(sums, "seq", 1)
+    sums, edge, q_rows = lax.optimization_barrier((sums, edge, q_rows))
+    far_sums = flipped(sums, "seq", 4)
     next_rows = shifted(edge, "seq", -1)
+    (gsteps,) = call(
+        log_kernel, [wide_heads], [], q_rows, r_rows, four, col_sums, row_sums, decay_rates,
+        scalars=1, limit=SMALL_LIMIT,
+    )
     ahead = jnp.concatenate([jnp.zeros_like(next_rows), next_rows], axis=0)
     added = last[16 - rim :]
     for k in range(rim):
         added = added + conv_weight[k][None] * ahead[rim - k : 2 * rim - k]
     ending = jnp.concatenate([last[: 16 - rim], added], axis=0).astype(BF16)
     grad_in = lax.dynamic_update_slice(grad_in, ending, (GROUP - 16, 0))
-    sums = total_over_devices(params)
-    tiles = PAIRS + 2
-    grad_weight = sums[: KCONV * tiles].reshape(KCONV, channels)
-    grad_bias = sums[KCONV * tiles : (KCONV + 1) * tiles].reshape(channels)
-    grad_rates = sums[(KCONV + 1) * tiles, :HEADS]
-    grad_skip = sums[(KCONV + 1) * tiles + 1, :HEADS]
+    grad_weight, grad_bias, grad_rates, grad_skip = call(
+        unpack_kernel,
+        [((KCONV, channels), F32), ((channels,), F32), ((HEADS,), F32), ((HEADS,), F32)],
+        [(params.shape, F32)],
+        sums, far_sums, limit=SMALL_LIMIT,
+    )
     return (grad_in[None], gsteps[None], grad_weight, grad_bias, grad_rates, grad_skip)
 
 

time: 149 us -> 151 us (1.013)
  waiting for transfers between devices: 31.8 us -> 37 us
  local copies, waits for them, and re-layouts: 3.35 us -> 0.17 us
    ppermute x11, waiting for transfers between devices: 12.7 us -> 16.7 us  [flipped(): lax.ppermute(array, axis, [(i, i ^ bits) for i in range(lax.axis_size(axi...]
    ppermute x2, waiting for transfers between devices: 0.01 us -> 1.87 us  [shifted(): return lax.ppermute(array, axis, pairs)]
    all_to_all x1, starting transfers between devices: 10.9 us -> 12.6 us  [shards(): got = lax.all_to_all(msg, 'seq', 0, 0, tiled=True)]
    pallas_call x5 -> x7, Pallas kernels: 36 us -> 36.6 us  [call(): pl.pallas_call(kernel, out_shape=[out_space(*out) if large_out or i in ke...]
  transfers between devices with their start and end apart: 14 -> 14, of which waited for: 8 -> 11; matrix products, arithmetic and copies ran while one was open for 1% -> 1% of each run, Pallas kernels for 13% -> 12%
where the time goes in v4:
time: 151 us; the launch traced here: 150 us
  blocking collectives  39.7 us (26%)
  waiting for transfers between devices  37 us (25%)
  Pallas kernels  36.6 us (24%)
  starting transfers between devices  34.6 us (23%)
    all_to_all x1, blocking collectives, shards(): back = lax.all_to_all(turned, 'seq', 0, 0, tiled=True)  39.7 us
    pallas_call x7, Pallas kernels, call(): pl.pallas_call(kernel, out_shape=[out_space(*out) if large_out or i in ke...  36.6 us
    all_to_all x1, waiting for transfers between devices, shards(): got = lax.all_to_all(msg, 'seq', 0, 0, tiled=True)  18.4 us
    ppermute x11, waiting for transfers between devices, flipped(): lax.ppermute(array, axis, [(i, i ^ bits) for i in range(lax.axis_size(axi...  16.7 us
    ppermute x11, starting transfers between devices, flipped(): lax.ppermute(array, axis, [(i, i ^ bits) for i in range(lax.axis_size(axi...  15.8 us
    all_to_all x1, starting transfers between devices, shards(): got = lax.all_to_all(msg, 'seq', 0, 0, tiled=True)  12.6 us
    ppermute x2, starting transfers between devices, shifted(): return lax.ppermute(array, axis, pairs)  6.26 us
  transfers between devices with their start and end apart: 14, of which 11 were waited for; matrix products, arithmetic and copies ran while one was open for 1% of the time, Pallas kernels for 12%

profile of v4, /device:TPU:32, one launch (start us, length us, event | category | flops | bytes accessed | tf_op | source)
XLA Modules:
  0.0 149.8 jit_solution(14119374450976988628)
XLA Ops:
  0.6 2.2 %shard_map.118 = (bf16[2560,256]{1,0:T(8,128)(2,1)S(1)}, f32[40,256]{1,0:T(8,128)S(1)}, f32[40,256]{1,0:T(8,128)S(1)}, bf16[3,2816]{1,0:T(4,128)(2,1)S(1)}) custom-call(f32[40,256]{1,0:T(8,128)} %bitcast.9, f32[40]{0:T(128)} %rate_ref.3, bf16[256,2560]{1,0:T(8,128)(2,1)} %bitcast.16, bf16[256,2816]{1,0:T(8,128)(2,1)} %bitcast.12), custom_call_target="tpu_custom_call" | custom-call | tf_op jit(solution)/shard_map/pallas_call | solution.py:432
  2.8 3.8 %collective-permute-start = (bf16[3,2816]{1,0:T(4,128)(2,1)S(1)}, bf16[3,2816]{1,0:T(4,128)(2,1)S(1)}, u32[]{:S(2)}, u32[]{:S(2)}) collective-permute-start(bf16[3,2816]{1,0:T(4,128)(2,1)S(1)} %get-tuple-element.40), channel_id=1, source_target_pairs={{0,1},{1,2},{2,3},{3,4},{4,5},{5,6},{6,7},{7,8},{8,9},{9,10},{10,1... | collective-permute-start | bytes 50696 | tf_op jit(solution)/shard_map/ppermute | solution.py:448
  6.6 1.9 %collective-permute-done.halo_ref = bf16[3,2816]{1,0:T(4,128)(2,1)S(1)} collective-permute-done((bf16[3,2816]{1,0:T(4,128)(2,1)S(1)}, bf16[3,2816]{1,0:T(4,128)(2,1)S(1)}, u32[]{:S(2)}, u32[]{:S(2)}) %collective-permute-start) | collective-permute-done | bytes 16928 | tf_op jit(solution)/shard_map/ppermute | solution.py:448
  8.5 4.9 %shard_map.119 = bf16[32,176,128]{2,1,0:T(8,128)(2,1)} custom-call(bf16[3,2816]{1,0:T(4,128)(2,1)S(1)} %collective-permute-done.halo_ref, bf16[2560,256]{1,0:T(8,128)(2,1)S(1)} %get-tuple-element.41.dywt_ref, f32[40,256]{1,0:T(8,128)S(1)} %get-tuple-element.42.tail_ref, f32[40,256]{1,0:T(8,128)S(1)} %get-tuple-element.43.head_ref, ...), custom_call_target="tpu_custom_call" | custom-call | tf_op jit(solution)/shard_map/pallas_call | solution.py:432
  13.4 12.6 %all-to-all-start = ((bf16[32,176,128]{2,1,0:T(8,128)(2,1)}), bf16[32,176,128]{2,1,0:T(8,128)(2,1)S(1)}, u32[]{:S(2)}, u32[]{:S(2)}) async-start(bf16[32,176,128]{2,1,0:T(8,128)(2,1)} %shard_map.119), calls=%async_computation | async-start | bytes 2883584 | tf_op jit(solution)/shard_map/all_to_all | solution.py:504
  26.0 16.8 %shard_map.120 = (f32[256,2560]{1,0:T(8,128)}, bf16[256,2560]{1,0:T(8,128)(2,1)}, bf16[2560,256]{1,0:T(8,128)(2,1)}, bf16[2560,256]{1,0:T(8,128)(2,1)}, bf16[256...) custom-call(bf16[256,2816]{1,0:T(8,128)(2,1)} %bitcast.14, ...), custom_call_target="tpu_custom_call" | custom-call | tf_op jit(solution)/shard_map/pallas_call | solution.py:432
  42.9 18.4 %all-to-all-done.got_ref = bf16[32,176,128]{2,1,0:T(8,128)(2,1)S(1)} async-done(((bf16[32,176,128]{2,1,0:T(8,128)(2,1)}), bf16[32,176,128]{2,1,0:T(8,128)(2,1)S(1)}, u32[]{:S(2)}, u32[]{:S(2)}) %all-to-all-start) | async-done | bytes 1441824 | tf_op jit(solution)/shard_map/all_to_all | solution.py:504
  61.3 1.4 shard_map.121
  62.8 39.7 %all_to_all.10.back_ref = bf16[32,160,128]{2,1,0:T(8,128)(2,1)S(1)} all-to-all(bf16[32,160,128]{2,1,0:T(8,128)(2,1)} %shard_map.121), channel_id=1, replica_groups=mesh['dp'=8,'seq'=32] {'seq'}, dimensions={0} | all-to-all | bytes 2621440 | tf_op jit(solution)/shard_map/all_to_all | solution.py:542
  102.6 9.1 %shard_map.122 = (bf16[256,2816]{1,0:T(8,128)(2,1)}, f32[16,2816]{1,0:T(8,128)S(1)}, f32[3,2816]{1,0:T(4,128)S(1)}, f32[40,256]{1,0:T(8,128)S(1)}, f32[40,256]{1...) custom-call(bf16[32,160,128]{2,1,0:T(8,128)(2,1)S(1)} %all_to_all.10.back_ref, ...), custom_call_target="tpu_custom_call" | custom-call | tf_op jit(solution)/shard_map/pallas_call | solution.py:432
  111.9 1.2 collective-permute-done.1
  113.1 1.6 %collective-permute-start.2 = (f32[112,128]{1,0:T(8,128)S(1)}, f32[112,128]{1,0:T(8,128)S(1)}, u32[]{:S(2)}, u32[]{:S(2)}) collective-permute-start(f32[112,128]{1,0:T(8,128)S(1)} %add.41), channel_id=1, source_target_pairs={{0,64},{32,96},{64,0},{96,32},{128,192},{160,224},{192,128},{224,1... | collective-permute-start | bytes 172040 | tf_op jit(solution)/shard_map/ppermute | solution.py:452
  114.7 2.7 %collective-permute-start.3 = (f32[112,128]{1,0:T(8,128)S(1)}, f32[112,128]{1,0:T(8,128)S(1)}, u32[]{:S(2)}, u32[]{:S(2)}) collective-permute-start(f32[112,128]{1,0:T(8,128)S(1)} %add.41), channel_id=1, source_target_pairs={{0,128},{32,160},{64,192},{96,224},{128,0},{160,32},{192,64},{224,... | collective-permute-start | bytes 172040 | tf_op jit(solution)/shard_map/ppermute | solution.py:452
  117.9 2.7 %collective-permute-done.3 = f32[112,128]{1,0:T(8,128)S(1)} collective-permute-done((f32[112,128]{1,0:T(8,128)S(1)}, f32[112,128]{1,0:T(8,128)S(1)}, u32[]{:S(2)}, u32[]{:S(2)}) %collective-permute-start.3) | collective-permute-done | bytes 57376 | tf_op jit(solution)/shard_map/ppermute | solution.py:452
  120.5 2.3 %collective-permute-done.4 = f32[112,128]{1,0:T(8,128)S(1)} collective-permute-done((f32[112,128]{1,0:T(8,128)S(1)}, f32[112,128]{1,0:T(8,128)S(1)}, u32[]{:S(2)}, u32[]{:S(2)}) %collective-permute-start.4) | collective-permute-done | bytes 57376 | tf_op jit(solution)/shard_map/ppermute | solution.py:452
  122.8 0.6 collective-permute-start.5
  123.4 2.1 %collective-permute-start.6 = (f32[112,128]{1,0:T(8,128)S(1)}, f32[112,128]{1,0:T(8,128)S(1)}, u32[]{:S(2)}, u32[]{:S(2)}) collective-permute-start(f32[112,128]{1,0:T(8,128)S(1)} %add_add_fusion.2), channel_id=1, source_target_pairs={{0,16},{1,17},{2,18},{3,19},{4,20},{5,21},{6,22},{7,23},{8,24},{9,... | collective-permute-start | bytes 172040 | tf_op jit(solution)/shard_map/ppermute | solution.py:452
  125.6 2.0 %collective-permute-start.7 = (f32[112,128]{1,0:T(8,128)S(1)}, f32[112,128]{1,0:T(8,128)S(1)}, u32[]{:S(2)}, u32[]{:S(2)}) collective-permute-start(f32[112,128]{1,0:T(8,128)S(1)} %add_add_fusion.2), channel_id=1, source_target_pairs={{0,24},{1,25},{2,26},{3,27},{4,28},{5,29},{6,30},{7,31},{8,16},{9,... | collective-permute-start | bytes 172040 | tf_op jit(solution)/shard_map/ppermute | solution.py:452
  127.6 1.5 %collective-permute-done.6 = f32[112,128]{1,0:T(8,128)S(1)} collective-permute-done((f32[112,128]{1,0:T(8,128)S(1)}, f32[112,128]{1,0:T(8,128)S(1)}, u32[]{:S(2)}, u32[]{:S(2)}) %collective-permute-start.6) | collective-permute-done | bytes 57376 | tf_op jit(solution)/shard_map/ppermute | solution.py:452
  129.1 1.8 %collective-permute-done.7 = f32[112,128]{1,0:T(8,128)S(1)} collective-permute-done((f32[112,128]{1,0:T(8,128)S(1)}, f32[112,128]{1,0:T(8,128)S(1)}, u32[]{:S(2)}, u32[]{:S(2)}) %collective-permute-start.7) | collective-permute-done | bytes 57376 | tf_op jit(solution)/shard_map/ppermute | solution.py:452
  131.0 0.9 collective-permute-start.10
  131.9 1.5 collective-permute-start.8
  133.3 1.2 collective-permute-start.9
  134.6 0.6 collective-permute-done.10
  135.2 0.9 collective-permute-done.8
  136.1 2.4 %collective-permute-done.9 = f32[112,128]{1,0:T(8,128)S(1)} collective-permute-done((f32[112,128]{1,0:T(8,128)S(1)}, f32[112,128]{1,0:T(8,128)S(1)}, u32[]{:S(2)}, u32[]{:S(2)}) %collective-permute-start.9) | collective-permute-done | bytes 57376 | tf_op jit(solution)/shard_map/ppermute | solution.py:452
  138.5 2.4 %collective-permute-start.11 = (f32[3,2816]{1,0:T(4,128)S(1)}, f32[3,2816]{1,0:T(4,128)S(1)}, u32[]{:S(2)}, u32[]{:S(2)}) collective-permute-start(f32[3,2816]{1,0:T(4,128)S(1)} %get-tuple-element.65), channel_id=1, source_target_pairs={{1,0},{2,1},{3,2},{4,3},{5,4},{6,5},{7,6},{8,7},{9,8},{10,9},{11,1... | collective-permute-start | bytes 101384 | tf_op jit(solution)/shard_map/ppermute | solution.py:448
  141.0 2.6 %collective-permute-start.12 = (f32[112,128]{1,0:T(8,128)S(1)}, f32[112,128]{1,0:T(8,128)S(1)}, u32[]{:S(2)}, u32[]{:S(2)}) collective-permute-start(f32[112,128]{1,0:T(8,128)S(1)} %add_add_fusion.near_ref), channel_id=1, source_target_pairs={{0,4},{1,5},{2,6},{3,7},{4,0},{5,1},{6,2},{7,3},{8,12},{9,13},{10,... | collective-permute-start | bytes 172040 | tf_op jit(solution)/shard_map/ppermute | solution.py:452
  143.5 1.5 %shard_map.123 = f32[40,256]{1,0:T(8,128)} custom-call(f32[40,256]{1,0:T(8,128)S(1)} %get-tuple-element.66.q_ref, f32[40,256]{1,0:T(8,128)S(1)} %get-tuple-element.67.r_ref, f32[40,128]{1,0:T(8,128)S(1)} %get-tuple-element.68.four_ref, f32[40,256]{1,0:T(8,128)S(1)} %copy-done.5, f32[40,256]{1,0:T(8,128)S(1)} %copy-done.6, f32[40]{0:T(128)S(1)} %copy-done.14), custom_call_target="tpu_custom_call" | custom-call | tf_op jit(solution)/shard_map/pallas_call | solution.py:432
  145.1 0.7 maximum_dynamic-update-slice_fusion
  145.8 3.4 %collective-permute-done.12.far_ref = f32[112,128]{1,0:T(8,128)S(1)} collective-permute-done((f32[112,128]{1,0:T(8,128)S(1)}, f32[112,128]{1,0:T(8,128)S(1)}, u32[]{:S(2)}, u32[]{:S(2)}) %collective-permute-start.12) | collective-permute-done | bytes 57376 | tf_op jit(solution)/shard_map/ppermute | solution.py:452
  149.1 0.7 shard_map.124
  (42 shorter events, 0.8 us)
Async XLA Ops:
  2.8 5.7 %collective-permute-start = (bf16[3,2816]{1,0:T(4,128)(2,1)S(1)}, bf16[3,2816]{1,0:T(4,128)(2,1)S(1)}, u32[]{:S(2)}, u32[]{:S(2)}) collective-permute-start(bf16[3,2816]{1,0:T(4,128)(2,1)S(1)} %get-tuple-element.40), channel_id=1, source_target_pairs={{0,1},{1,2},{2,3},{3,4},{4,5},{5,6},{6,7},{7,8},{8,9},{9,10},{10,1... | collective-permute-start | bytes 50696 | tf_op jit(solution)/shard_map/ppermute | solution.py:448
  8.5 4.9 %copy-start.3 = (bf16[3,2816]{1,0:T(4,128)(2,1)}, bf16[3,2816]{1,0:T(4,128)(2,1)S(1)}, u32[]{:S(2)}) copy-start(bf16[3,2816]{1,0:T(4,128)(2,1)S(1)} %collective-permute-done.halo_ref) | copy-start | bytes 50692
  13.4 47.8 %all-to-all-start = ((bf16[32,176,128]{2,1,0:T(8,128)(2,1)}), bf16[32,176,128]{2,1,0:T(8,128)(2,1)S(1)}, u32[]{:S(2)}, u32[]{:S(2)}) async-start(bf16[32,176,128]{2,1,0:T(8,128)(2,1)} %shard_map.119), calls=%async_computation | async-start | bytes 2883584 | tf_op jit(solution)/shard_map/all_to_all | solution.py:504
  62.7 39.8 %copy-start = (f32[4,2816]{1,0:T(4,128)S(1)}, f32[4,2816]{1,0:T(4,128)}, u32[]{:S(2)}) copy-start(f32[4,2816]{1,0:T(4,128)} %w_ref.3) | copy-start | bytes 135172
  62.7 39.8 %copy-start.1 = (f32[1,40,256]{2,1,0:T(8,128)S(1)}, f32[1,40,256]{2,1,0:T(8,128)}, u32[]{:S(2)}) copy-start(f32[1,40,256]{2,1,0:T(8,128)} %param.10) | copy-start | bytes 122884
  62.7 39.8 %copy-start.2 = (f32[256,256]{1,0:T(8,128)S(1)}, f32[256,256]{1,0:T(8,128)}, u32[]{:S(2)}) copy-start(f32[256,256]{1,0:T(8,128)} %get-tuple-element.48.slope_ref) | copy-start | bytes 786436
  62.7 39.8 %copy-start.4 = (bf16[3,2816]{1,0:T(4,128)(2,1)S(1)}, bf16[3,2816]{1,0:T(4,128)(2,1)}, u32[]{:S(2)}) copy-start(bf16[3,2816]{1,0:T(4,128)(2,1)} %copy-done.3) | copy-start | bytes 50692
  62.7 39.8 %copy-start.5 = (f32[40,256]{1,0:T(8,128)S(1)}, f32[40,256]{1,0:T(8,128)}, u32[]{:S(2)}) copy-start(f32[40,256]{1,0:T(8,128)} %get-tuple-element.51.colin_ref.col_ref) | copy-start | bytes 122884
  62.7 39.8 %copy-start.6 = (f32[40,256]{1,0:T(8,128)S(1)}, f32[40,256]{1,0:T(8,128)}, u32[]{:S(2)}) copy-start(f32[40,256]{1,0:T(8,128)} %get-tuple-element.52.row_ref) | copy-start | bytes 122884
  62.7 39.8 %copy-start.7 = (bf16[256,256]{1,0:T(8,128)(2,1)S(1)}, bf16[256,256]{1,0:T(8,128)(2,1)}, u32[]{:S(2)}) copy-start(bf16[256,256]{1,0:T(8,128)(2,1)} %get-tuple-element.46.bc_ref) | copy-start | bytes 393220
  62.7 39.8 %copy-start.8 = (bf16[256,256]{1,0:T(8,128)(2,1)S(1)}, bf16[256,256]{1,0:T(8,128)(2,1)}, u32[]{:S(2)}) copy-start(bf16[256,256]{1,0:T(8,128)(2,1)} %get-tuple-element.47.bct_ref) | copy-start | bytes 393220
  62.8 39.8 %copy-start.9 = (f32[128,256]{1,0:T(8,128)S(1)}, f32[128,256]{1,0:T(8,128)}, u32[]{:S(2)}) copy-start(f32[128,256]{1,0:T(8,128)} %get-tuple-element.49.gbin_ref) | copy-start | bytes 393220
  62.8 39.8 %copy-start.10 = (f32[128,256]{1,0:T(8,128)S(1)}, f32[128,256]{1,0:T(8,128)}, u32[]{:S(2)}) copy-start(f32[128,256]{1,0:T(8,128)} %get-tuple-element.50.gcin_ref) | copy-start | bytes 393220
  62.8 39.8 %copy-start.11 = (f32[40,256]{1,0:T(8,128)S(1)}, f32[40,256]{1,0:T(8,128)}, u32[]{:S(2)}) copy-start(f32[40,256]{1,0:T(8,128)} %get-tuple-element.53.skiprow_ref) | copy-start | bytes 122884
  62.8 39.8 %copy-start.12 = (f32[40,256]{1,0:T(8,128)S(1)}, f32[40,256]{1,0:T(8,128)}, u32[]{:S(2)}) copy-start(f32[40,256]{1,0:T(8,128)} %get-tuple-element.54.sofar_ref) | copy-start | bytes 122884
  62.8 39.8 %copy-start.13 = (f32[40,128]{1,0:T(8,128)S(1)}, f32[40,128]{1,0:T(8,128)}, u32[]{:S(2)}) copy-start(f32[40,128]{1,0:T(8,128)} %get-tuple-element.55.end_ref) | copy-start | bytes 61444
  102.6 40.9 %copy-start.14 = (f32[40]{0:T(128)S(1)}, f32[40]{0:T(128)}, u32[]{:S(2)}) copy-start(f32[40]{0:T(128)} %rate_ref.3) | copy-start | bytes 484
  111.8 1.3 collective-permute-start.1
  113.1 4.8 %collective-permute-start.2 = (f32[112,128]{1,0:T(8,128)S(1)}, f32[112,128]{1,0:T(8,128)S(1)}, u32[]{:S(2)}, u32[]{:S(2)}) collective-permute-start(f32[112,128]{1,0:T(8,128)S(1)} %add.41), channel_id=1, source_target_pairs={{0,64},{32,96},{64,0},{96,32},{128,192},{160,224},{192,128},{224,1... | collective-permute-start | bytes 172040 | tf_op jit(solution)/shard_map/ppermute | solution.py:452
  114.7 5.9 %collective-permute-start.3 = (f32[112,128]{1,0:T(8,128)S(1)}, f32[112,128]{1,0:T(8,128)S(1)}, u32[]{:S(2)}, u32[]{:S(2)}) collective-permute-start(f32[112,128]{1,0:T(8,128)S(1)} %add.41), channel_id=1, source_target_pairs={{0,128},{32,160},{64,192},{96,224},{128,0},{160,32},{192,64},{224,... | collective-permute-start | bytes 172040 | tf_op jit(solution)/shard_map/ppermute | solution.py:452
  117.4 5.4 %collective-permute-start.4 = (f32[112,128]{1,0:T(8,128)S(1)}, f32[112,128]{1,0:T(8,128)S(1)}, u32[]{:S(2)}, u32[]{:S(2)}) collective-permute-start(f32[112,128]{1,0:T(8,128)S(1)} %add.41), channel_id=1, source_target_pairs={{0,192},{32,224},{64,128},{96,160},{128,64},{160,96},{192,0},{224,... | collective-permute-start | bytes 172040 | tf_op jit(solution)/shard_map/ppermute | solution.py:452
  122.8 4.8 %collective-permute-start.5 = (f32[112,128]{1,0:T(8,128)S(1)}, f32[112,128]{1,0:T(8,128)S(1)}, u32[]{:S(2)}, u32[]{:S(2)}) collective-permute-start(f32[112,128]{1,0:T(8,128)S(1)} %add_add_fusion.2), channel_id=1, source_target_pairs={{0,8},{1,9},{2,10},{3,11},{4,12},{5,13},{6,14},{7,15},{8,0},{9,1},... | collective-permute-start | bytes 172040 | tf_op jit(solution)/shard_map/ppermute | solution.py:452
  123.4 5.7 %collective-permute-start.6 = (f32[112,128]{1,0:T(8,128)S(1)}, f32[112,128]{1,0:T(8,128)S(1)}, u32[]{:S(2)}, u32[]{:S(2)}) collective-permute-start(f32[112,128]{1,0:T(8,128)S(1)} %add_add_fusion.2), channel_id=1, source_target_pairs={{0,16},{1,17},{2,18},{3,19},{4,20},{5,21},{6,22},{7,23},{8,24},{9,... | collective-permute-start | bytes 172040 | tf_op jit(solution)/shard_map/ppermute | solution.py:452
  125.6 5.4 %collective-permute-start.7 = (f32[112,128]{1,0:T(8,128)S(1)}, f32[112,128]{1,0:T(8,128)S(1)}, u32[]{:S(2)}, u32[]{:S(2)}) collective-permute-start(f32[112,128]{1,0:T(8,128)S(1)} %add_add_fusion.2), channel_id=1, source_target_pairs={{0,24},{1,25},{2,26},{3,27},{4,28},{5,29},{6,30},{7,31},{8,16},{9,... | collective-permute-start | bytes 172040 | tf_op jit(solution)/shard_map/ppermute | solution.py:452
  131.0 4.3 %collective-permute-start.10 = (f32[112,128]{1,0:T(8,128)S(1)}, f32[112,128]{1,0:T(8,128)S(1)}, u32[]{:S(2)}, u32[]{:S(2)}) collective-permute-start(f32[112,128]{1,0:T(8,128)S(1)} %add_add_fusion.1), channel_id=1, source_target_pairs={{0,3},{1,2},{2,1},{3,0},{4,7},{5,6},{6,5},{7,4},{8,11},{9,10},{10,... | collective-permute-start | bytes 172040 | tf_op jit(solution)/shard_map/ppermute | solution.py:452
  131.9 4.3 %collective-permute-start.8 = (f32[112,128]{1,0:T(8,128)S(1)}, f32[112,128]{1,0:T(8,128)S(1)}, u32[]{:S(2)}, u32[]{:S(2)}) collective-permute-start(f32[112,128]{1,0:T(8,128)S(1)} %add_add_fusion.1), channel_id=1, source_target_pairs={{0,1},{1,0},{2,3},{3,2},{4,5},{5,4},{6,7},{7,6},{8,9},{9,8},{10,11... | collective-permute-start | bytes 172040 | tf_op jit(solution)/shard_map/ppermute | solution.py:452
  133.3 5.1 %collective-permute-start.9 = (f32[112,128]{1,0:T(8,128)S(1)}, f32[112,128]{1,0:T(8,128)S(1)}, u32[]{:S(2)}, u32[]{:S(2)}) collective-permute-start(f32[112,128]{1,0:T(8,128)S(1)} %add_add_fusion.1), channel_id=1, source_target_pairs={{0,2},{1,3},{2,0},{3,1},{4,6},{5,7},{6,4},{7,5},{8,10},{9,11},{10,... | collective-permute-start | bytes 172040 | tf_op jit(solution)/shard_map/ppermute | solution.py:452
  138.5 6.6 %collective-permute-start.11 = (f32[3,2816]{1,0:T(4,128)S(1)}, f32[3,2816]{1,0:T(4,128)S(1)}, u32[]{:S(2)}, u32[]{:S(2)}) collective-permute-start(f32[3,2816]{1,0:T(4,128)S(1)} %get-tuple-element.65), channel_id=1, source_target_pairs={{1,0},{2,1},{3,2},{4,3},{5,4},{6,5},{7,6},{8,7},{9,8},{10,9},{11,1... | collective-permute-start | bytes 101384 | tf_op jit(solution)/shard_map/ppermute | solution.py:448
  141.0 8.2 %collective-permute-start.12 = (f32[112,128]{1,0:T(8,128)S(1)}, f32[112,128]{1,0:T(8,128)S(1)}, u32[]{:S(2)}, u32[]{:S(2)}) collective-permute-start(f32[112,128]{1,0:T(8,128)S(1)} %add_add_fusion.near_ref), channel_id=1, source_target_pairs={{0,4},{1,5},{2,6},{3,7},{4,0},{5,1},{6,2},{7,3},{8,12},{9,13},{10,... | collective-permute-start | bytes 172040 | tf_op jit(solution)/shard_map/ppermute | solution.py:452

commit v5 on v4

--- a/solution.py
+++ b/solution.py
@@ -17,7 +17,7 @@
 F32 = jnp.float32
 X_WIDTH = HEADS * HEAD_DIM
 PAIRS = HEADS // 2
-TAIL_ROWS = 16
+TAIL_ROWS = 8
 VMEM_LIMIT = 56 * 1024 * 1024
 SMALL_LIMIT = 24 * 1024 * 1024
 PARTS = 4
@@ -572,12 +572,14 @@
         large=5, limit=SMALL_LIMIT,
     )
     sums = params + flipped(params, "dp", 1)
+    sums, edge = lax.optimization_barrier((sums, edge))
+    next_rows = shifted(edge, "seq", -1)
     sums = four_summed(sums, "dp", 2)
+    sums, q_rows = lax.optimization_barrier((sums, q_rows))
     sums = four_summed(sums, "seq", 8)
+    sums, last = lax.optimization_barrier((sums, last))
     sums = four_summed(sums, "seq", 1)
-    sums, edge, q_rows = lax.optimization_barrier((sums, edge, q_rows))
     far_sums = flipped(sums, "seq", 4)
-    next_rows = shifted(edge, "seq", -1)
     (gsteps,) = call(
         log_kernel, [wide_heads], [], q_rows, r_rows, four, col_sums, row_sums, decay_rates,
         scalars=1, limit=SMALL_LIMIT,

time: 151 us -> 147 us (0.974)
  waiting for transfers between devices: 37 us -> 32.2 us
    ppermute x11, waiting for transfers between devices: 16.7 us -> 13.2 us  [flipped(): lax.ppermute(array, axis, [(i, i ^ bits) for i in range(lax.axis_size(axi...]
  transfers between devices with their start and end apart: 14 -> 14, of which waited for: 11 -> 9; matrix products, arithmetic and copies ran while one was open for 1% -> 1% of each run, Pallas kernels for 12% -> 13%
where the time goes in v5:
time: 147 us; the launch traced here: 145 us
  blocking collectives  38.6 us (26%)
  Pallas kernels  36.6 us (25%)
  starting transfers between devices  36 us (24%)
  waiting for transfers between devices  32.2 us (22%)
    all_to_all x1, blocking collectives, shards(): back = lax.all_to_all(turned, 'seq', 0, 0, tiled=True)  38.6 us
    pallas_call x7, Pallas kernels, call(): pl.pallas_call(kernel, out_shape=[out_space(*out) if large_out or i in ke...  36.6 us
    ppermute x11, starting transfers between devices, flipped(): lax.ppermute(array, axis, [(i, i ^ bits) for i in range(lax.axis_size(axi...  17.3 us
    all_to_all x1, waiting for transfers between devices, shards(): got = lax.all_to_all(msg, 'seq', 0, 0, tiled=True)  17.1 us
    ppermute x11, waiting for transfers between devices, flipped(): lax.ppermute(array, axis, [(i, i ^ bits) for i in range(lax.axis_size(axi...  13.2 us
    all_to_all x1, starting transfers between devices, shards(): got = lax.all_to_all(msg, 'seq', 0, 0, tiled=True)  12.6 us
    ppermute x2, starting transfers between devices, shifted(): return lax.ppermute(array, axis, pairs)  6.13 us
  transfers between devices with their start and end apart: 14, of which 9 were waited for; matrix products, arithmetic and copies ran while one was open for 1% of the time, Pallas kernels for 13%

profile of v5, /device:TPU:32, one launch (start us, length us, event | category | flops | bytes accessed | tf_op | source)
XLA Modules:
  0.0 145.3 jit_solution(1876757129008990132)
XLA Ops:
  0.6 2.2 %shard_map.118 = (bf16[2560,256]{1,0:T(8,128)(2,1)S(1)}, f32[40,256]{1,0:T(8,128)S(1)}, f32[40,256]{1,0:T(8,128)S(1)}, bf16[3,2816]{1,0:T(4,128)(2,1)S(1)}) custom-call(f32[40,256]{1,0:T(8,128)} %bitcast.9, f32[40]{0:T(128)} %rate_ref.3, bf16[256,2560]{1,0:T(8,128)(2,1)} %bitcast.16, bf16[256,2816]{1,0:T(8,128)(2,1)} %bitcast.12), custom_call_target="tpu_custom_call" | custom-call | tf_op jit(solution)/shard_map/pallas_call | solution.py:432
  2.8 3.8 %collective-permute-start = (bf16[3,2816]{1,0:T(4,128)(2,1)S(1)}, bf16[3,2816]{1,0:T(4,128)(2,1)S(1)}, u32[]{:S(2)}, u32[]{:S(2)}) collective-permute-start(bf16[3,2816]{1,0:T(4,128)(2,1)S(1)} %get-tuple-element.43), channel_id=1, source_target_pairs={{0,1},{1,2},{2,3},{3,4},{4,5},{5,6},{6,7},{7,8},{8,9},{9,10},{10,1... | collective-permute-start | bytes 50696 | tf_op jit(solution)/shard_map/ppermute | solution.py:448
  6.6 1.9 %collective-permute-done.halo_ref = bf16[3,2816]{1,0:T(4,128)(2,1)S(1)} collective-permute-done((bf16[3,2816]{1,0:T(4,128)(2,1)S(1)}, bf16[3,2816]{1,0:T(4,128)(2,1)S(1)}, u32[]{:S(2)}, u32[]{:S(2)}) %collective-permute-start) | collective-permute-done | bytes 16928 | tf_op jit(solution)/shard_map/ppermute | solution.py:448
  8.5 4.9 %shard_map.119 = bf16[32,168,128]{2,1,0:T(8,128)(2,1)} custom-call(bf16[3,2816]{1,0:T(4,128)(2,1)S(1)} %collective-permute-done.halo_ref, bf16[2560,256]{1,0:T(8,128)(2,1)S(1)} %get-tuple-element.44.dywt_ref, f32[40,256]{1,0:T(8,128)S(1)} %get-tuple-element.45.tail_ref, f32[40,256]{1,0:T(8,128)S(1)} %get-tuple-element.46.head_ref, ...), custom_call_target="tpu_custom_call" | custom-call | tf_op jit(solution)/shard_map/pallas_call | solution.py:432
  13.4 12.6 %all-to-all-start = ((bf16[32,168,128]{2,1,0:T(8,128)(2,1)}), bf16[32,168,128]{2,1,0:T(8,128)(2,1)S(1)}, u32[]{:S(2)}, u32[]{:S(2)}) async-start(bf16[32,168,128]{2,1,0:T(8,128)(2,1)} %shard_map.119), calls=%async_computation | async-start | bytes 2752512 | tf_op jit(solution)/shard_map/all_to_all | solution.py:504
  26.0 16.8 %shard_map.120 = (f32[256,2560]{1,0:T(8,128)}, bf16[256,2560]{1,0:T(8,128)(2,1)}, bf16[2560,256]{1,0:T(8,128)(2,1)}, bf16[2560,256]{1,0:T(8,128)(2,1)}, bf16[256...) custom-call(bf16[256,2816]{1,0:T(8,128)(2,1)} %bitcast.14, ...), custom_call_target="tpu_custom_call" | custom-call | tf_op jit(solution)/shard_map/pallas_call | solution.py:432
  42.8 17.1 %all-to-all-done.got_ref = bf16[32,168,128]{2,1,0:T(8,128)(2,1)S(1)} async-done(((bf16[32,168,128]{2,1,0:T(8,128)(2,1)}), bf16[32,168,128]{2,1,0:T(8,128)(2,1)S(1)}, u32[]{:S(2)}, u32[]{:S(2)}) %all-to-all-start) | async-done | bytes 1376288 | tf_op jit(solution)/shard_map/all_to_all | solution.py:504
  59.9 1.4 shard_map.121
  61.5 38.6 %all_to_all.10.back_ref = bf16[32,160,128]{2,1,0:T(8,128)(2,1)S(1)} all-to-all(bf16[32,160,128]{2,1,0:T(8,128)(2,1)} %shard_map.121), channel_id=1, replica_groups=mesh['dp'=8,'seq'=32] {'seq'}, dimensions={0} | all-to-all | bytes 2621440 | tf_op jit(solution)/shard_map/all_to_all | solution.py:542
  100.2 9.1 %shard_map.122 = (bf16[256,2816]{1,0:T(8,128)(2,1)}, f32[16,2816]{1,0:T(8,128)S(1)}, f32[3,2816]{1,0:T(4,128)S(1)}, f32[40,256]{1,0:T(8,128)S(1)}, f32[40,256]{1...) custom-call(bf16[32,160,128]{2,1,0:T(8,128)(2,1)S(1)} %all_to_all.10.back_ref, ...), custom_call_target="tpu_custom_call" | custom-call | tf_op jit(solution)/shard_map/pallas_call | solution.py:432
  109.3 0.1 collective-permute-start.1
  109.4 1.2 collective-permute-done.1
  110.7 1.6 %collective-permute-start.2 = (f32[112,128]{1,0:T(8,128)S(1)}, f32[112,128]{1,0:T(8,128)S(1)}, u32[]{:S(2)}, u32[]{:S(2)}) collective-permute-start(f32[112,128]{1,0:T(8,128)S(1)} %add.41), channel_id=1, source_target_pairs={{0,64},{32,96},{64,0},{96,32},{128,192},{160,224},{192,128},{224,1... | collective-permute-start | bytes 172040 | tf_op jit(solution)/shard_map/ppermute | solution.py:452
  112.3 2.7 %collective-permute-start.3 = (f32[112,128]{1,0:T(8,128)S(1)}, f32[112,128]{1,0:T(8,128)S(1)}, u32[]{:S(2)}, u32[]{:S(2)}) collective-permute-start(f32[112,128]{1,0:T(8,128)S(1)} %add.41), channel_id=1, source_target_pairs={{0,128},{32,160},{64,192},{96,224},{128,0},{160,32},{192,64},{224,... | collective-permute-start | bytes 172040 | tf_op jit(solution)/shard_map/ppermute | solution.py:452
  115.0 0.5 collective-permute-start.4
  115.5 2.7 %collective-permute-done.3 = f32[112,128]{1,0:T(8,128)S(1)} collective-permute-done((f32[112,128]{1,0:T(8,128)S(1)}, f32[112,128]{1,0:T(8,128)S(1)}, u32[]{:S(2)}, u32[]{:S(2)}) %collective-permute-start.3) | collective-permute-done | bytes 57376 | tf_op jit(solution)/shard_map/ppermute | solution.py:452
  118.1 2.3 %collective-permute-done.4 = f32[112,128]{1,0:T(8,128)S(1)} collective-permute-done((f32[112,128]{1,0:T(8,128)S(1)}, f32[112,128]{1,0:T(8,128)S(1)}, u32[]{:S(2)}, u32[]{:S(2)}) %collective-permute-start.4) | collective-permute-done | bytes 57376 | tf_op jit(solution)/shard_map/ppermute | solution.py:452
  120.4 0.7 collective-permute-start.5
  121.1 2.0 %collective-permute-start.6 = (f32[112,128]{1,0:T(8,128)S(1)}, f32[112,128]{1,0:T(8,128)S(1)}, u32[]{:S(2)}, u32[]{:S(2)}) collective-permute-start(f32[112,128]{1,0:T(8,128)S(1)} %add_add_fusion.2), channel_id=1, source_target_pairs={{0,16},{1,17},{2,18},{3,19},{4,20},{5,21},{6,22},{7,23},{8,24},{9,... | collective-permute-start | bytes 172040 | tf_op jit(solution)/shard_map/ppermute | solution.py:452
  123.1 2.1 %collective-permute-start.7 = (f32[112,128]{1,0:T(8,128)S(1)}, f32[112,128]{1,0:T(8,128)S(1)}, u32[]{:S(2)}, u32[]{:S(2)}) collective-permute-start(f32[112,128]{1,0:T(8,128)S(1)} %add_add_fusion.2), channel_id=1, source_target_pairs={{0,24},{1,25},{2,26},{3,27},{4,28},{5,29},{6,30},{7,31},{8,16},{9,... | collective-permute-start | bytes 172040 | tf_op jit(solution)/shard_map/ppermute | solution.py:452
  125.2 0.1 slice_reduce_fusion.2
  125.3 2.3 %collective-permute-start.8 = (f32[3,2816]{1,0:T(4,128)S(1)}, f32[3,2816]{1,0:T(4,128)S(1)}, u32[]{:S(2)}, u32[]{:S(2)}) collective-permute-start(f32[3,2816]{1,0:T(4,128)S(1)} %get-tuple-element.71), channel_id=1, source_target_pairs={{1,0},{2,1},{3,2},{4,3},{5,4},{6,5},{7,6},{8,7},{9,8},{10,9},{11,1... | collective-permute-start | bytes 101384 | tf_op jit(solution)/shard_map/ppermute | solution.py:448
  127.6 1.5 %shard_map.123 = f32[40,256]{1,0:T(8,128)} custom-call(f32[40,256]{1,0:T(8,128)S(1)} %get-tuple-element.72.q_ref, f32[40,256]{1,0:T(8,128)S(1)} %get-tuple-element.73.r_ref, f32[40,128]{1,0:T(8,128)S(1)} %get-tuple-element.74.four_ref, f32[40,256]{1,0:T(8,128)S(1)} %copy-done.5, f32[40,256]{1,0:T(8,128)S(1)} %copy-done.6, f32[40]{0:T(128)S(1)} %copy-done.14), custom_call_target="tpu_custom_call" | custom-call | tf_op jit(solution)/shard_map/pallas_call | solution.py:432
  129.2 1.9 %collective-permute-start.10 = (f32[112,128]{1,0:T(8,128)S(1)}, f32[112,128]{1,0:T(8,128)S(1)}, u32[]{:S(2)}, u32[]{:S(2)}) collective-permute-start(f32[112,128]{1,0:T(8,128)S(1)} %add_add_fusion.1), channel_id=1, source_target_pairs={{0,2},{1,3},{2,0},{3,1},{4,6},{5,7},{6,4},{7,5},{8,10},{9,11},{10,... | collective-permute-start | bytes 172040 | tf_op jit(solution)/shard_map/ppermute | solution.py:452
  131.1 2.6 %collective-permute-start.9 = (f32[112,128]{1,0:T(8,128)S(1)}, f32[112,128]{1,0:T(8,128)S(1)}, u32[]{:S(2)}, u32[]{:S(2)}) collective-permute-start(f32[112,128]{1,0:T(8,128)S(1)} %add_add_fusion.1), channel_id=1, source_target_pairs={{0,1},{1,0},{2,3},{3,2},{4,5},{5,4},{6,7},{7,6},{8,9},{9,8},{10,11... | collective-permute-start | bytes 172040 | tf_op jit(solution)/shard_map/ppermute | solution.py:452
  133.7 0.6 collective-permute-done.10
  134.3 0.9 collective-permute-done.11
  135.3 1.2 collective-permute-done.9
  136.4 3.2 %collective-permute-start.12 = (f32[112,128]{1,0:T(8,128)S(1)}, f32[112,128]{1,0:T(8,128)S(1)}, u32[]{:S(2)}, u32[]{:S(2)}) collective-permute-start(f32[112,128]{1,0:T(8,128)S(1)} %add_add_fusion.near_ref), channel_id=1, source_target_pairs={{0,4},{1,5},{2,6},{3,7},{4,0},{5,1},{6,2},{7,3},{8,12},{9,13},{10,... | collective-permute-start | bytes 172040 | tf_op jit(solution)/shard_map/ppermute | solution.py:452
  139.6 0.7 maximum_dynamic-update-slice_fusion
  140.3 4.3 %collective-permute-done.12.far_ref = f32[112,128]{1,0:T(8,128)S(1)} collective-permute-done((f32[112,128]{1,0:T(8,128)S(1)}, f32[112,128]{1,0:T(8,128)S(1)}, u32[]{:S(2)}, u32[]{:S(2)}) %collective-permute-start.12) | collective-permute-done | bytes 57376 | tf_op jit(solution)/shard_map/ppermute | solution.py:452
  144.6 0.7 shard_map.124
  (42 shorter events, 0.2 us)
Async XLA Ops:
  2.8 5.7 %collective-permute-start = (bf16[3,2816]{1,0:T(4,128)(2,1)S(1)}, bf16[3,2816]{1,0:T(4,128)(2,1)S(1)}, u32[]{:S(2)}, u32[]{:S(2)}) collective-permute-start(bf16[3,2816]{1,0:T(4,128)(2,1)S(1)} %get-tuple-element.43), channel_id=1, source_target_pairs={{0,1},{1,2},{2,3},{3,4},{4,5},{5,6},{6,7},{7,8},{8,9},{9,10},{10,1... | collective-permute-start | bytes 50696 | tf_op jit(solution)/shard_map/ppermute | solution.py:448
  8.5 4.9 %copy-start.3 = (bf16[3,2816]{1,0:T(4,128)(2,1)}, bf16[3,2816]{1,0:T(4,128)(2,1)S(1)}, u32[]{:S(2)}) copy-start(bf16[3,2816]{1,0:T(4,128)(2,1)S(1)} %collective-permute-done.halo_ref) | copy-start | bytes 50692
  13.4 46.5 %all-to-all-start = ((bf16[32,168,128]{2,1,0:T(8,128)(2,1)}), bf16[32,168,128]{2,1,0:T(8,128)(2,1)S(1)}, u32[]{:S(2)}, u32[]{:S(2)}) async-start(bf16[32,168,128]{2,1,0:T(8,128)(2,1)} %shard_map.119), calls=%async_computation | async-start | bytes 2752512 | tf_op jit(solution)/shard_map/all_to_all | solution.py:504
  61.3 38.8 %copy-start = (f32[4,2816]{1,0:T(4,128)S(1)}, f32[4,2816]{1,0:T(4,128)}, u32[]{:S(2)}) copy-start(f32[4,2816]{1,0:T(4,128)} %w_ref.3) | copy-start | bytes 135172
  61.3 38.7 %copy-start.1 = (f32[1,40,256]{2,1,0:T(8,128)S(1)}, f32[1,40,256]{2,1,0:T(8,128)}, u32[]{:S(2)}) copy-start(f32[1,40,256]{2,1,0:T(8,128)} %param.10) | copy-start | bytes 122884
  61.4 38.7 %copy-start.2 = (f32[256,256]{1,0:T(8,128)S(1)}, f32[256,256]{1,0:T(8,128)}, u32[]{:S(2)}) copy-start(f32[256,256]{1,0:T(8,128)} %get-tuple-element.51.slope_ref) | copy-start | bytes 786436
  61.4 38.7 %copy-start.4 = (bf16[3,2816]{1,0:T(4,128)(2,1)S(1)}, bf16[3,2816]{1,0:T(4,128)(2,1)}, u32[]{:S(2)}) copy-start(bf16[3,2816]{1,0:T(4,128)(2,1)} %copy-done.3) | copy-start | bytes 50692
  61.4 38.7 %copy-start.5 = (f32[40,256]{1,0:T(8,128)S(1)}, f32[40,256]{1,0:T(8,128)}, u32[]{:S(2)}) copy-start(f32[40,256]{1,0:T(8,128)} %get-tuple-element.54.colin_ref.col_ref) | copy-start | bytes 122884
  61.4 38.7 %copy-start.6 = (f32[40,256]{1,0:T(8,128)S(1)}, f32[40,256]{1,0:T(8,128)}, u32[]{:S(2)}) copy-start(f32[40,256]{1,0:T(8,128)} %get-tuple-element.55.row_ref) | copy-start | bytes 122884
  61.4 38.7 %copy-start.7 = (bf16[256,256]{1,0:T(8,128)(2,1)S(1)}, bf16[256,256]{1,0:T(8,128)(2,1)}, u32[]{:S(2)}) copy-start(bf16[256,256]{1,0:T(8,128)(2,1)} %get-tuple-element.49.bc_ref) | copy-start | bytes 393220
  61.4 38.7 %copy-start.8 = (bf16[256,256]{1,0:T(8,128)(2,1)S(1)}, bf16[256,256]{1,0:T(8,128)(2,1)}, u32[]{:S(2)}) copy-start(bf16[256,256]{1,0:T(8,128)(2,1)} %get-tuple-element.50.bct_ref) | copy-start | bytes 393220
  61.4 38.7 %copy-start.9 = (f32[128,256]{1,0:T(8,128)S(1)}, f32[128,256]{1,0:T(8,128)}, u32[]{:S(2)}) copy-start(f32[128,256]{1,0:T(8,128)} %get-tuple-element.52.gbin_ref) | copy-start | bytes 393220
  61.4 38.7 %copy-start.10 = (f32[128,256]{1,0:T(8,128)S(1)}, f32[128,256]{1,0:T(8,128)}, u32[]{:S(2)}) copy-start(f32[128,256]{1,0:T(8,128)} %get-tuple-element.53.gcin_ref) | copy-start | bytes 393220
  61.4 38.7 %copy-start.11 = (f32[40,256]{1,0:T(8,128)S(1)}, f32[40,256]{1,0:T(8,128)}, u32[]{:S(2)}) copy-start(f32[40,256]{1,0:T(8,128)} %get-tuple-element.56.skiprow_ref) | copy-start | bytes 122884
  61.4 38.7 %copy-start.12 = (f32[40,256]{1,0:T(8,128)S(1)}, f32[40,256]{1,0:T(8,128)}, u32[]{:S(2)}) copy-start(f32[40,256]{1,0:T(8,128)} %get-tuple-element.57.sofar_ref) | copy-start | bytes 122884
  61.5 38.7 %copy-start.13 = (f32[40,128]{1,0:T(8,128)S(1)}, f32[40,128]{1,0:T(8,128)}, u32[]{:S(2)}) copy-start(f32[40,128]{1,0:T(8,128)} %get-tuple-element.58.end_ref) | copy-start | bytes 61444
  100.2 27.4 %copy-start.14 = (f32[40]{0:T(128)S(1)}, f32[40]{0:T(128)}, u32[]{:S(2)}) copy-start(f32[40]{0:T(128)} %rate_ref.3) | copy-start | bytes 484
  109.3 1.3 collective-permute-start.1
  110.7 4.8 %collective-permute-start.2 = (f32[112,128]{1,0:T(8,128)S(1)}, f32[112,128]{1,0:T(8,128)S(1)}, u32[]{:S(2)}, u32[]{:S(2)}) collective-permute-start(f32[112,128]{1,0:T(8,128)S(1)} %add.41), channel_id=1, source_target_pairs={{0,64},{32,96},{64,0},{96,32},{128,192},{160,224},{192,128},{224,1... | collective-permute-start | bytes 172040 | tf_op jit(solution)/shard_map/ppermute | solution.py:452
  112.3 5.9 %collective-permute-start.3 = (f32[112,128]{1,0:T(8,128)S(1)}, f32[112,128]{1,0:T(8,128)S(1)}, u32[]{:S(2)}, u32[]{:S(2)}) collective-permute-start(f32[112,128]{1,0:T(8,128)S(1)} %add.41), channel_id=1, source_target_pairs={{0,128},{32,160},{64,192},{96,224},{128,0},{160,32},{192,64},{224,... | collective-permute-start | bytes 172040 | tf_op jit(solution)/shard_map/ppermute | solution.py:452
  115.0 5.4 %collective-permute-start.4 = (f32[112,128]{1,0:T(8,128)S(1)}, f32[112,128]{1,0:T(8,128)S(1)}, u32[]{:S(2)}, u32[]{:S(2)}) collective-permute-start(f32[112,128]{1,0:T(8,128)S(1)} %add.41), channel_id=1, source_target_pairs={{0,192},{32,224},{64,128},{96,160},{128,64},{160,96},{192,0},{224,... | collective-permute-start | bytes 172040 | tf_op jit(solution)/shard_map/ppermute | solution.py:452
  120.4 8.7 %collective-permute-start.5 = (f32[112,128]{1,0:T(8,128)S(1)}, f32[112,128]{1,0:T(8,128)S(1)}, u32[]{:S(2)}, u32[]{:S(2)}) collective-permute-start(f32[112,128]{1,0:T(8,128)S(1)} %add_add_fusion.2), channel_id=1, source_target_pairs={{0,8},{1,9},{2,10},{3,11},{4,12},{5,13},{6,14},{7,15},{8,0},{9,1},... | collective-permute-start | bytes 172040 | tf_op jit(solution)/shard_map/ppermute | solution.py:452
  121.1 8.0 %collective-permute-start.6 = (f32[112,128]{1,0:T(8,128)S(1)}, f32[112,128]{1,0:T(8,128)S(1)}, u32[]{:S(2)}, u32[]{:S(2)}) collective-permute-start(f32[112,128]{1,0:T(8,128)S(1)} %add_add_fusion.2), channel_id=1, source_target_pairs={{0,16},{1,17},{2,18},{3,19},{4,20},{5,21},{6,22},{7,23},{8,24},{9,... | collective-permute-start | bytes 172040 | tf_op jit(solution)/shard_map/ppermute | solution.py:452
  123.1 6.1 %collective-permute-start.7 = (f32[112,128]{1,0:T(8,128)S(1)}, f32[112,128]{1,0:T(8,128)S(1)}, u32[]{:S(2)}, u32[]{:S(2)}) collective-permute-start(f32[112,128]{1,0:T(8,128)S(1)} %add_add_fusion.2), channel_id=1, source_target_pairs={{0,24},{1,25},{2,26},{3,27},{4,28},{5,29},{6,30},{7,31},{8,16},{9,... | collective-permute-start | bytes 172040 | tf_op jit(solution)/shard_map/ppermute | solution.py:452
  125.3 8.4 %collective-permute-start.8 = (f32[3,2816]{1,0:T(4,128)S(1)}, f32[3,2816]{1,0:T(4,128)S(1)}, u32[]{:S(2)}, u32[]{:S(2)}) collective-permute-start(f32[3,2816]{1,0:T(4,128)S(1)} %get-tuple-element.71), channel_id=1, source_target_pairs={{1,0},{2,1},{3,2},{4,3},{5,4},{6,5},{7,6},{8,7},{9,8},{10,9},{11,1... | collective-permute-start | bytes 101384 | tf_op jit(solution)/shard_map/ppermute | solution.py:448
  129.2 5.2 %collective-permute-start.10 = (f32[112,128]{1,0:T(8,128)S(1)}, f32[112,128]{1,0:T(8,128)S(1)}, u32[]{:S(2)}, u32[]{:S(2)}) collective-permute-start(f32[112,128]{1,0:T(8,128)S(1)} %add_add_fusion.1), channel_id=1, source_target_pairs={{0,2},{1,3},{2,0},{3,1},{4,6},{5,7},{6,4},{7,5},{8,10},{9,11},{10,... | collective-permute-start | bytes 172040 | tf_op jit(solution)/shard_map/ppermute | solution.py:452
  131.1 4.2 %collective-permute-start.11 = (f32[112,128]{1,0:T(8,128)S(1)}, f32[112,128]{1,0:T(8,128)S(1)}, u32[]{:S(2)}, u32[]{:S(2)}) collective-permute-start(f32[112,128]{1,0:T(8,128)S(1)} %add_add_fusion.1), channel_id=1, source_target_pairs={{0,3},{1,2},{2,1},{3,0},{4,7},{5,6},{6,5},{7,4},{8,11},{9,10},{10,... | collective-permute-start | bytes 172040 | tf_op jit(solution)/shard_map/ppermute | solution.py:452
  131.1 5.3 %collective-permute-start.9 = (f32[112,128]{1,0:T(8,128)S(1)}, f32[112,128]{1,0:T(8,128)S(1)}, u32[]{:S(2)}, u32[]{:S(2)}) collective-permute-start(f32[112,128]{1,0:T(8,128)S(1)} %add_add_fusion.1), channel_id=1, source_target_pairs={{0,1},{1,0},{2,3},{3,2},{4,5},{5,4},{6,7},{7,6},{8,9},{9,8},{10,11... | collective-permute-start | bytes 172040 | tf_op jit(solution)/shard_map/ppermute | solution.py:452
  136.4 8.2 %collective-permute-start.12 = (f32[112,128]{1,0:T(8,128)S(1)}, f32[112,128]{1,0:T(8,128)S(1)}, u32[]{:S(2)}, u32[]{:S(2)}) collective-permute-start(f32[112,128]{1,0:T(8,128)S(1)} %add_add_fusion.near_ref), channel_id=1, source_target_pairs={{0,4},{1,5},{2,6},{3,7},{4,0},{5,1},{6,2},{7,3},{8,12},{9,13},{10,... | collective-permute-start | bytes 172040 | tf_op jit(solution)/shard_map/ppermute | solution.py:452

commit v6 on v4

--- a/solution.py
+++ b/solution.py
@@ -17,7 +17,7 @@
 F32 = jnp.float32
 X_WIDTH = HEADS * HEAD_DIM
 PAIRS = HEADS // 2
-TAIL_ROWS = 16
+TAIL_ROWS = 8
 VMEM_LIMIT = 56 * 1024 * 1024
 SMALL_LIMIT = 24 * 1024 * 1024
 PARTS = 4
@@ -85,19 +85,16 @@
 
 
 def decay_kernel(
-    step_hbm, rate_hbm, dy_hbm, x_hbm,
-    dywt_ref, tail_ref, head_ref, rim_ref,
-    step_ref, rate_ref, dy_ref, last_ref, few_sem, dy_sem,
+    step_hbm, rate_hbm, dy_hbm,
+    dywt_ref, tail_ref, head_ref,
+    step_ref, rate_ref, dy_ref, few_sem, dy_sem,
 ):
     span = X_WIDTH // PARTS
-    few = started(
-        few_sem, (step_hbm, step_ref), (rate_hbm, rate_ref), (x_hbm.at[GROUP - 16 :], last_ref)
-    )
+    few = started(few_sem, (step_hbm, step_ref), (rate_hbm, rate_ref))
     cuts = [slice(g * span, (g + 1) * span) for g in range(PARTS)]
     many = started(dy_sem, *[(dy_hbm.at[:, cut], dy_ref.at[:, cut]) for cut in cuts])
     for copy in few:
         copy.wait()
-    rim_ref[...] = last_ref[...].astype(F32)[16 - (KCONV - 1) :].astype(BF16)
     cum = logs_of(step_ref, rate_ref)
     tail_ref[...] = jnp.exp(cum[:, GROUP - 1 :] - cum)
     head_ref[...] = jnp.exp(cum)
@@ -287,9 +284,9 @@
 def back_kernel(
     back_ref, bc_ref, bct_ref, slope_ref,
     gbin_ref, gcin_ref, colin_ref, row_ref, skiprow_ref,
-    halo_ref, w_ref, step_ref, sofar_ref, end_ref,
+    halo_ref, step_ref, sofar_ref, end_ref,
     own_hbm, scale_hbm, xwt_hbm, dywt_hbm, x_hbm,
-    gin_ref, last_ref, edge_ref, q_ref, r_ref, four_ref, params_ref,
+    gpre_ref, edge_ref, q_ref, r_ref, four_ref, params_ref,
     own_ref, scale_ref, xwt_ref, dywt_ref, x_ref,
     cdot_ref, bdot_ref, btok_ref, product_ref, grad_ref, sums_ref, flip_ref, part_sem,
     *, chunks, rows,
@@ -301,22 +298,19 @@
 
     def finish(c, grad):
         edge_ref[:, lanes(c)] = grad[:rim]
+        gpre_ref[:, lanes(c)] = grad
         x = x_ref[:, lanes(c)].astype(F32)
         halo = halo_ref[:, lanes(c)].astype(F32)
         full = jnp.concatenate([grad, jnp.zeros((8, LANE), F32)], axis=0)
-        spread = w_ref[rim : rim + 1, lanes(c)] * grad
         found = []
         for k in range(rim):
             moved = full[rim - k : rim - k + GROUP]
-            spread = spread + w_ref[k : k + 1, lanes(c)] * moved
             entering = jnp.sum(grad[: rim - k] * halo[k:], axis=0, keepdims=True)
             found.append(jnp.sum(moved * x, axis=0, keepdims=True) + entering)
         found.append(jnp.sum(grad * x, axis=0, keepdims=True))
         found.append(jnp.sum(grad, axis=0, keepdims=True))
         found.append(jnp.zeros((8 - len(found), LANE), F32))
         sums_ref[c] = jnp.concatenate(found, axis=0)
-        gin_ref[:, lanes(c)] = spread.astype(BF16)
-        last_ref[:, lanes(c)] = spread[GROUP - 16 :]
 
     def begin(g):
         if g == PARTS:
@@ -394,6 +388,22 @@
             params_ref[at : at + 1, :] = sums[k : k + 1]
     at = (KCONV + 1) * tiles
     params_ref[at : at + 2, :] = flip_ref[...].T[:2]
+
+
+def spread_kernel(gpre_ref, next_ref, w_ref, gin_ref):
+    rim = KCONV - 1
+
+    def tile(c, carry):
+        grad = gpre_ref[:, lanes(c)]
+        below = jnp.concatenate([next_ref[:, lanes(c)], jnp.zeros((8 - rim, LANE), F32)], axis=0)
+        full = jnp.concatenate([grad, below], axis=0)
+        spread = w_ref[rim : rim + 1, lanes(c)] * grad
+        for k in range(rim):
+            spread = spread + w_ref[k : k + 1, lanes(c)] * full[rim - k : rim - k + GROUP]
+        gin_ref[:, lanes(c)] = spread.astype(BF16)
+        return carry
+
+    lax.fori_loop(0, PAIRS + 2, tile, 0, unroll=2)
 
 
 def log_kernel(q_ref, r_ref, four_ref, col_ref, row_ref, rate_ref, gsteps_ref):
@@ -470,20 +480,13 @@
     wide_heads = ((HEADS, GROUP), F32)
     by_head = ((X_WIDTH, GROUP), BF16)
     dma = pltpu.SemaphoreType.DMA
-    dywt, tail, head, x_rim = call(
+    halo = shifted(x_in[GROUP - rim :], "seq", 1)
+    dywt, tail, head = call(
         decay_kernel,
-        [((X_WIDTH, GROUP), BF16), wide_heads, wide_heads, ((rim, channels), BF16)],
-        [
-            wide_heads,
-            pltpu.SMEM((HEADS,), F32),
-            ((GROUP, X_WIDTH), BF16),
-            ((16, channels), BF16),
-            dma((3,)),
-            dma((PARTS,)),
-        ],
-        steps, decay_rates, dy, x_in, large=4, kept=(0,), limit=SMALL_LIMIT,
-    )
-    halo = shifted(x_rim, "seq", 1)
+        [((X_WIDTH, GROUP), BF16), wide_heads, wide_heads],
+        [wide_heads, pltpu.SMEM((HEADS,), F32), ((GROUP, X_WIDTH), BF16), dma((2,)), dma((PARTS,))],
+        steps, decay_rates, dy, large=3, kept=(0,), limit=SMALL_LIMIT,
+    )
     (msg,) = call(
         functools.partial(front_kernel, chunks=chunks, rows=rows),
         [((chunks, 2 * rows + TAIL_ROWS, LANE), BF16)],
@@ -540,11 +543,10 @@
         got, large_out=True, limit=SMALL_LIMIT,
     )
     back = lax.all_to_all(turned, "seq", 0, 0, tiled=True)
-    grad_in, last, edge, q_rows, r_rows, four, params = call(
+    gpre, edge, q_rows, r_rows, four, params = call(
         functools.partial(back_kernel, chunks=chunks, rows=rows),
         [
-            ((GROUP, channels), BF16),
-            ((16, channels), F32),
+            ((GROUP, channels), F32),
             ((rim, channels), F32),
             wide_heads,
             wide_heads,
@@ -567,27 +569,28 @@
             dma((PARTS + 1, 5)),
         ],
         back, bc, bct, slope, gb, gc, col_sums, row_sums, skip_rows,
-        halo, conv_weight, steps, sofar, d_end,
+        halo, steps, sofar, d_end,
         own, scale, xwt, dywt, x_in,
         large=5, limit=SMALL_LIMIT,
     )
     sums = params + flipped(params, "dp", 1)
-    sums = four_summed(sums, "dp", 2)
-    sums = four_summed(sums, "seq", 8)
-    sums = four_summed(sums, "seq", 1)
     sums, edge, q_rows = lax.optimization_barrier((sums, edge, q_rows))
-    far_sums = flipped(sums, "seq", 4)
     next_rows = shifted(edge, "seq", -1)
     (gsteps,) = call(
         log_kernel, [wide_heads], [], q_rows, r_rows, four, col_sums, row_sums, decay_rates,
         scalars=1, limit=SMALL_LIMIT,
     )
-    ahead = jnp.concatenate([jnp.zeros_like(next_rows), next_rows], axis=0)
-    added = last[16 - rim :]
-    for k in range(rim):
-        added = added + conv_weight[k][None] * ahead[rim - k : 2 * rim - k]
-    ending = jnp.concatenate([last[: 16 - rim], added], axis=0).astype(BF16)
-    grad_in = lax.dynamic_update_slice(grad_in, ending, (GROUP - 16, 0))
+    sums = four_summed(sums, "dp", 2)
+    sums, gsteps = lax.optimization_barrier((sums, gsteps))
+    sums = four_summed(sums, "seq", 8)
+    sums, next_rows = lax.optimization_barrier((sums, next_rows))
+    sums = four_summed(sums, "seq", 1)
+    sums, gpre = lax.optimization_barrier((sums, gpre))
+    far_sums = flipped(sums, "seq", 4)
+    (grad_in,) = call(
+        spread_kernel, [((GROUP, channels), BF16)], [], gpre, next_rows, conv_weight,
+        limit=SMALL_LIMIT,
+    )
     grad_weight, grad_bias, grad_rates, grad_skip = call(
         unpack_kernel,
         [((KCONV, channels), F32), ((channels,), F32), ((HEADS,), F32), ((HEADS,), F32)],

time: 151 us -> 144 us (0.954)
  starting transfers between devices: 34.6 us -> 31.5 us
  waiting for transfers between devices: 37 us -> 34.2 us
    ppermute x11, waiting for transfers between devices: 16.7 us -> 12.3 us  [flipped(): lax.ppermute(array, axis, [(i, i ^ bits) for i in range(lax.axis_size(axi...]
    ppermute x2, waiting for transfers between devices: 1.87 us -> 4.85 us  [shifted(): return lax.ppermute(array, axis, pairs)]
    ppermute x11, starting transfers between devices: 15.8 us -> 12.9 us  [flipped(): lax.ppermute(array, axis, [(i, i ^ bits) for i in range(lax.axis_size(axi...]
    pallas_call x7 -> x8, Pallas kernels: 36.6 us -> 36.5 us  [call(): pl.pallas_call(kernel, out_shape=[out_space(*out) if large_out or i in ke...]
  transfers between devices with their start and end apart: 14 -> 14, of which waited for: 11 -> 10; matrix products, arithmetic and copies ran while one was open for 1% -> 0% of each run, Pallas kernels for 12% -> 16%
where the time goes in v6:
time: 144 us; the launch traced here: 143 us
  blocking collectives  38.6 us (27%)
  Pallas kernels  36.5 us (25%)
  waiting for transfers between devices  34.2 us (24%)
  starting transfers between devices  31.5 us (22%)
    all_to_all x1, blocking collectives, shards(): back = lax.all_to_all(turned, 'seq', 0, 0, tiled=True)  38.6 us
    pallas_call x8, Pallas kernels, call(): pl.pallas_call(kernel, out_shape=[out_space(*out) if large_out or i in ke...  36.5 us
    all_to_all x1, waiting for transfers between devices, shards(): got = lax.all_to_all(msg, 'seq', 0, 0, tiled=True)  17 us
    ppermute x11, starting transfers between devices, flipped(): lax.ppermute(array, axis, [(i, i ^ bits) for i in range(lax.axis_size(axi...  12.9 us
    all_to_all x1, starting transfers between devices, shards(): got = lax.all_to_all(msg, 'seq', 0, 0, tiled=True)  12.5 us
    ppermute x11, waiting for transfers between devices, flipped(): lax.ppermute(array, axis, [(i, i ^ bits) for i in range(lax.axis_size(axi...  12.3 us
    ppermute x2, starting transfers between devices, shifted(): return lax.ppermute(array, axis, pairs)  6.13 us
    ppermute x2, waiting for transfers between devices, shifted(): return lax.ppermute(array, axis, pairs)  4.85 us
  transfers between devices with their start and end apart: 14, of which 10 were waited for; matrix products, arithmetic and copies ran while one was open for 0% of the time, Pallas kernels for 16%

profile of v6, /device:TPU:32, one launch (start us, length us, event | category | flops | bytes accessed | tf_op | source)
XLA Modules:
  0.0 142.8 jit_solution(9946841065130106527)
XLA Ops:
  0.6 0.8 slice_bitcast_fusion
  1.4 3.8 %collective-permute-start = (bf16[3,2816]{1,0:T(4,128)(2,1)S(1)}, bf16[3,2816]{1,0:T(4,128)(2,1)S(1)}, u32[]{:S(2)}, u32[]{:S(2)}) collective-permute-start(bf16[3,2816]{1,0:T(4,128)(2,1)S(1)} %slice_bitcast_fusion), channel_id=1, source_target_pairs={{0,1},{1,2},{2,3},{3,4},{4,5},{5,6},{6,7},{7,8},{8,9},{9,10},{10,1... | collective-permute-start | bytes 50696 | tf_op jit(solution)/shard_map/ppermute | solution.py:458
  5.3 1.9 %shard_map.118 = (bf16[2560,256]{1,0:T(8,128)(2,1)S(1)}, f32[40,256]{1,0:T(8,128)S(1)}, f32[40,256]{1,0:T(8,128)S(1)}) custom-call(f32[40,256]{1,0:T(8,128)} %bitcast.7, f32[40]{0:T(128)} %rate_ref.3, bf16[256,2560]{1,0:T(8,128)(2,1)} %bitcast.13), custom_call_target="tpu_custom_call" | custom-call | tf_op jit(solution)/shard_map/pallas_call | solution.py:442
  7.2 4.9 %shard_map.119 = bf16[32,168,128]{2,1,0:T(8,128)(2,1)} custom-call(bf16[3,2816]{1,0:T(4,128)(2,1)S(1)} %collective-permute-done.halo_ref, bf16[2560,256]{1,0:T(8,128)(2,1)S(1)} %get-tuple-element.44.dywt_ref, f32[40,256]{1,0:T(8,128)S(1)} %get-tuple-element.45.tail_ref, f32[40,256]{1,0:T(8,128)S(1)} %get-tuple-element.46.head_ref, ...), custom_call_target="tpu_custom_call" | custom-call | tf_op jit(solution)/shard_map/pallas_call | solution.py:442
  12.1 12.5 %all-to-all-start = ((bf16[32,168,128]{2,1,0:T(8,128)(2,1)}), bf16[32,168,128]{2,1,0:T(8,128)(2,1)S(1)}, u32[]{:S(2)}, u32[]{:S(2)}) async-start(bf16[32,168,128]{2,1,0:T(8,128)(2,1)} %shard_map.119), calls=%async_computation | async-start | bytes 2752512 | tf_op jit(solution)/shard_map/all_to_all | solution.py:507
  24.6 16.9 %shard_map.120 = (f32[256,2560]{1,0:T(8,128)}, bf16[256,2560]{1,0:T(8,128)(2,1)}, bf16[2560,256]{1,0:T(8,128)(2,1)}, bf16[2560,256]{1,0:T(8,128)(2,1)}, bf16[256...) custom-call(bf16[256,2816]{1,0:T(8,128)(2,1)} %bitcast.11, ...), custom_call_target="tpu_custom_call" | custom-call | tf_op jit(solution)/shard_map/pallas_call | solution.py:442
  41.6 17.0 %all-to-all-done.got_ref = bf16[32,168,128]{2,1,0:T(8,128)(2,1)S(1)} async-done(((bf16[32,168,128]{2,1,0:T(8,128)(2,1)}), bf16[32,168,128]{2,1,0:T(8,128)(2,1)S(1)}, u32[]{:S(2)}, u32[]{:S(2)}) %all-to-all-start) | async-done | bytes 1376288 | tf_op jit(solution)/shard_map/all_to_all | solution.py:507
  58.6 1.4 shard_map.121
  60.1 38.6 %all_to_all.10.back_ref = bf16[32,160,128]{2,1,0:T(8,128)(2,1)S(1)} all-to-all(bf16[32,160,128]{2,1,0:T(8,128)(2,1)} %shard_map.121), channel_id=1, replica_groups=mesh['dp'=8,'seq'=32] {'seq'}, dimensions={0} | all-to-all | bytes 2621440 | tf_op jit(solution)/shard_map/all_to_all | solution.py:545
  98.8 6.7 %shard_map.122 = (f32[256,2816]{1,0:T(8,128)S(1)}, f32[3,2816]{1,0:T(4,128)S(1)}, f32[40,256]{1,0:T(8,128)S(1)}, f32[40,256]{1,0:T(8,128)S(1)}, f32[40,128]{1,0:T(8,128)S(1)}, /*index=5*/f32[112,128]{1,0:T(8,128)S(1)}) custom-call(bf16[32,160,128]{2,1,0:T(8,128)(2,1)S(1)} %all_to_all.10.back_ref, bf16[256,256]{1,0:T(8,128)(2,1)S(1)} %copy-done.7, ...), custom_call_target="tpu_custom_call" | custom-call | tf_op jit(solution)/shard_map/pallas_call | solution.py:442
  105.5 0.1 collective-permute-start.1
  105.6 1.2 collective-permute-done.1
  106.8 2.8 %collective-permute-start.4 = (f32[112,128]{1,0:T(8,128)S(1)}, f32[112,128]{1,0:T(8,128)S(1)}, u32[]{:S(2)}, u32[]{:S(2)}) collective-permute-start(f32[112,128]{1,0:T(8,128)S(1)} %add.30), channel_id=1, source_target_pairs={{0,192},{32,224},{64,128},{96,160},{128,64},{160,96},{192,0},{224,... | collective-permute-start | bytes 172040 | tf_op jit(solution)/shard_map/ppermute | solution.py:462
  109.7 0.8 collective-permute-start.3
  110.5 0.5 collective-permute-start.2
  111.0 1.5 %shard_map.123 = f32[40,256]{1,0:T(8,128)} custom-call(f32[40,256]{1,0:T(8,128)S(1)} %get-tuple-element.67.q_ref, f32[40,256]{1,0:T(8,128)S(1)} %get-tuple-element.68.r_ref, f32[40,128]{1,0:T(8,128)S(1)} %get-tuple-element.69.four_ref, f32[40,256]{1,0:T(8,128)S(1)} %copy-done.5, f32[40,256]{1,0:T(8,128)S(1)} %copy-done.6, f32[40]{0:T(128)S(1)} %copy-done.14), custom_call_target="tpu_custom_call" | custom-call | tf_op jit(solution)/shard_map/pallas_call | solution.py:442
  112.6 2.9 %collective-permute-done.3 = f32[112,128]{1,0:T(8,128)S(1)} collective-permute-done((f32[112,128]{1,0:T(8,128)S(1)}, f32[112,128]{1,0:T(8,128)S(1)}, u32[]{:S(2)}, u32[]{:S(2)}) %collective-permute-start.3) | collective-permute-done | bytes 57376 | tf_op jit(solution)/shard_map/ppermute | solution.py:462
  115.5 1.2 collective-permute-start.7
  116.7 1.6 %collective-permute-start.6 = (f32[112,128]{1,0:T(8,128)S(1)}, f32[112,128]{1,0:T(8,128)S(1)}, u32[]{:S(2)}, u32[]{:S(2)}) collective-permute-start(f32[112,128]{1,0:T(8,128)S(1)} %add_add_fusion.2), channel_id=1, source_target_pairs={{0,16},{1,17},{2,18},{3,19},{4,20},{5,21},{6,22},{7,23},{8,24},{9,... | collective-permute-start | bytes 172040 | tf_op jit(solution)/shard_map/ppermute | solution.py:462
  118.3 1.4 collective-permute-start.5
  119.7 2.3 %collective-permute-start.8 = (f32[3,2816]{1,0:T(4,128)S(1)}, f32[3,2816]{1,0:T(4,128)S(1)}, u32[]{:S(2)}, u32[]{:S(2)}) collective-permute-start(f32[3,2816]{1,0:T(4,128)S(1)} %get-tuple-element.71), channel_id=1, source_target_pairs={{1,0},{2,1},{3,2},{4,3},{5,4},{6,5},{7,6},{8,7},{9,8},{10,9},{11,1... | collective-permute-start | bytes 101384 | tf_op jit(solution)/shard_map/ppermute | solution.py:458
  122.0 0.4 collective-permute-done.6
  122.5 4.8 %collective-permute-done.8.next_ref = f32[3,2816]{1,0:T(4,128)S(1)} collective-permute-done((f32[3,2816]{1,0:T(4,128)S(1)}, f32[3,2816]{1,0:T(4,128)S(1)}, u32[]{:S(2)}, u32[]{:S(2)}) %collective-permute-start.8) | collective-permute-done | bytes 33824 | tf_op jit(solution)/shard_map/ppermute | solution.py:458
  127.3 1.1 collective-permute-start.10
  128.4 2.4 %collective-permute-start.9 = (f32[112,128]{1,0:T(8,128)S(1)}, f32[112,128]{1,0:T(8,128)S(1)}, u32[]{:S(2)}, u32[]{:S(2)}) collective-permute-start(f32[112,128]{1,0:T(8,128)S(1)} %add_add_fusion.1), channel_id=1, source_target_pairs={{0,1},{1,0},{2,3},{3,2},{4,5},{5,4},{6,7},{7,6},{8,9},{9,8},{10,11... | collective-permute-start | bytes 172040 | tf_op jit(solution)/shard_map/ppermute | solution.py:462
  130.8 0.7 collective-permute-done.11
  131.5 0.9 collective-permute-done.10
  132.4 1.5 %collective-permute-done.9 = f32[112,128]{1,0:T(8,128)S(1)} collective-permute-done((f32[112,128]{1,0:T(8,128)S(1)}, f32[112,128]{1,0:T(8,128)S(1)}, u32[]{:S(2)}, u32[]{:S(2)}) %collective-permute-start.9) | collective-permute-done | bytes 57376 | tf_op jit(solution)/shard_map/ppermute | solution.py:462
  133.9 1.0 collective-permute-start.12
  134.9 2.5 %shard_map.124 = bf16[256,2816]{1,0:T(8,128)(2,1)} custom-call(f32[256,2816]{1,0:T(8,128)S(1)} %get-tuple-element.74.gpre_ref, f32[3,2816]{1,0:T(4,128)S(1)} %collective-permute-done.8.next_ref, f32[4,2816]{1,0:T(4,128)S(1)} %copy-done), custom_call_target="tpu_custom_call" | custom-call | tf_op jit(solution)/shard_map/pallas_call | solution.py:442
  137.5 4.6 %collective-permute-done.12.far_ref = f32[112,128]{1,0:T(8,128)S(1)} collective-permute-done((f32[112,128]{1,0:T(8,128)S(1)}, f32[112,128]{1,0:T(8,128)S(1)}, u32[]{:S(2)}, u32[]{:S(2)}) %collective-permute-start.12) | collective-permute-done | bytes 57376 | tf_op jit(solution)/shard_map/ppermute | solution.py:462
  142.1 0.7 shard_map.125
  (40 shorter events, 0.2 us)
Async XLA Ops:
  1.4 5.8 %collective-permute-start = (bf16[3,2816]{1,0:T(4,128)(2,1)S(1)}, bf16[3,2816]{1,0:T(4,128)(2,1)S(1)}, u32[]{:S(2)}, u32[]{:S(2)}) collective-permute-start(bf16[3,2816]{1,0:T(4,128)(2,1)S(1)} %slice_bitcast_fusion), channel_id=1, source_target_pairs={{0,1},{1,2},{2,3},{3,4},{4,5},{5,6},{6,7},{7,8},{8,9},{9,10},{10,1... | collective-permute-start | bytes 50696 | tf_op jit(solution)/shard_map/ppermute | solution.py:458
  7.2 4.9 %copy-start.3 = (bf16[3,2816]{1,0:T(4,128)(2,1)}, bf16[3,2816]{1,0:T(4,128)(2,1)S(1)}, u32[]{:S(2)}) copy-start(bf16[3,2816]{1,0:T(4,128)(2,1)S(1)} %collective-permute-done.halo_ref) | copy-start | bytes 50692
  12.1 46.5 %all-to-all-start = ((bf16[32,168,128]{2,1,0:T(8,128)(2,1)}), bf16[32,168,128]{2,1,0:T(8,128)(2,1)S(1)}, u32[]{:S(2)}, u32[]{:S(2)}) async-start(bf16[32,168,128]{2,1,0:T(8,128)(2,1)} %shard_map.119), calls=%async_computation | async-start | bytes 2752512 | tf_op jit(solution)/shard_map/all_to_all | solution.py:507
  60.0 38.7 %copy-start.1 = (f32[1,40,256]{2,1,0:T(8,128)S(1)}, f32[1,40,256]{2,1,0:T(8,128)}, u32[]{:S(2)}) copy-start(f32[1,40,256]{2,1,0:T(8,128)} %param.10) | copy-start | bytes 122884
  60.0 38.7 %copy-start.2 = (f32[256,256]{1,0:T(8,128)S(1)}, f32[256,256]{1,0:T(8,128)}, u32[]{:S(2)}) copy-start(f32[256,256]{1,0:T(8,128)} %get-tuple-element.51.slope_ref) | copy-start | bytes 786436
  60.0 38.7 %copy-start.4 = (bf16[3,2816]{1,0:T(4,128)(2,1)S(1)}, bf16[3,2816]{1,0:T(4,128)(2,1)}, u32[]{:S(2)}) copy-start(bf16[3,2816]{1,0:T(4,128)(2,1)} %copy-done.3) | copy-start | bytes 50692
  60.0 38.7 %copy-start.5 = (f32[40,256]{1,0:T(8,128)S(1)}, f32[40,256]{1,0:T(8,128)}, u32[]{:S(2)}) copy-start(f32[40,256]{1,0:T(8,128)} %get-tuple-element.54.colin_ref.col_ref) | copy-start | bytes 122884
  60.0 38.7 %copy-start.6 = (f32[40,256]{1,0:T(8,128)S(1)}, f32[40,256]{1,0:T(8,128)}, u32[]{:S(2)}) copy-start(f32[40,256]{1,0:T(8,128)} %get-tuple-element.55.row_ref) | copy-start | bytes 122884
  60.0 38.7 %copy-start.7 = (bf16[256,256]{1,0:T(8,128)(2,1)S(1)}, bf16[256,256]{1,0:T(8,128)(2,1)}, u32[]{:S(2)}) copy-start(bf16[256,256]{1,0:T(8,128)(2,1)} %get-tuple-element.49.bc_ref) | copy-start | bytes 393220
  60.0 38.7 %copy-start.8 = (bf16[256,256]{1,0:T(8,128)(2,1)S(1)}, bf16[256,256]{1,0:T(8,128)(2,1)}, u32[]{:S(2)}) copy-start(bf16[256,256]{1,0:T(8,128)(2,1)} %get-tuple-element.50.bct_ref) | copy-start | bytes 393220
  60.0 38.7 %copy-start.9 = (f32[128,256]{1,0:T(8,128)S(1)}, f32[128,256]{1,0:T(8,128)}, u32[]{:S(2)}) copy-start(f32[128,256]{1,0:T(8,128)} %get-tuple-element.52.gbin_ref) | copy-start | bytes 393220
  60.1 38.7 %copy-start.10 = (f32[128,256]{1,0:T(8,128)S(1)}, f32[128,256]{1,0:T(8,128)}, u32[]{:S(2)}) copy-start(f32[128,256]{1,0:T(8,128)} %get-tuple-element.53.gcin_ref) | copy-start | bytes 393220
  60.1 38.7 %copy-start.11 = (f32[40,256]{1,0:T(8,128)S(1)}, f32[40,256]{1,0:T(8,128)}, u32[]{:S(2)}) copy-start(f32[40,256]{1,0:T(8,128)} %get-tuple-element.56.skiprow_ref) | copy-start | bytes 122884
  60.1 38.7 %copy-start.12 = (f32[40,256]{1,0:T(8,128)S(1)}, f32[40,256]{1,0:T(8,128)}, u32[]{:S(2)}) copy-start(f32[40,256]{1,0:T(8,128)} %get-tuple-element.57.sofar_ref) | copy-start | bytes 122884
  60.1 38.7 %copy-start.13 = (f32[40,128]{1,0:T(8,128)S(1)}, f32[40,128]{1,0:T(8,128)}, u32[]{:S(2)}) copy-start(f32[40,128]{1,0:T(8,128)} %get-tuple-element.58.end_ref) | copy-start | bytes 61444
  98.8 12.2 %copy-start.14 = (f32[40]{0:T(128)S(1)}, f32[40]{0:T(128)}, u32[]{:S(2)}) copy-start(f32[40]{0:T(128)} %rate_ref.3) | copy-start | bytes 484
  98.8 36.1 %copy-start = (f32[4,2816]{1,0:T(4,128)S(1)}, f32[4,2816]{1,0:T(4,128)}, u32[]{:S(2)}) copy-start(f32[4,2816]{1,0:T(4,128)} %w_ref.3) | copy-start | bytes 135172
  105.5 1.3 collective-permute-start.1
  106.8 5.7 %collective-permute-start.4 = (f32[112,128]{1,0:T(8,128)S(1)}, f32[112,128]{1,0:T(8,128)S(1)}, u32[]{:S(2)}, u32[]{:S(2)}) collective-permute-start(f32[112,128]{1,0:T(8,128)S(1)} %add.30), channel_id=1, source_target_pairs={{0,192},{32,224},{64,128},{96,160},{128,64},{160,96},{192,0},{224,... | collective-permute-start | bytes 172040 | tf_op jit(solution)/shard_map/ppermute | solution.py:462
  109.7 5.8 %collective-permute-start.3 = (f32[112,128]{1,0:T(8,128)S(1)}, f32[112,128]{1,0:T(8,128)S(1)}, u32[]{:S(2)}, u32[]{:S(2)}) collective-permute-start(f32[112,128]{1,0:T(8,128)S(1)} %add.30), channel_id=1, source_target_pairs={{0,128},{32,160},{64,192},{96,224},{128,0},{160,32},{192,64},{224,... | collective-permute-start | bytes 172040 | tf_op jit(solution)/shard_map/ppermute | solution.py:462
  110.5 5.0 %collective-permute-start.2 = (f32[112,128]{1,0:T(8,128)S(1)}, f32[112,128]{1,0:T(8,128)S(1)}, u32[]{:S(2)}, u32[]{:S(2)}) collective-permute-start(f32[112,128]{1,0:T(8,128)S(1)} %add.30), channel_id=1, source_target_pairs={{0,64},{32,96},{64,0},{96,32},{128,192},{160,224},{192,128},{224,1... | collective-permute-start | bytes 172040 | tf_op jit(solution)/shard_map/ppermute | solution.py:462
  115.5 6.5 %collective-permute-start.7 = (f32[112,128]{1,0:T(8,128)S(1)}, f32[112,128]{1,0:T(8,128)S(1)}, u32[]{:S(2)}, u32[]{:S(2)}) collective-permute-start(f32[112,128]{1,0:T(8,128)S(1)} %add_add_fusion.2), channel_id=1, source_target_pairs={{0,24},{1,25},{2,26},{3,27},{4,28},{5,29},{6,30},{7,31},{8,16},{9,... | collective-permute-start | bytes 172040 | tf_op jit(solution)/shard_map/ppermute | solution.py:462
  116.7 5.7 %collective-permute-start.6 = (f32[112,128]{1,0:T(8,128)S(1)}, f32[112,128]{1,0:T(8,128)S(1)}, u32[]{:S(2)}, u32[]{:S(2)}) collective-permute-start(f32[112,128]{1,0:T(8,128)S(1)} %add_add_fusion.2), channel_id=1, source_target_pairs={{0,16},{1,17},{2,18},{3,19},{4,20},{5,21},{6,22},{7,23},{8,24},{9,... | collective-permute-start | bytes 172040 | tf_op jit(solution)/shard_map/ppermute | solution.py:462
  118.3 4.2 %collective-permute-start.5 = (f32[112,128]{1,0:T(8,128)S(1)}, f32[112,128]{1,0:T(8,128)S(1)}, u32[]{:S(2)}, u32[]{:S(2)}) collective-permute-start(f32[112,128]{1,0:T(8,128)S(1)} %add_add_fusion.2), channel_id=1, source_target_pairs={{0,8},{1,9},{2,10},{3,11},{4,12},{5,13},{6,14},{7,15},{8,0},{9,1},... | collective-permute-start | bytes 172040 | tf_op jit(solution)/shard_map/ppermute | solution.py:462
  119.7 7.6 %collective-permute-start.8 = (f32[3,2816]{1,0:T(4,128)S(1)}, f32[3,2816]{1,0:T(4,128)S(1)}, u32[]{:S(2)}, u32[]{:S(2)}) collective-permute-start(f32[3,2816]{1,0:T(4,128)S(1)} %get-tuple-element.71), channel_id=1, source_target_pairs={{1,0},{2,1},{3,2},{4,3},{5,4},{6,5},{7,6},{8,7},{9,8},{10,9},{11,1... | collective-permute-start | bytes 101384 | tf_op jit(solution)/shard_map/ppermute | solution.py:458
  127.3 4.2 %collective-permute-start.11 = (f32[112,128]{1,0:T(8,128)S(1)}, f32[112,128]{1,0:T(8,128)S(1)}, u32[]{:S(2)}, u32[]{:S(2)}) collective-permute-start(f32[112,128]{1,0:T(8,128)S(1)} %add_add_fusion.1), channel_id=1, source_target_pairs={{0,3},{1,2},{2,1},{3,0},{4,7},{5,6},{6,5},{7,4},{8,11},{9,10},{10,... | collective-permute-start | bytes 172040 | tf_op jit(solution)/shard_map/ppermute | solution.py:462
  127.3 5.1 %collective-permute-start.10 = (f32[112,128]{1,0:T(8,128)S(1)}, f32[112,128]{1,0:T(8,128)S(1)}, u32[]{:S(2)}, u32[]{:S(2)}) collective-permute-start(f32[112,128]{1,0:T(8,128)S(1)} %add_add_fusion.1), channel_id=1, source_target_pairs={{0,2},{1,3},{2,0},{3,1},{4,6},{5,7},{6,4},{7,5},{8,10},{9,11},{10,... | collective-permute-start | bytes 172040 | tf_op jit(solution)/shard_map/ppermute | solution.py:462
  128.4 5.5 %collective-permute-start.9 = (f32[112,128]{1,0:T(8,128)S(1)}, f32[112,128]{1,0:T(8,128)S(1)}, u32[]{:S(2)}, u32[]{:S(2)}) collective-permute-start(f32[112,128]{1,0:T(8,128)S(1)} %add_add_fusion.1), channel_id=1, source_target_pairs={{0,1},{1,0},{2,3},{3,2},{4,5},{5,4},{6,7},{7,6},{8,9},{9,8},{10,11... | collective-permute-start | bytes 172040 | tf_op jit(solution)/shard_map/ppermute | solution.py:462
  133.9 8.2 %collective-permute-start.12 = (f32[112,128]{1,0:T(8,128)S(1)}, f32[112,128]{1,0:T(8,128)S(1)}, u32[]{:S(2)}, u32[]{:S(2)}) collective-permute-start(f32[112,128]{1,0:T(8,128)S(1)} %add_add_fusion.near_ref), channel_id=1, source_target_pairs={{0,4},{1,5},{2,6},{3,7},{4,0},{5,1},{6,2},{7,3},{8,12},{9,13},{10,... | collective-permute-start | bytes 172040 | tf_op jit(solution)/shard_map/ppermute | solution.py:462

commit v7 on v6

--- a/solution.py
+++ b/solution.py
@@ -574,8 +574,7 @@
         large=5, limit=SMALL_LIMIT,
     )
     sums = params + flipped(params, "dp", 1)
-    sums, edge, q_rows = lax.optimization_barrier((sums, edge, q_rows))
-    next_rows = shifted(edge, "seq", -1)
+    sums, q_rows = lax.optimization_barrier((sums, q_rows))
     (gsteps,) = call(
         log_kernel, [wide_heads], [], q_rows, r_rows, four, col_sums, row_sums, decay_rates,
         scalars=1, limit=SMALL_LIMIT,
@@ -583,9 +582,10 @@
     sums = four_summed(sums, "dp", 2)
     sums, gsteps = lax.optimization_barrier((sums, gsteps))
     sums = four_summed(sums, "seq", 8)
-    sums, next_rows = lax.optimization_barrier((sums, next_rows))
+    sums, edge = lax.optimization_barrier((sums, edge))
+    next_rows = shifted(edge, "seq", -1)
     sums = four_summed(sums, "seq", 1)
-    sums, gpre = lax.optimization_barrier((sums, gpre))
+    sums, gpre, next_rows = lax.optimization_barrier((sums, gpre, next_rows))
     far_sums = flipped(sums, "seq", 4)
     (grad_in,) = call(
         spread_kernel, [((GROUP, channels), BF16)], [], gpre, next_rows, conv_weight,

time: 144 us -> 143 us (level)
  waiting for transfers between devices: 34.2 us -> 30.9 us
    ppermute x2, waiting for transfers between devices: 4.85 us -> 2.45 us  [shifted(): return lax.ppermute(array, axis, pairs)]
  transfers between devices with their start and end apart: 14 -> 14, of which waited for: 10 -> 9; matrix products, arithmetic and copies ran while one was open for 0% -> 0% of each run, Pallas kernels for 16% -> 16%
where the time goes in v7:
time: 143 us; the launch traced here: 141 us
  blocking collectives  38.6 us (27%)
  Pallas kernels  36.5 us (26%)
  starting transfers between devices  32.8 us (23%)
  waiting for transfers between devices  30.9 us (22%)
    all_to_all x1, blocking collectives, shards(): back = lax.all_to_all(turned, 'seq', 0, 0, tiled=True)  38.6 us
    pallas_call x8, Pallas kernels, call(): pl.pallas_call(kernel, out_shape=[out_space(*out) if large_out or i in ke...  36.5 us
    all_to_all x1, waiting for transfers between devices, shards(): got = lax.all_to_all(msg, 'seq', 0, 0, tiled=True)  17 us
    ppermute x11, starting transfers between devices, flipped(): lax.ppermute(array, axis, [(i, i ^ bits) for i in range(lax.axis_size(axi...  13.3 us
    all_to_all x1, starting transfers between devices, shards(): got = lax.all_to_all(msg, 'seq', 0, 0, tiled=True)  12.5 us
    ppermute x11, waiting for transfers between devices, flipped(): lax.ppermute(array, axis, [(i, i ^ bits) for i in range(lax.axis_size(axi...  11.4 us
    ppermute x2, starting transfers between devices, shifted(): return lax.ppermute(array, axis, pairs)  7.03 us
  transfers between devices with their start and end apart: 14, of which 9 were waited for; matrix products, arithmetic and copies ran while one was open for 0% of the time, Pallas kernels for 16%

profile of v7, /device:TPU:32, one launch (start us, length us, event | category | flops | bytes accessed | tf_op | source)
XLA Modules:
  0.0 140.7 jit_solution(3752050598097897632)
XLA Ops:
  0.6 0.8 slice_bitcast_fusion
  1.4 3.8 %collective-permute-start = (bf16[3,2816]{1,0:T(4,128)(2,1)S(1)}, bf16[3,2816]{1,0:T(4,128)(2,1)S(1)}, u32[]{:S(2)}, u32[]{:S(2)}) collective-permute-start(bf16[3,2816]{1,0:T(4,128)(2,1)S(1)} %slice_bitcast_fusion), channel_id=1, source_target_pairs={{0,1},{1,2},{2,3},{3,4},{4,5},{5,6},{6,7},{7,8},{8,9},{9,10},{10,1... | collective-permute-start | bytes 50696 | tf_op jit(solution)/shard_map/ppermute | solution.py:458
  5.3 1.9 %shard_map.118 = (bf16[2560,256]{1,0:T(8,128)(2,1)S(1)}, f32[40,256]{1,0:T(8,128)S(1)}, f32[40,256]{1,0:T(8,128)S(1)}) custom-call(f32[40,256]{1,0:T(8,128)} %bitcast.7, f32[40]{0:T(128)} %rate_ref.3, bf16[256,2560]{1,0:T(8,128)(2,1)} %bitcast.13), custom_call_target="tpu_custom_call" | custom-call | tf_op jit(solution)/shard_map/pallas_call | solution.py:442
  7.2 4.9 %shard_map.119 = bf16[32,168,128]{2,1,0:T(8,128)(2,1)} custom-call(bf16[3,2816]{1,0:T(4,128)(2,1)S(1)} %collective-permute-done.halo_ref, bf16[2560,256]{1,0:T(8,128)(2,1)S(1)} %get-tuple-element.44.dywt_ref, f32[40,256]{1,0:T(8,128)S(1)} %get-tuple-element.45.tail_ref, f32[40,256]{1,0:T(8,128)S(1)} %get-tuple-element.46.head_ref, ...), custom_call_target="tpu_custom_call" | custom-call | tf_op jit(solution)/shard_map/pallas_call | solution.py:442
  12.1 12.5 %all-to-all-start = ((bf16[32,168,128]{2,1,0:T(8,128)(2,1)}), bf16[32,168,128]{2,1,0:T(8,128)(2,1)S(1)}, u32[]{:S(2)}, u32[]{:S(2)}) async-start(bf16[32,168,128]{2,1,0:T(8,128)(2,1)} %shard_map.119), calls=%async_computation | async-start | bytes 2752512 | tf_op jit(solution)/shard_map/all_to_all | solution.py:507
  24.6 16.9 %shard_map.120 = (f32[256,2560]{1,0:T(8,128)}, bf16[256,2560]{1,0:T(8,128)(2,1)}, bf16[2560,256]{1,0:T(8,128)(2,1)}, bf16[2560,256]{1,0:T(8,128)(2,1)}, bf16[256...) custom-call(bf16[256,2816]{1,0:T(8,128)(2,1)} %bitcast.11, ...), custom_call_target="tpu_custom_call" | custom-call | tf_op jit(solution)/shard_map/pallas_call | solution.py:442
  41.6 17.0 %all-to-all-done.got_ref = bf16[32,168,128]{2,1,0:T(8,128)(2,1)S(1)} async-done(((bf16[32,168,128]{2,1,0:T(8,128)(2,1)}), bf16[32,168,128]{2,1,0:T(8,128)(2,1)S(1)}, u32[]{:S(2)}, u32[]{:S(2)}) %all-to-all-start) | async-done | bytes 1376288 | tf_op jit(solution)/shard_map/all_to_all | solution.py:507
  58.6 1.4 shard_map.121
  60.1 38.6 %all_to_all.10.back_ref = bf16[32,160,128]{2,1,0:T(8,128)(2,1)S(1)} all-to-all(bf16[32,160,128]{2,1,0:T(8,128)(2,1)} %shard_map.121), channel_id=1, replica_groups=mesh['dp'=8,'seq'=32] {'seq'}, dimensions={0} | all-to-all | bytes 2621440 | tf_op jit(solution)/shard_map/all_to_all | solution.py:545
  98.8 6.7 %shard_map.122 = (f32[256,2816]{1,0:T(8,128)S(1)}, f32[3,2816]{1,0:T(4,128)S(1)}, f32[40,256]{1,0:T(8,128)S(1)}, f32[40,256]{1,0:T(8,128)S(1)}, f32[40,128]{1,0:T(8,128)S(1)}, /*index=5*/f32[112,128]{1,0:T(8,128)S(1)}) custom-call(bf16[32,160,128]{2,1,0:T(8,128)(2,1)S(1)} %all_to_all.10.back_ref, bf16[256,256]{1,0:T(8,128)(2,1)S(1)} %copy-done.7, ...), custom_call_target="tpu_custom_call" | custom-call | tf_op jit(solution)/shard_map/pallas_call | solution.py:442
  105.5 0.1 collective-permute-start.1
  105.6 1.2 collective-permute-done.1
  106.8 2.8 %collective-permute-start.4 = (f32[112,128]{1,0:T(8,128)S(1)}, f32[112,128]{1,0:T(8,128)S(1)}, u32[]{:S(2)}, u32[]{:S(2)}) collective-permute-start(f32[112,128]{1,0:T(8,128)S(1)} %add.30), channel_id=1, source_target_pairs={{0,192},{32,224},{64,128},{96,160},{128,64},{160,96},{192,0},{224,... | collective-permute-start | bytes 172040 | tf_op jit(solution)/shard_map/ppermute | solution.py:462
  109.7 0.8 collective-permute-start.3
  110.5 0.5 collective-permute-start.2
  111.0 1.5 %shard_map.123 = f32[40,256]{1,0:T(8,128)} custom-call(f32[40,256]{1,0:T(8,128)S(1)} %get-tuple-element.66.q_ref, f32[40,256]{1,0:T(8,128)S(1)} %get-tuple-element.67.r_ref, f32[40,128]{1,0:T(8,128)S(1)} %get-tuple-element.68.four_ref, f32[40,256]{1,0:T(8,128)S(1)} %copy-done.5, f32[40,256]{1,0:T(8,128)S(1)} %copy-done.6, f32[40]{0:T(128)S(1)} %copy-done.14), custom_call_target="tpu_custom_call" | custom-call | tf_op jit(solution)/shard_map/pallas_call | solution.py:442
  112.6 2.9 %collective-permute-done.3 = f32[112,128]{1,0:T(8,128)S(1)} collective-permute-done((f32[112,128]{1,0:T(8,128)S(1)}, f32[112,128]{1,0:T(8,128)S(1)}, u32[]{:S(2)}, u32[]{:S(2)}) %collective-permute-start.3) | collective-permute-done | bytes 57376 | tf_op jit(solution)/shard_map/ppermute | solution.py:462
  115.5 1.2 collective-permute-start.7
  116.7 1.6 %collective-permute-start.6 = (f32[112,128]{1,0:T(8,128)S(1)}, f32[112,128]{1,0:T(8,128)S(1)}, u32[]{:S(2)}, u32[]{:S(2)}) collective-permute-start(f32[112,128]{1,0:T(8,128)S(1)} %add_add_fusion.2), channel_id=1, source_target_pairs={{0,16},{1,17},{2,18},{3,19},{4,20},{5,21},{6,22},{7,23},{8,24},{9,... | collective-permute-start | bytes 172040 | tf_op jit(solution)/shard_map/ppermute | solution.py:462
  118.3 1.4 %collective-permute-start.5 = (f32[112,128]{1,0:T(8,128)S(1)}, f32[112,128]{1,0:T(8,128)S(1)}, u32[]{:S(2)}, u32[]{:S(2)}) collective-permute-start(f32[112,128]{1,0:T(8,128)S(1)} %add_add_fusion.2), channel_id=1, source_target_pairs={{0,8},{1,9},{2,10},{3,11},{4,12},{5,13},{6,14},{7,15},{8,0},{9,1},... | collective-permute-start | bytes 172040 | tf_op jit(solution)/shard_map/ppermute | solution.py:462
  119.7 1.3 collective-permute-done.7
  121.0 1.4 %collective-permute-done.6 = f32[112,128]{1,0:T(8,128)S(1)} collective-permute-done((f32[112,128]{1,0:T(8,128)S(1)}, f32[112,128]{1,0:T(8,128)S(1)}, u32[]{:S(2)}, u32[]{:S(2)}) %collective-permute-start.6) | collective-permute-done | bytes 57376 | tf_op jit(solution)/shard_map/ppermute | solution.py:462
  122.5 0.9 collective-permute-start.10
  123.3 2.0 %collective-permute-start.9 = (f32[112,128]{1,0:T(8,128)S(1)}, f32[112,128]{1,0:T(8,128)S(1)}, u32[]{:S(2)}, u32[]{:S(2)}) collective-permute-start(f32[112,128]{1,0:T(8,128)S(1)} %add_add_fusion.1), channel_id=1, source_target_pairs={{0,2},{1,3},{2,0},{3,1},{4,6},{5,7},{6,4},{7,5},{8,10},{9,11},{10,... | collective-permute-start | bytes 172040 | tf_op jit(solution)/shard_map/ppermute | solution.py:462
  125.3 0.7 collective-permute-start.8
  126.0 3.2 %collective-permute-start.11 = (f32[3,2816]{1,0:T(4,128)S(1)}, f32[3,2816]{1,0:T(4,128)S(1)}, u32[]{:S(2)}, u32[]{:S(2)}) collective-permute-start(f32[3,2816]{1,0:T(4,128)S(1)} %get-tuple-element.73), channel_id=1, source_target_pairs={{1,0},{2,1},{3,2},{4,3},{5,4},{6,5},{7,6},{8,7},{9,8},{10,9},{11,1... | collective-permute-start | bytes 101384 | tf_op jit(solution)/shard_map/ppermute | solution.py:458
  129.3 0.2 collective-permute-done.8
  129.5 2.4 %collective-permute-done.11.next_ref = f32[3,2816]{1,0:T(4,128)S(1)} collective-permute-done((f32[3,2816]{1,0:T(4,128)S(1)}, f32[3,2816]{1,0:T(4,128)S(1)}, u32[]{:S(2)}, u32[]{:S(2)}) %collective-permute-start.11) | collective-permute-done | bytes 33824 | tf_op jit(solution)/shard_map/ppermute | solution.py:458
  132.0 1.3 collective-permute-start.12
  133.2 2.5 %shard_map.124 = bf16[256,2816]{1,0:T(8,128)(2,1)} custom-call(f32[256,2816]{1,0:T(8,128)S(1)} %get-tuple-element.74.gpre_ref, f32[3,2816]{1,0:T(4,128)S(1)} %collective-permute-done.11.next_ref, f32[4,2816]{1,0:T(4,128)S(1)} %copy-done), custom_call_target="tpu_custom_call" | custom-call | tf_op jit(solution)/shard_map/pallas_call | solution.py:442
  135.8 4.3 %collective-permute-done.12.far_ref = f32[112,128]{1,0:T(8,128)S(1)} collective-permute-done((f32[112,128]{1,0:T(8,128)S(1)}, f32[112,128]{1,0:T(8,128)S(1)}, u32[]{:S(2)}, u32[]{:S(2)}) %collective-permute-start.12) | collective-permute-done | bytes 57376 | tf_op jit(solution)/shard_map/ppermute | solution.py:462
  140.1 0.7 shard_map.125
  (40 shorter events, 0.2 us)
Async XLA Ops:
  1.4 5.8 %collective-permute-start = (bf16[3,2816]{1,0:T(4,128)(2,1)S(1)}, bf16[3,2816]{1,0:T(4,128)(2,1)S(1)}, u32[]{:S(2)}, u32[]{:S(2)}) collective-permute-start(bf16[3,2816]{1,0:T(4,128)(2,1)S(1)} %slice_bitcast_fusion), channel_id=1, source_target_pairs={{0,1},{1,2},{2,3},{3,4},{4,5},{5,6},{6,7},{7,8},{8,9},{9,10},{10,1... | collective-permute-start | bytes 50696 | tf_op jit(solution)/shard_map/ppermute | solution.py:458
  7.2 4.9 %copy-start.3 = (bf16[3,2816]{1,0:T(4,128)(2,1)}, bf16[3,2816]{1,0:T(4,128)(2,1)S(1)}, u32[]{:S(2)}) copy-start(bf16[3,2816]{1,0:T(4,128)(2,1)S(1)} %collective-permute-done.halo_ref) | copy-start | bytes 50692
  12.1 46.5 %all-to-all-start = ((bf16[32,168,128]{2,1,0:T(8,128)(2,1)}), bf16[32,168,128]{2,1,0:T(8,128)(2,1)S(1)}, u32[]{:S(2)}, u32[]{:S(2)}) async-start(bf16[32,168,128]{2,1,0:T(8,128)(2,1)} %shard_map.119), calls=%async_computation | async-start | bytes 2752512 | tf_op jit(solution)/shard_map/all_to_all | solution.py:507
  60.0 38.7 %copy-start.1 = (f32[1,40,256]{2,1,0:T(8,128)S(1)}, f32[1,40,256]{2,1,0:T(8,128)}, u32[]{:S(2)}) copy-start(f32[1,40,256]{2,1,0:T(8,128)} %param.10) | copy-start | bytes 122884
  60.0 38.7 %copy-start.2 = (f32[256,256]{1,0:T(8,128)S(1)}, f32[256,256]{1,0:T(8,128)}, u32[]{:S(2)}) copy-start(f32[256,256]{1,0:T(8,128)} %get-tuple-element.51.slope_ref) | copy-start | bytes 786436
  60.0 38.7 %copy-start.4 = (bf16[3,2816]{1,0:T(4,128)(2,1)S(1)}, bf16[3,2816]{1,0:T(4,128)(2,1)}, u32[]{:S(2)}) copy-start(bf16[3,2816]{1,0:T(4,128)(2,1)} %copy-done.3) | copy-start | bytes 50692
  60.0 38.7 %copy-start.5 = (f32[40,256]{1,0:T(8,128)S(1)}, f32[40,256]{1,0:T(8,128)}, u32[]{:S(2)}) copy-start(f32[40,256]{1,0:T(8,128)} %get-tuple-element.54.colin_ref.col_ref) | copy-start | bytes 122884
  60.0 38.7 %copy-start.6 = (f32[40,256]{1,0:T(8,128)S(1)}, f32[40,256]{1,0:T(8,128)}, u32[]{:S(2)}) copy-start(f32[40,256]{1,0:T(8,128)} %get-tuple-element.55.row_ref) | copy-start | bytes 122884
  60.0 38.7 %copy-start.7 = (bf16[256,256]{1,0:T(8,128)(2,1)S(1)}, bf16[256,256]{1,0:T(8,128)(2,1)}, u32[]{:S(2)}) copy-start(bf16[256,256]{1,0:T(8,128)(2,1)} %get-tuple-element.49.bc_ref) | copy-start | bytes 393220
  60.0 38.7 %copy-start.8 = (bf16[256,256]{1,0:T(8,128)(2,1)S(1)}, bf16[256,256]{1,0:T(8,128)(2,1)}, u32[]{:S(2)}) copy-start(bf16[256,256]{1,0:T(8,128)(2,1)} %get-tuple-element.50.bct_ref) | copy-start | bytes 393220
  60.0 38.7 %copy-start.9 = (f32[128,256]{1,0:T(8,128)S(1)}, f32[128,256]{1,0:T(8,128)}, u32[]{:S(2)}) copy-start(f32[128,256]{1,0:T(8,128)} %get-tuple-element.52.gbin_ref) | copy-start | bytes 393220
  60.1 38.7 %copy-start.10 = (f32[128,256]{1,0:T(8,128)S(1)}, f32[128,256]{1,0:T(8,128)}, u32[]{:S(2)}) copy-start(f32[128,256]{1,0:T(8,128)} %get-tuple-element.53.gcin_ref) | copy-start | bytes 393220
  60.1 38.7 %copy-start.11 = (f32[40,256]{1,0:T(8,128)S(1)}, f32[40,256]{1,0:T(8,128)}, u32[]{:S(2)}) copy-start(f32[40,256]{1,0:T(8,128)} %get-tuple-element.56.skiprow_ref) | copy-start | bytes 122884
  60.1 38.7 %copy-start.12 = (f32[40,256]{1,0:T(8,128)S(1)}, f32[40,256]{1,0:T(8,128)}, u32[]{:S(2)}) copy-start(f32[40,256]{1,0:T(8,128)} %get-tuple-element.57.sofar_ref) | copy-start | bytes 122884
  60.1 38.7 %copy-start.13 = (f32[40,128]{1,0:T(8,128)S(1)}, f32[40,128]{1,0:T(8,128)}, u32[]{:S(2)}) copy-start(f32[40,128]{1,0:T(8,128)} %get-tuple-element.58.end_ref) | copy-start | bytes 61444
  98.8 12.2 %copy-start.14 = (f32[40]{0:T(128)S(1)}, f32[40]{0:T(128)}, u32[]{:S(2)}) copy-start(f32[40]{0:T(128)} %rate_ref.3) | copy-start | bytes 484
  98.8 34.4 %copy-start = (f32[4,2816]{1,0:T(4,128)S(1)}, f32[4,2816]{1,0:T(4,128)}, u32[]{:S(2)}) copy-start(f32[4,2816]{1,0:T(4,128)} %w_ref.3) | copy-start | bytes 135172
  105.5 1.3 collective-permute-start.1
  106.8 5.7 %collective-permute-start.4 = (f32[112,128]{1,0:T(8,128)S(1)}, f32[112,128]{1,0:T(8,128)S(1)}, u32[]{:S(2)}, u32[]{:S(2)}) collective-permute-start(f32[112,128]{1,0:T(8,128)S(1)} %add.30), channel_id=1, source_target_pairs={{0,192},{32,224},{64,128},{96,160},{128,64},{160,96},{192,0},{224,... | collective-permute-start | bytes 172040 | tf_op jit(solution)/shard_map/ppermute | solution.py:462
  109.7 5.8 %collective-permute-start.3 = (f32[112,128]{1,0:T(8,128)S(1)}, f32[112,128]{1,0:T(8,128)S(1)}, u32[]{:S(2)}, u32[]{:S(2)}) collective-permute-start(f32[112,128]{1,0:T(8,128)S(1)} %add.30), channel_id=1, source_target_pairs={{0,128},{32,160},{64,192},{96,224},{128,0},{160,32},{192,64},{224,... | collective-permute-start | bytes 172040 | tf_op jit(solution)/shard_map/ppermute | solution.py:462
  110.5 5.0 %collective-permute-start.2 = (f32[112,128]{1,0:T(8,128)S(1)}, f32[112,128]{1,0:T(8,128)S(1)}, u32[]{:S(2)}, u32[]{:S(2)}) collective-permute-start(f32[112,128]{1,0:T(8,128)S(1)} %add.30), channel_id=1, source_target_pairs={{0,64},{32,96},{64,0},{96,32},{128,192},{160,224},{192,128},{224,1... | collective-permute-start | bytes 172040 | tf_op jit(solution)/shard_map/ppermute | solution.py:462
  115.5 5.5 %collective-permute-start.7 = (f32[112,128]{1,0:T(8,128)S(1)}, f32[112,128]{1,0:T(8,128)S(1)}, u32[]{:S(2)}, u32[]{:S(2)}) collective-permute-start(f32[112,128]{1,0:T(8,128)S(1)} %add_add_fusion.2), channel_id=1, source_target_pairs={{0,24},{1,25},{2,26},{3,27},{4,28},{5,29},{6,30},{7,31},{8,16},{9,... | collective-permute-start | bytes 172040 | tf_op jit(solution)/shard_map/ppermute | solution.py:462
  116.7 5.7 %collective-permute-start.6 = (f32[112,128]{1,0:T(8,128)S(1)}, f32[112,128]{1,0:T(8,128)S(1)}, u32[]{:S(2)}, u32[]{:S(2)}) collective-permute-start(f32[112,128]{1,0:T(8,128)S(1)} %add_add_fusion.2), channel_id=1, source_target_pairs={{0,16},{1,17},{2,18},{3,19},{4,20},{5,21},{6,22},{7,23},{8,24},{9,... | collective-permute-start | bytes 172040 | tf_op jit(solution)/shard_map/ppermute | solution.py:462
  118.3 4.2 %collective-permute-start.5 = (f32[112,128]{1,0:T(8,128)S(1)}, f32[112,128]{1,0:T(8,128)S(1)}, u32[]{:S(2)}, u32[]{:S(2)}) collective-permute-start(f32[112,128]{1,0:T(8,128)S(1)} %add_add_fusion.2), channel_id=1, source_target_pairs={{0,8},{1,9},{2,10},{3,11},{4,12},{5,13},{6,14},{7,15},{8,0},{9,1},... | collective-permute-start | bytes 172040 | tf_op jit(solution)/shard_map/ppermute | solution.py:462
  122.5 6.8 %collective-permute-start.10 = (f32[112,128]{1,0:T(8,128)S(1)}, f32[112,128]{1,0:T(8,128)S(1)}, u32[]{:S(2)}, u32[]{:S(2)}) collective-permute-start(f32[112,128]{1,0:T(8,128)S(1)} %add_add_fusion.1), channel_id=1, source_target_pairs={{0,3},{1,2},{2,1},{3,0},{4,7},{5,6},{6,5},{7,4},{8,11},{9,10},{10,... | collective-permute-start | bytes 172040 | tf_op jit(solution)/shard_map/ppermute | solution.py:462
  123.3 5.9 %collective-permute-start.9 = (f32[112,128]{1,0:T(8,128)S(1)}, f32[112,128]{1,0:T(8,128)S(1)}, u32[]{:S(2)}, u32[]{:S(2)}) collective-permute-start(f32[112,128]{1,0:T(8,128)S(1)} %add_add_fusion.1), channel_id=1, source_target_pairs={{0,2},{1,3},{2,0},{3,1},{4,6},{5,7},{6,4},{7,5},{8,10},{9,11},{10,... | collective-permute-start | bytes 172040 | tf_op jit(solution)/shard_map/ppermute | solution.py:462
  125.3 4.2 %collective-permute-start.8 = (f32[112,128]{1,0:T(8,128)S(1)}, f32[112,128]{1,0:T(8,128)S(1)}, u32[]{:S(2)}, u32[]{:S(2)}) collective-permute-start(f32[112,128]{1,0:T(8,128)S(1)} %add_add_fusion.1), channel_id=1, source_target_pairs={{0,1},{1,0},{2,3},{3,2},{4,5},{5,4},{6,7},{7,6},{8,9},{9,8},{10,11... | collective-permute-start | bytes 172040 | tf_op jit(solution)/shard_map/ppermute | solution.py:462
  126.0 5.9 %collective-permute-start.11 = (f32[3,2816]{1,0:T(4,128)S(1)}, f32[3,2816]{1,0:T(4,128)S(1)}, u32[]{:S(2)}, u32[]{:S(2)}) collective-permute-start(f32[3,2816]{1,0:T(4,128)S(1)} %get-tuple-element.73), channel_id=1, source_target_pairs={{1,0},{2,1},{3,2},{4,3},{5,4},{6,5},{7,6},{8,7},{9,8},{10,9},{11,1... | collective-permute-start | bytes 101384 | tf_op jit(solution)/shard_map/ppermute | solution.py:458
  132.0 8.1 %collective-permute-start.12 = (f32[112,128]{1,0:T(8,128)S(1)}, f32[112,128]{1,0:T(8,128)S(1)}, u32[]{:S(2)}, u32[]{:S(2)}) collective-permute-start(f32[112,128]{1,0:T(8,128)S(1)} %add_add_fusion.near_ref), channel_id=1, source_target_pairs={{0,4},{1,5},{2,6},{3,7},{4,0},{5,1},{6,2},{7,3},{8,12},{9,13},{10,... | collective-permute-start | bytes 172040 | tf_op jit(solution)/shard_map/ppermute | solution.py:462

commit v8 on v7

--- a/solution.py
+++ b/solution.py
@@ -390,17 +390,17 @@
     params_ref[at : at + 2, :] = flip_ref[...].T[:2]
 
 
-def spread_kernel(gpre_ref, next_ref, w_ref, gin_ref):
+def spread_kernel(gpre_ref, w_ref, gin_ref, last_ref):
     rim = KCONV - 1
 
     def tile(c, carry):
         grad = gpre_ref[:, lanes(c)]
-        below = jnp.concatenate([next_ref[:, lanes(c)], jnp.zeros((8 - rim, LANE), F32)], axis=0)
-        full = jnp.concatenate([grad, below], axis=0)
+        full = jnp.concatenate([grad, jnp.zeros((8, LANE), F32)], axis=0)
         spread = w_ref[rim : rim + 1, lanes(c)] * grad
         for k in range(rim):
             spread = spread + w_ref[k : k + 1, lanes(c)] * full[rim - k : rim - k + GROUP]
         gin_ref[:, lanes(c)] = spread.astype(BF16)
+        last_ref[:, lanes(c)] = spread[GROUP - 16 :]
         return carry
 
     lax.fori_loop(0, PAIRS + 2, tile, 0, unroll=2)
@@ -580,17 +580,23 @@
         scalars=1, limit=SMALL_LIMIT,
     )
     sums = four_summed(sums, "dp", 2)
-    sums, gsteps = lax.optimization_barrier((sums, gsteps))
+    sums, gsteps, gpre = lax.optimization_barrier((sums, gsteps, gpre))
+    grad_in, last = call(
+        spread_kernel, [((GROUP, channels), BF16), ((16, channels), F32)], [], gpre, conv_weight,
+        limit=SMALL_LIMIT,
+    )
     sums = four_summed(sums, "seq", 8)
-    sums, edge = lax.optimization_barrier((sums, edge))
+    sums, edge, grad_in = lax.optimization_barrier((sums, edge, grad_in))
     next_rows = shifted(edge, "seq", -1)
     sums = four_summed(sums, "seq", 1)
-    sums, gpre, next_rows = lax.optimization_barrier((sums, gpre, next_rows))
+    sums, last = lax.optimization_barrier((sums, last))
     far_sums = flipped(sums, "seq", 4)
-    (grad_in,) = call(
-        spread_kernel, [((GROUP, channels), BF16)], [], gpre, next_rows, conv_weight,
-        limit=SMALL_LIMIT,
-    )
+    ahead = jnp.concatenate([jnp.zeros_like(next_rows), next_rows], axis=0)
+    added = last[16 - rim :]
+    for k in range(rim):
+        added = added + conv_weight[k][None] * ahead[rim - k : 2 * rim - k]
+    ending = jnp.concatenate([last[: 16 - rim], added], axis=0).astype(BF16)
+    grad_in = lax.dynamic_update_slice(grad_in, ending, (GROUP - 16, 0))
     grad_weight, grad_bias, grad_rates, grad_skip = call(
         unpack_kernel,
         [((KCONV, channels), F32), ((channels,), F32), ((HEADS,), F32), ((HEADS,), F32)],

time: 143 us -> 142 us (level); the launches traced: 141 us -> 142 us
  starting transfers between devices: 32.8 us -> 35.1 us
  waiting for transfers between devices: 30.9 us -> 29.1 us
    ppermute x2, waiting for transfers between devices: 2.45 us -> 0.14 us  [shifted(): return lax.ppermute(array, axis, pairs)]
    ppermute x11, starting transfers between devices: 13.3 us -> 15.5 us  [flipped(): lax.ppermute(array, axis, [(i, i ^ bits) for i in range(lax.axis_size(axi...]
  transfers between devices with their start and end apart: 14 -> 14, of which waited for: 9 -> 8; matrix products, arithmetic and copies ran while one was open for 0% -> 1% of each run, Pallas kernels for 16% -> 16%
where the time goes in v8:
time: 142 us
  blocking collectives  38.6 us (27%)
  Pallas kernels  36.4 us (26%)
  starting transfers between devices  35.1 us (25%)
  waiting for transfers between devices  29.1 us (20%)
    all_to_all x1, blocking collectives, shards(): back = lax.all_to_all(turned, 'seq', 0, 0, tiled=True)  38.6 us
    pallas_call x8, Pallas kernels, call(): pl.pallas_call(kernel, out_shape=[out_space(*out) if large_out or i in ke...  36.4 us
    all_to_all x1, waiting for transfers between devices, shards(): got = lax.all_to_all(msg, 'seq', 0, 0, tiled=True)  17.1 us
    ppermute x11, starting transfers between devices, flipped(): lax.ppermute(array, axis, [(i, i ^ bits) for i in range(lax.axis_size(axi...  15.5 us
    all_to_all x1, starting transfers between devices, shards(): got = lax.all_to_all(msg, 'seq', 0, 0, tiled=True)  12.5 us
    ppermute x11, waiting for transfers between devices, flipped(): lax.ppermute(array, axis, [(i, i ^ bits) for i in range(lax.axis_size(axi...  11.9 us
    ppermute x2, starting transfers between devices, shifted(): return lax.ppermute(array, axis, pairs)  7.09 us
  transfers between devices with their start and end apart: 14, of which 8 were waited for; matrix products, arithmetic and copies ran while one was open for 1% of the time, Pallas kernels for 16%

profile of v8, /device:TPU:32, one launch (start us, length us, event | category | flops | bytes accessed | tf_op | source)
XLA Modules:
  0.0 142.0 jit_solution(12787863781074908516)
XLA Ops:
  0.6 0.8 slice_bitcast_fusion
  1.4 3.8 %collective-permute-start = (bf16[3,2816]{1,0:T(4,128)(2,1)S(1)}, bf16[3,2816]{1,0:T(4,128)(2,1)S(1)}, u32[]{:S(2)}, u32[]{:S(2)}) collective-permute-start(bf16[3,2816]{1,0:T(4,128)(2,1)S(1)} %slice_bitcast_fusion), channel_id=1, source_target_pairs={{0,1},{1,2},{2,3},{3,4},{4,5},{5,6},{6,7},{7,8},{8,9},{9,10},{10,1... | collective-permute-start | bytes 50696 | tf_op jit(solution)/shard_map/ppermute | solution.py:458
  5.3 1.9 %shard_map.118 = (bf16[2560,256]{1,0:T(8,128)(2,1)S(1)}, f32[40,256]{1,0:T(8,128)S(1)}, f32[40,256]{1,0:T(8,128)S(1)}) custom-call(f32[40,256]{1,0:T(8,128)} %bitcast.11, f32[40]{0:T(128)} %rate_ref.3, bf16[256,2560]{1,0:T(8,128)(2,1)} %bitcast.17), custom_call_target="tpu_custom_call" | custom-call | tf_op jit(solution)/shard_map/pallas_call | solution.py:442
  7.2 4.9 %shard_map.119 = bf16[32,168,128]{2,1,0:T(8,128)(2,1)} custom-call(bf16[3,2816]{1,0:T(4,128)(2,1)S(1)} %collective-permute-done.halo_ref, bf16[2560,256]{1,0:T(8,128)(2,1)S(1)} %get-tuple-element.47.dywt_ref, f32[40,256]{1,0:T(8,128)S(1)} %get-tuple-element.48.tail_ref, f32[40,256]{1,0:T(8,128)S(1)} %get-tuple-element.49.head_ref, ...), custom_call_target="tpu_custom_call" | custom-call | tf_op jit(solution)/shard_map/pallas_call | solution.py:442
  12.1 12.5 %all-to-all-start = ((bf16[32,168,128]{2,1,0:T(8,128)(2,1)}), bf16[32,168,128]{2,1,0:T(8,128)(2,1)S(1)}, u32[]{:S(2)}, u32[]{:S(2)}) async-start(bf16[32,168,128]{2,1,0:T(8,128)(2,1)} %shard_map.119), calls=%async_computation | async-start | bytes 2752512 | tf_op jit(solution)/shard_map/all_to_all | solution.py:507
  24.6 16.9 %shard_map.120 = (f32[256,2560]{1,0:T(8,128)}, bf16[256,2560]{1,0:T(8,128)(2,1)}, bf16[2560,256]{1,0:T(8,128)(2,1)}, bf16[2560,256]{1,0:T(8,128)(2,1)}, bf16[256...) custom-call(bf16[256,2816]{1,0:T(8,128)(2,1)} %bitcast.15, ...), custom_call_target="tpu_custom_call" | custom-call | tf_op jit(solution)/shard_map/pallas_call | solution.py:442
  41.5 17.1 %all-to-all-done.got_ref = bf16[32,168,128]{2,1,0:T(8,128)(2,1)S(1)} async-done(((bf16[32,168,128]{2,1,0:T(8,128)(2,1)}), bf16[32,168,128]{2,1,0:T(8,128)(2,1)S(1)}, u32[]{:S(2)}, u32[]{:S(2)}) %all-to-all-start) | async-done | bytes 1376288 | tf_op jit(solution)/shard_map/all_to_all | solution.py:507
  58.6 1.4 shard_map.121
  60.1 38.6 %all_to_all.10.back_ref = bf16[32,160,128]{2,1,0:T(8,128)(2,1)S(1)} all-to-all(bf16[32,160,128]{2,1,0:T(8,128)(2,1)} %shard_map.121), channel_id=1, replica_groups=mesh['dp'=8,'seq'=32] {'seq'}, dimensions={0} | all-to-all | bytes 2621440 | tf_op jit(solution)/shard_map/all_to_all | solution.py:545
  98.8 6.7 %shard_map.122 = (f32[256,2816]{1,0:T(8,128)S(1)}, f32[3,2816]{1,0:T(4,128)S(1)}, f32[40,256]{1,0:T(8,128)S(1)}, f32[40,256]{1,0:T(8,128)S(1)}, f32[40,128]{1,0:T(8,128)S(1)}, /*index=5*/f32[112,128]{1,0:T(8,128)S(1)}) custom-call(bf16[32,160,128]{2,1,0:T(8,128)(2,1)S(1)} %all_to_all.10.back_ref, bf16[256,256]{1,0:T(8,128)(2,1)S(1)} %copy-done.7, ...), custom_call_target="tpu_custom_call" | custom-call | tf_op jit(solution)/shard_map/pallas_call | solution.py:442
  105.6 1.2 collective-permute-done.1
  106.9 1.6 %collective-permute-start.2 = (f32[112,128]{1,0:T(8,128)S(1)}, f32[112,128]{1,0:T(8,128)S(1)}, u32[]{:S(2)}, u32[]{:S(2)}) collective-permute-start(f32[112,128]{1,0:T(8,128)S(1)} %add.41), channel_id=1, source_target_pairs={{0,64},{32,96},{64,0},{96,32},{128,192},{160,224},{192,128},{224,1... | collective-permute-start | bytes 172040 | tf_op jit(solution)/shard_map/ppermute | solution.py:462
  108.5 2.7 %collective-permute-start.3 = (f32[112,128]{1,0:T(8,128)S(1)}, f32[112,128]{1,0:T(8,128)S(1)}, u32[]{:S(2)}, u32[]{:S(2)}) collective-permute-start(f32[112,128]{1,0:T(8,128)S(1)} %add.41), channel_id=1, source_target_pairs={{0,128},{32,160},{64,192},{96,224},{128,0},{160,32},{192,64},{224,... | collective-permute-start | bytes 172040 | tf_op jit(solution)/shard_map/ppermute | solution.py:462
  111.2 0.5 collective-permute-start.4
  111.7 1.5 %shard_map.123 = f32[40,256]{1,0:T(8,128)} custom-call(f32[40,256]{1,0:T(8,128)S(1)} %get-tuple-element.69.q_ref, f32[40,256]{1,0:T(8,128)S(1)} %get-tuple-element.70.r_ref, f32[40,128]{1,0:T(8,128)S(1)} %get-tuple-element.71.four_ref, f32[40,256]{1,0:T(8,128)S(1)} %copy-done.5, f32[40,256]{1,0:T(8,128)S(1)} %copy-done.6, f32[40]{0:T(128)S(1)} %copy-done.14), custom_call_target="tpu_custom_call" | custom-call | tf_op jit(solution)/shard_map/pallas_call | solution.py:442
  113.2 1.1 collective-permute-done.3
  114.3 2.3 %collective-permute-done.4 = f32[112,128]{1,0:T(8,128)S(1)} collective-permute-done((f32[112,128]{1,0:T(8,128)S(1)}, f32[112,128]{1,0:T(8,128)S(1)}, u32[]{:S(2)}, u32[]{:S(2)}) %collective-permute-start.4) | collective-permute-done | bytes 57376 | tf_op jit(solution)/shard_map/ppermute | solution.py:462
  116.6 0.7 collective-permute-start.5
  117.3 2.0 %collective-permute-start.6 = (f32[112,128]{1,0:T(8,128)S(1)}, f32[112,128]{1,0:T(8,128)S(1)}, u32[]{:S(2)}, u32[]{:S(2)}) collective-permute-start(f32[112,128]{1,0:T(8,128)S(1)} %add_add_fusion.2), channel_id=1, source_target_pairs={{0,16},{1,17},{2,18},{3,19},{4,20},{5,21},{6,22},{7,23},{8,24},{9,... | collective-permute-start | bytes 172040 | tf_op jit(solution)/shard_map/ppermute | solution.py:462
  119.3 2.1 %collective-permute-start.7 = (f32[112,128]{1,0:T(8,128)S(1)}, f32[112,128]{1,0:T(8,128)S(1)}, u32[]{:S(2)}, u32[]{:S(2)}) collective-permute-start(f32[112,128]{1,0:T(8,128)S(1)} %add_add_fusion.2), channel_id=1, source_target_pairs={{0,24},{1,25},{2,26},{3,27},{4,28},{5,29},{6,30},{7,31},{8,16},{9,... | collective-permute-start | bytes 172040 | tf_op jit(solution)/shard_map/ppermute | solution.py:462
  121.4 2.5 %shard_map.124 = (bf16[256,2816]{1,0:T(8,128)(2,1)}, f32[16,2816]{1,0:T(8,128)S(1)}) custom-call(f32[256,2816]{1,0:T(8,128)S(1)} %get-tuple-element.75.gpre_ref, f32[4,2816]{1,0:T(4,128)S(1)} %copy-done), custom_call_target="tpu_custom_call" | custom-call | tf_op jit(solution)/shard_map/pallas_call | solution.py:442
  123.9 0.8 collective-permute-done.7
  124.7 0.9 collective-permute-start.10
  125.6 1.5 %collective-permute-start.8 = (f32[112,128]{1,0:T(8,128)S(1)}, f32[112,128]{1,0:T(8,128)S(1)}, u32[]{:S(2)}, u32[]{:S(2)}) collective-permute-start(f32[112,128]{1,0:T(8,128)S(1)} %add_add_fusion.1), channel_id=1, source_target_pairs={{0,1},{1,0},{2,3},{3,2},{4,5},{5,4},{6,7},{7,6},{8,9},{9,8},{10,11... | collective-permute-start | bytes 172040 | tf_op jit(solution)/shard_map/ppermute | solution.py:462
  127.1 1.2 collective-permute-start.9
  128.4 3.3 %collective-permute-start.11 = (f32[3,2816]{1,0:T(4,128)S(1)}, f32[3,2816]{1,0:T(4,128)S(1)}, u32[]{:S(2)}, u32[]{:S(2)}) collective-permute-start(f32[3,2816]{1,0:T(4,128)S(1)} %get-tuple-element.81), channel_id=1, source_target_pairs={{1,0},{2,1},{3,2},{4,3},{5,4},{6,5},{7,6},{8,7},{9,8},{10,9},{11,1... | collective-permute-start | bytes 101384 | tf_op jit(solution)/shard_map/ppermute | solution.py:458
  131.6 0.8 collective-permute-done.9
  132.5 2.3 %collective-permute-start.12 = (f32[112,128]{1,0:T(8,128)S(1)}, f32[112,128]{1,0:T(8,128)S(1)}, u32[]{:S(2)}, u32[]{:S(2)}) collective-permute-start(f32[112,128]{1,0:T(8,128)S(1)} %add_add_fusion.near_ref), channel_id=1, source_target_pairs={{0,4},{1,5},{2,6},{3,7},{4,0},{5,1},{6,2},{7,3},{8,12},{9,13},{10,... | collective-permute-start | bytes 172040 | tf_op jit(solution)/shard_map/ppermute | solution.py:462
  134.8 0.1 collective-permute-done.11
  135.0 0.7 maximum_dynamic-update-slice_fusion
  135.6 5.6 %collective-permute-done.12.far_ref = f32[112,128]{1,0:T(8,128)S(1)} collective-permute-done((f32[112,128]{1,0:T(8,128)S(1)}, f32[112,128]{1,0:T(8,128)S(1)}, u32[]{:S(2)}, u32[]{:S(2)}) %collective-permute-start.12) | collective-permute-done | bytes 57376 | tf_op jit(solution)/shard_map/ppermute | solution.py:462
  141.3 0.7 shard_map.125
  (44 shorter events, 0.4 us)
Async XLA Ops:
  1.4 5.8 %collective-permute-start = (bf16[3,2816]{1,0:T(4,128)(2,1)S(1)}, bf16[3,2816]{1,0:T(4,128)(2,1)S(1)}, u32[]{:S(2)}, u32[]{:S(2)}) collective-permute-start(bf16[3,2816]{1,0:T(4,128)(2,1)S(1)} %slice_bitcast_fusion), channel_id=1, source_target_pairs={{0,1},{1,2},{2,3},{3,4},{4,5},{5,6},{6,7},{7,8},{8,9},{9,10},{10,1... | collective-permute-start | bytes 50696 | tf_op jit(solution)/shard_map/ppermute | solution.py:458
  7.2 4.9 %copy-start.3 = (bf16[3,2816]{1,0:T(4,128)(2,1)}, bf16[3,2816]{1,0:T(4,128)(2,1)S(1)}, u32[]{:S(2)}) copy-start(bf16[3,2816]{1,0:T(4,128)(2,1)S(1)} %collective-permute-done.halo_ref) | copy-start | bytes 50692
  12.1 46.5 %all-to-all-start = ((bf16[32,168,128]{2,1,0:T(8,128)(2,1)}), bf16[32,168,128]{2,1,0:T(8,128)(2,1)S(1)}, u32[]{:S(2)}, u32[]{:S(2)}) async-start(bf16[32,168,128]{2,1,0:T(8,128)(2,1)} %shard_map.119), calls=%async_computation | async-start | bytes 2752512 | tf_op jit(solution)/shard_map/all_to_all | solution.py:507
  60.0 38.7 %copy-start.1 = (f32[1,40,256]{2,1,0:T(8,128)S(1)}, f32[1,40,256]{2,1,0:T(8,128)}, u32[]{:S(2)}) copy-start(f32[1,40,256]{2,1,0:T(8,128)} %param.10) | copy-start | bytes 122884
  60.0 38.7 %copy-start.2 = (f32[256,256]{1,0:T(8,128)S(1)}, f32[256,256]{1,0:T(8,128)}, u32[]{:S(2)}) copy-start(f32[256,256]{1,0:T(8,128)} %get-tuple-element.54.slope_ref) | copy-start | bytes 786436
  60.0 38.7 %copy-start.4 = (bf16[3,2816]{1,0:T(4,128)(2,1)S(1)}, bf16[3,2816]{1,0:T(4,128)(2,1)}, u32[]{:S(2)}) copy-start(bf16[3,2816]{1,0:T(4,128)(2,1)} %copy-done.3) | copy-start | bytes 50692
  60.0 38.7 %copy-start.5 = (f32[40,256]{1,0:T(8,128)S(1)}, f32[40,256]{1,0:T(8,128)}, u32[]{:S(2)}) copy-start(f32[40,256]{1,0:T(8,128)} %get-tuple-element.57.colin_ref.col_ref) | copy-start | bytes 122884
  60.0 38.7 %copy-start.6 = (f32[40,256]{1,0:T(8,128)S(1)}, f32[40,256]{1,0:T(8,128)}, u32[]{:S(2)}) copy-start(f32[40,256]{1,0:T(8,128)} %get-tuple-element.58.row_ref) | copy-start | bytes 122884
  60.0 38.7 %copy-start.7 = (bf16[256,256]{1,0:T(8,128)(2,1)S(1)}, bf16[256,256]{1,0:T(8,128)(2,1)}, u32[]{:S(2)}) copy-start(bf16[256,256]{1,0:T(8,128)(2,1)} %get-tuple-element.52.bc_ref) | copy-start | bytes 393220
  60.0 38.7 %copy-start.8 = (bf16[256,256]{1,0:T(8,128)(2,1)S(1)}, bf16[256,256]{1,0:T(8,128)(2,1)}, u32[]{:S(2)}) copy-start(bf16[256,256]{1,0:T(8,128)(2,1)} %get-tuple-element.53.bct_ref) | copy-start | bytes 393220
  60.0 38.7 %copy-start.9 = (f32[128,256]{1,0:T(8,128)S(1)}, f32[128,256]{1,0:T(8,128)}, u32[]{:S(2)}) copy-start(f32[128,256]{1,0:T(8,128)} %get-tuple-element.55.gbin_ref) | copy-start | bytes 393220
  60.1 38.7 %copy-start.10 = (f32[128,256]{1,0:T(8,128)S(1)}, f32[128,256]{1,0:T(8,128)}, u32[]{:S(2)}) copy-start(f32[128,256]{1,0:T(8,128)} %get-tuple-element.56.gcin_ref) | copy-start | bytes 393220
  60.1 38.7 %copy-start.11 = (f32[40,256]{1,0:T(8,128)S(1)}, f32[40,256]{1,0:T(8,128)}, u32[]{:S(2)}) copy-start(f32[40,256]{1,0:T(8,128)} %get-tuple-element.59.skiprow_ref) | copy-start | bytes 122884
  60.1 38.7 %copy-start.12 = (f32[40,256]{1,0:T(8,128)S(1)}, f32[40,256]{1,0:T(8,128)}, u32[]{:S(2)}) copy-start(f32[40,256]{1,0:T(8,128)} %get-tuple-element.60.sofar_ref) | copy-start | bytes 122884
  60.1 38.7 %copy-start.13 = (f32[40,128]{1,0:T(8,128)S(1)}, f32[40,128]{1,0:T(8,128)}, u32[]{:S(2)}) copy-start(f32[40,128]{1,0:T(8,128)} %get-tuple-element.61.end_ref) | copy-start | bytes 61444
  98.8 12.9 %copy-start.14 = (f32[40]{0:T(128)S(1)}, f32[40]{0:T(128)}, u32[]{:S(2)}) copy-start(f32[40]{0:T(128)} %rate_ref.3) | copy-start | bytes 484
  98.8 22.6 %copy-start = (f32[4,2816]{1,0:T(4,128)S(1)}, f32[4,2816]{1,0:T(4,128)}, u32[]{:S(2)}) copy-start(f32[4,2816]{1,0:T(4,128)} %w_ref.3) | copy-start | bytes 135172
  105.5 1.3 collective-permute-start.1
  106.9 6.3 %collective-permute-start.2 = (f32[112,128]{1,0:T(8,128)S(1)}, f32[112,128]{1,0:T(8,128)S(1)}, u32[]{:S(2)}, u32[]{:S(2)}) collective-permute-start(f32[112,128]{1,0:T(8,128)S(1)} %add.41), channel_id=1, source_target_pairs={{0,64},{32,96},{64,0},{96,32},{128,192},{160,224},{192,128},{224,1... | collective-permute-start | bytes 172040 | tf_op jit(solution)/shard_map/ppermute | solution.py:462
  108.5 5.9 %collective-permute-start.3 = (f32[112,128]{1,0:T(8,128)S(1)}, f32[112,128]{1,0:T(8,128)S(1)}, u32[]{:S(2)}, u32[]{:S(2)}) collective-permute-start(f32[112,128]{1,0:T(8,128)S(1)} %add.41), channel_id=1, source_target_pairs={{0,128},{32,160},{64,192},{96,224},{128,0},{160,32},{192,64},{224,... | collective-permute-start | bytes 172040 | tf_op jit(solution)/shard_map/ppermute | solution.py:462
  111.2 5.4 %collective-permute-start.4 = (f32[112,128]{1,0:T(8,128)S(1)}, f32[112,128]{1,0:T(8,128)S(1)}, u32[]{:S(2)}, u32[]{:S(2)}) collective-permute-start(f32[112,128]{1,0:T(8,128)S(1)} %add.41), channel_id=1, source_target_pairs={{0,192},{32,224},{64,128},{96,160},{128,64},{160,96},{192,0},{224,... | collective-permute-start | bytes 172040 | tf_op jit(solution)/shard_map/ppermute | solution.py:462
  116.6 7.3 %collective-permute-start.5 = (f32[112,128]{1,0:T(8,128)S(1)}, f32[112,128]{1,0:T(8,128)S(1)}, u32[]{:S(2)}, u32[]{:S(2)}) collective-permute-start(f32[112,128]{1,0:T(8,128)S(1)} %add_add_fusion.2), channel_id=1, source_target_pairs={{0,8},{1,9},{2,10},{3,11},{4,12},{5,13},{6,14},{7,15},{8,0},{9,1},... | collective-permute-start | bytes 172040 | tf_op jit(solution)/shard_map/ppermute | solution.py:462
  117.3 6.6 %collective-permute-start.6 = (f32[112,128]{1,0:T(8,128)S(1)}, f32[112,128]{1,0:T(8,128)S(1)}, u32[]{:S(2)}, u32[]{:S(2)}) collective-permute-start(f32[112,128]{1,0:T(8,128)S(1)} %add_add_fusion.2), channel_id=1, source_target_pairs={{0,16},{1,17},{2,18},{3,19},{4,20},{5,21},{6,22},{7,23},{8,24},{9,... | collective-permute-start | bytes 172040 | tf_op jit(solution)/shard_map/ppermute | solution.py:462
  119.3 5.4 %collective-permute-start.7 = (f32[112,128]{1,0:T(8,128)S(1)}, f32[112,128]{1,0:T(8,128)S(1)}, u32[]{:S(2)}, u32[]{:S(2)}) collective-permute-start(f32[112,128]{1,0:T(8,128)S(1)} %add_add_fusion.2), channel_id=1, source_target_pairs={{0,24},{1,25},{2,26},{3,27},{4,28},{5,29},{6,30},{7,31},{8,16},{9,... | collective-permute-start | bytes 172040 | tf_op jit(solution)/shard_map/ppermute | solution.py:462
  124.7 6.9 %collective-permute-start.10 = (f32[112,128]{1,0:T(8,128)S(1)}, f32[112,128]{1,0:T(8,128)S(1)}, u32[]{:S(2)}, u32[]{:S(2)}) collective-permute-start(f32[112,128]{1,0:T(8,128)S(1)} %add_add_fusion.1), channel_id=1, source_target_pairs={{0,3},{1,2},{2,1},{3,0},{4,7},{5,6},{6,5},{7,4},{8,11},{9,10},{10,... | collective-permute-start | bytes 172040 | tf_op jit(solution)/shard_map/ppermute | solution.py:462
  125.6 6.0 %collective-permute-start.8 = (f32[112,128]{1,0:T(8,128)S(1)}, f32[112,128]{1,0:T(8,128)S(1)}, u32[]{:S(2)}, u32[]{:S(2)}) collective-permute-start(f32[112,128]{1,0:T(8,128)S(1)} %add_add_fusion.1), channel_id=1, source_target_pairs={{0,1},{1,0},{2,3},{3,2},{4,5},{5,4},{6,7},{7,6},{8,9},{9,8},{10,11... | collective-permute-start | bytes 172040 | tf_op jit(solution)/shard_map/ppermute | solution.py:462
  127.1 5.4 %collective-permute-start.9 = (f32[112,128]{1,0:T(8,128)S(1)}, f32[112,128]{1,0:T(8,128)S(1)}, u32[]{:S(2)}, u32[]{:S(2)}) collective-permute-start(f32[112,128]{1,0:T(8,128)S(1)} %add_add_fusion.1), channel_id=1, source_target_pairs={{0,2},{1,3},{2,0},{3,1},{4,6},{5,7},{6,4},{7,5},{8,10},{9,11},{10,... | collective-permute-start | bytes 172040 | tf_op jit(solution)/shard_map/ppermute | solution.py:462
  128.4 6.6 %collective-permute-start.11 = (f32[3,2816]{1,0:T(4,128)S(1)}, f32[3,2816]{1,0:T(4,128)S(1)}, u32[]{:S(2)}, u32[]{:S(2)}) collective-permute-start(f32[3,2816]{1,0:T(4,128)S(1)} %get-tuple-element.81), channel_id=1, source_target_pairs={{1,0},{2,1},{3,2},{4,3},{5,4},{6,5},{7,6},{8,7},{9,8},{10,9},{11,1... | collective-permute-start | bytes 101384 | tf_op jit(solution)/shard_map/ppermute | solution.py:458
  132.5 8.8 %collective-permute-start.12 = (f32[112,128]{1,0:T(8,128)S(1)}, f32[112,128]{1,0:T(8,128)S(1)}, u32[]{:S(2)}, u32[]{:S(2)}) collective-permute-start(f32[112,128]{1,0:T(8,128)S(1)} %add_add_fusion.near_ref), channel_id=1, source_target_pairs={{0,4},{1,5},{2,6},{3,7},{4,0},{5,1},{6,2},{7,3},{8,12},{9,13},{10,... | collective-permute-start | bytes 172040 | tf_op jit(solution)/shard_map/ppermute | solution.py:462

commit v9 on v8

--- a/solution.py
+++ b/solution.py
@@ -85,14 +85,15 @@
 
 
 def decay_kernel(
-    step_hbm, rate_hbm, dy_hbm,
-    dywt_ref, tail_ref, head_ref,
-    step_ref, rate_ref, dy_ref, few_sem, dy_sem,
+    step_hbm, rate_hbm, dy_hbm, x_hbm, w_hbm, bias_hbm,
+    dywt_ref, x_ref, w_ref, bias_ref, tail_ref, head_ref,
+    step_ref, rate_ref, dy_ref, few_sem, dy_sem, next_sem,
 ):
     span = X_WIDTH // PARTS
     few = started(few_sem, (step_hbm, step_ref), (rate_hbm, rate_ref))
     cuts = [slice(g * span, (g + 1) * span) for g in range(PARTS)]
     many = started(dy_sem, *[(dy_hbm.at[:, cut], dy_ref.at[:, cut]) for cut in cuts])
+    ahead = started(next_sem, (x_hbm, x_ref), (w_hbm, w_ref), (bias_hbm, bias_ref))
     for copy in few:
         copy.wait()
     cum = logs_of(step_ref, rate_ref)
@@ -108,23 +109,20 @@
     for g in range(PARTS):
         many[g].wait()
         lax.fori_loop(g * per, (g + 1) * per, turn, 0, unroll=True)
+    for copy in ahead:
+        copy.wait()
 
 
 def front_kernel(
-    halo_ref, dywt_ref, tail_ref, head_ref,
-    x_hbm, w_hbm, bias_hbm,
+    halo_ref, dywt_ref, tail_ref, head_ref, x_ref, w_ref, bias_ref,
     msg_hbm,
-    x_ref, w_ref, bias_ref, msg_ref, bc_ref, xwt_ref, few_sem, x_sem, msg_sem,
+    msg_ref, bc_ref, xwt_ref, msg_sem,
     *, chunks, rows,
 ):
     per = PAIRS // PARTS
     span = per * LANE
     held = chunks // PARTS
-    few = started(
-        few_sem, (w_hbm, w_ref), (bias_hbm, bias_ref), (x_hbm.at[:, X_WIDTH:], x_ref.at[:, X_WIDTH:])
-    )
     cuts = [slice(g * span, (g + 1) * span) for g in range(PARTS)]
-    many = started(x_sem, *[(x_hbm.at[:, cut], x_ref.at[:, cut]) for cut in cuts])
 
     d_end = jnp.broadcast_to(head_ref[:, GROUP - 1 :], (HEADS, LANE))
     part_a = d_end.astype(BF16).astype(F32)
@@ -141,13 +139,10 @@
         pre = pre_act_of(taps_of(x_ref, halo_ref, c), w_ref, bias_ref, c)
         return (pre * jax.nn.sigmoid(pre)).astype(BF16)
 
-    for copy in few:
-        copy.wait()
     bc_ref[:, :STATE] = active(PAIRS)
     bc_ref[:, STATE:] = active(PAIRS + 1)
     sent = []
     for g in range(PARTS):
-        many[g].wait()
 
         def conv(p, carry, g=g):
             c = g * per + p
@@ -481,28 +476,37 @@
     by_head = ((X_WIDTH, GROUP), BF16)
     dma = pltpu.SemaphoreType.DMA
     halo = shifted(x_in[GROUP - rim :], "seq", 1)
-    dywt, tail, head = call(
+    dywt, x_near, w_near, bias_near, tail, head = call(
         decay_kernel,
-        [((X_WIDTH, GROUP), BF16), wide_heads, wide_heads],
-        [wide_heads, pltpu.SMEM((HEADS,), F32), ((GROUP, X_WIDTH), BF16), dma((2,)), dma((PARTS,))],
-        steps, decay_rates, dy, large=3, kept=(0,), limit=SMALL_LIMIT,
+        [
+            by_head,
+            ((GROUP, channels), BF16),
+            ((KCONV, channels), F32),
+            ((channels,), F32),
+            wide_heads,
+            wide_heads,
+        ],
+        [
+            wide_heads,
+            pltpu.SMEM((HEADS,), F32),
+            ((GROUP, X_WIDTH), BF16),
+            dma((2,)),
+            dma((PARTS,)),
+            dma((3,)),
+        ],
+        steps, decay_rates, dy, x_in, conv_weight, conv_bias,
+        large=6, kept=range(4), limit=SMALL_LIMIT,
     )
     (msg,) = call(
         functools.partial(front_kernel, chunks=chunks, rows=rows),
         [((chunks, 2 * rows + TAIL_ROWS, LANE), BF16)],
         [
-            ((GROUP, channels), BF16),
-            ((KCONV, channels), F32),
-            ((channels,), F32),
             ((chunks, 2 * rows + TAIL_ROWS, LANE), BF16),
             ((GROUP, 2 * STATE), BF16),
             ((X_WIDTH // PARTS, GROUP), BF16),
-            dma((3,)),
             dma((PARTS,)),
-            dma((PARTS,)),
-        ],
-        halo, dywt, tail, head, x_in, conv_weight, conv_bias,
-        large=3, large_out=True, limit=SMALL_LIMIT,
+        ],
+        halo, dywt, tail, head, x_near, w_near, bias_near, large_out=True, limit=SMALL_LIMIT,
     )
     got = lax.all_to_all(msg, "seq", 0, 0, tiled=True)
     (own, scale, xwt, dywt, bc, bct, slope, gb, gc, col_sums, row_sums, skip_rows, sofar, d_end) = call(

time: 142 us -> 141 us (level)
  transfers between devices with their start and end apart: 14 -> 14, of which waited for: 8 -> 8; matrix products, arithmetic and copies ran while one was open for 1% -> 1% of each run, Pallas kernels for 16% -> 17%
where the time goes in v9:
time: 141 us
  blocking collectives  38.6 us (27%)
  Pallas kernels  35.7 us (25%)
  starting transfers between devices  34.6 us (25%)
  waiting for transfers between devices  29.1 us (21%)
    all_to_all x1, blocking collectives, shards(): back = lax.all_to_all(turned, 'seq', 0, 0, tiled=True)  38.6 us
    pallas_call x8, Pallas kernels, call(): pl.pallas_call(kernel, out_shape=[out_space(*out) if large_out or i in ke...  35.7 us
    all_to_all x1, waiting for transfers between devices, shards(): got = lax.all_to_all(msg, 'seq', 0, 0, tiled=True)  17.1 us
    ppermute x11, starting transfers between devices, flipped(): lax.ppermute(array, axis, [(i, i ^ bits) for i in range(lax.axis_size(axi...  15.5 us
    all_to_all x1, starting transfers between devices, shards(): got = lax.all_to_all(msg, 'seq', 0, 0, tiled=True)  12 us
    ppermute x11, waiting for transfers between devices, flipped(): lax.ppermute(array, axis, [(i, i ^ bits) for i in range(lax.axis_size(axi...  11.9 us
    ppermute x2, starting transfers between devices, shifted(): return lax.ppermute(array, axis, pairs)  7.06 us
  transfers between devices with their start and end apart: 14, of which 8 were waited for; matrix products, arithmetic and copies ran while one was open for 1% of the time, Pallas kernels for 17%

profile of v9, /device:TPU:32, one launch (start us, length us, event | category | flops | bytes accessed | tf_op | source)
XLA Modules:
  0.0 140.7 jit_solution(877855753955280196)
XLA Ops:
  0.6 0.8 slice_bitcast_fusion
  1.4 3.8 %collective-permute-start = (bf16[3,2816]{1,0:T(4,128)(2,1)S(1)}, bf16[3,2816]{1,0:T(4,128)(2,1)S(1)}, u32[]{:S(2)}, u32[]{:S(2)}) collective-permute-start(bf16[3,2816]{1,0:T(4,128)(2,1)S(1)} %slice_bitcast_fusion), channel_id=1, source_target_pairs={{0,1},{1,2},{2,3},{3,4},{4,5},{5,6},{6,7},{7,8},{8,9},{9,10},{10,1... | collective-permute-start | bytes 50696 | tf_op jit(solution)/shard_map/ppermute | solution.py:453
  5.3 2.4 %shard_map.118 = (bf16[2560,256]{1,0:T(8,128)(2,1)S(1)}, bf16[256,2816]{1,0:T(8,128)(2,1)S(1)}, f32[4,2816]{1,0:T(4,128)S(1)}, f32[2816]{0:T(1024)S(1)}, f32[40,256]{1,0:T(8,128)S(1)}, /*index=5*/f32[40,256]{1,0:T(8,128)S(1)}) custom-call(f32[40,256]{1,0:T(8,128)} %bitcast.11, f32[40]{0:T(128)} %rate_ref.3, bf16[256,2560]{1,0:T(8,128)(2,1)} %bitcast.17, ...), custom_call_target="tpu_custom_call" | custom-call | tf_op jit(solution)/shard_map/pallas_call | solution.py:437
  7.7 3.7 %shard_map.119 = bf16[32,168,128]{2,1,0:T(8,128)(2,1)} custom-call(bf16[3,2816]{1,0:T(4,128)(2,1)S(1)} %collective-permute-done.halo_ref, bf16[2560,256]{1,0:T(8,128)(2,1)S(1)} %get-tuple-element.50.dywt_ref, f32[40,256]{1,0:T(8,128)S(1)} %get-tuple-element.51.tail_ref, f32[40,256]{1,0:T(8,128)S(1)} %get-tuple-element.52.head_ref, ...), custom_call_target="tpu_custom_call" | custom-call | tf_op jit(solution)/shard_map/pallas_call | solution.py:437
  11.4 12.0 %all-to-all-start = ((bf16[32,168,128]{2,1,0:T(8,128)(2,1)}), bf16[32,168,128]{2,1,0:T(8,128)(2,1)S(1)}, u32[]{:S(2)}, u32[]{:S(2)}) async-start(bf16[32,168,128]{2,1,0:T(8,128)(2,1)} %shard_map.119), calls=%async_computation | async-start | bytes 2752512 | tf_op jit(solution)/shard_map/all_to_all | solution.py:511
  23.4 16.8 %shard_map.120 = (f32[256,2560]{1,0:T(8,128)}, bf16[256,2560]{1,0:T(8,128)(2,1)}, bf16[2560,256]{1,0:T(8,128)(2,1)}, bf16[2560,256]{1,0:T(8,128)(2,1)}, bf16[256...) custom-call(bf16[256,2816]{1,0:T(8,128)(2,1)} %bitcast.15, ...), custom_call_target="tpu_custom_call" | custom-call | tf_op jit(solution)/shard_map/pallas_call | solution.py:437
  40.3 17.1 %all-to-all-done.got_ref = bf16[32,168,128]{2,1,0:T(8,128)(2,1)S(1)} async-done(((bf16[32,168,128]{2,1,0:T(8,128)(2,1)}), bf16[32,168,128]{2,1,0:T(8,128)(2,1)S(1)}, u32[]{:S(2)}, u32[]{:S(2)}) %all-to-all-start) | async-done | bytes 1376288 | tf_op jit(solution)/shard_map/all_to_all | solution.py:511
  57.4 1.4 shard_map.121
  58.9 38.6 %all_to_all.10.back_ref = bf16[32,160,128]{2,1,0:T(8,128)(2,1)S(1)} all-to-all(bf16[32,160,128]{2,1,0:T(8,128)(2,1)} %shard_map.121), channel_id=1, replica_groups=mesh['dp'=8,'seq'=32] {'seq'}, dimensions={0} | all-to-all | bytes 2621440 | tf_op jit(solution)/shard_map/all_to_all | solution.py:549
  97.6 6.7 %shard_map.122 = (f32[256,2816]{1,0:T(8,128)S(1)}, f32[3,2816]{1,0:T(4,128)S(1)}, f32[40,256]{1,0:T(8,128)S(1)}, f32[40,256]{1,0:T(8,128)S(1)}, f32[40,128]{1,0:T(8,128)S(1)}, /*index=5*/f32[112,128]{1,0:T(8,128)S(1)}) custom-call(bf16[32,160,128]{2,1,0:T(8,128)(2,1)S(1)} %all_to_all.10.back_ref, bf16[256,256]{1,0:T(8,128)(2,1)S(1)} %copy-done.7, ...), custom_call_target="tpu_custom_call" | custom-call | tf_op jit(solution)/shard_map/pallas_call | solution.py:437
  104.4 1.2 collective-permute-done.1
  105.7 1.6 %collective-permute-start.2 = (f32[112,128]{1,0:T(8,128)S(1)}, f32[112,128]{1,0:T(8,128)S(1)}, u32[]{:S(2)}, u32[]{:S(2)}) collective-permute-start(f32[112,128]{1,0:T(8,128)S(1)} %add.41), channel_id=1, source_target_pairs={{0,64},{32,96},{64,0},{96,32},{128,192},{160,224},{192,128},{224,1... | collective-permute-start | bytes 172040 | tf_op jit(solution)/shard_map/ppermute | solution.py:457
  107.3 2.7 %collective-permute-start.3 = (f32[112,128]{1,0:T(8,128)S(1)}, f32[112,128]{1,0:T(8,128)S(1)}, u32[]{:S(2)}, u32[]{:S(2)}) collective-permute-start(f32[112,128]{1,0:T(8,128)S(1)} %add.41), channel_id=1, source_target_pairs={{0,128},{32,160},{64,192},{96,224},{128,0},{160,32},{192,64},{224,... | collective-permute-start | bytes 172040 | tf_op jit(solution)/shard_map/ppermute | solution.py:457
  110.0 0.5 collective-permute-start.4
  110.5 1.5 %shard_map.123 = f32[40,256]{1,0:T(8,128)} custom-call(f32[40,256]{1,0:T(8,128)S(1)} %get-tuple-element.75.q_ref, f32[40,256]{1,0:T(8,128)S(1)} %get-tuple-element.76.r_ref, f32[40,128]{1,0:T(8,128)S(1)} %get-tuple-element.77.four_ref, f32[40,256]{1,0:T(8,128)S(1)} %copy-done.5, f32[40,256]{1,0:T(8,128)S(1)} %copy-done.6, f32[40]{0:T(128)S(1)} %copy-done.14), custom_call_target="tpu_custom_call" | custom-call | tf_op jit(solution)/shard_map/pallas_call | solution.py:437
  112.0 1.1 collective-permute-done.3
  113.1 2.3 %collective-permute-done.4 = f32[112,128]{1,0:T(8,128)S(1)} collective-permute-done((f32[112,128]{1,0:T(8,128)S(1)}, f32[112,128]{1,0:T(8,128)S(1)}, u32[]{:S(2)}, u32[]{:S(2)}) %collective-permute-start.4) | collective-permute-done | bytes 57376 | tf_op jit(solution)/shard_map/ppermute | solution.py:457
  115.4 0.7 collective-permute-start.5
  116.1 2.0 %collective-permute-start.6 = (f32[112,128]{1,0:T(8,128)S(1)}, f32[112,128]{1,0:T(8,128)S(1)}, u32[]{:S(2)}, u32[]{:S(2)}) collective-permute-start(f32[112,128]{1,0:T(8,128)S(1)} %add_add_fusion.2), channel_id=1, source_target_pairs={{0,16},{1,17},{2,18},{3,19},{4,20},{5,21},{6,22},{7,23},{8,24},{9,... | collective-permute-start | bytes 172040 | tf_op jit(solution)/shard_map/ppermute | solution.py:457
  118.1 2.1 %collective-permute-start.7 = (f32[112,128]{1,0:T(8,128)S(1)}, f32[112,128]{1,0:T(8,128)S(1)}, u32[]{:S(2)}, u32[]{:S(2)}) collective-permute-start(f32[112,128]{1,0:T(8,128)S(1)} %add_add_fusion.2), channel_id=1, source_target_pairs={{0,24},{1,25},{2,26},{3,27},{4,28},{5,29},{6,30},{7,31},{8,16},{9,... | collective-permute-start | bytes 172040 | tf_op jit(solution)/shard_map/ppermute | solution.py:457
  120.2 2.5 %shard_map.124 = (bf16[256,2816]{1,0:T(8,128)(2,1)}, f32[16,2816]{1,0:T(8,128)S(1)}) custom-call(f32[256,2816]{1,0:T(8,128)S(1)} %get-tuple-element.81.gpre_ref, f32[4,2816]{1,0:T(4,128)S(1)} %copy-done), custom_call_target="tpu_custom_call" | custom-call | tf_op jit(solution)/shard_map/pallas_call | solution.py:437
  122.7 0.8 collective-permute-done.7
  123.5 0.9 collective-permute-start.10
  124.4 1.5 %collective-permute-start.8 = (f32[112,128]{1,0:T(8,128)S(1)}, f32[112,128]{1,0:T(8,128)S(1)}, u32[]{:S(2)}, u32[]{:S(2)}) collective-permute-start(f32[112,128]{1,0:T(8,128)S(1)} %add_add_fusion.1), channel_id=1, source_target_pairs={{0,1},{1,0},{2,3},{3,2},{4,5},{5,4},{6,7},{7,6},{8,9},{9,8},{10,11... | collective-permute-start | bytes 172040 | tf_op jit(solution)/shard_map/ppermute | solution.py:457
  125.9 1.2 collective-permute-start.9
  127.2 3.2 %collective-permute-start.11 = (f32[3,2816]{1,0:T(4,128)S(1)}, f32[3,2816]{1,0:T(4,128)S(1)}, u32[]{:S(2)}, u32[]{:S(2)}) collective-permute-start(f32[3,2816]{1,0:T(4,128)S(1)} %get-tuple-element.87), channel_id=1, source_target_pairs={{1,0},{2,1},{3,2},{4,3},{5,4},{6,5},{7,6},{8,7},{9,8},{10,9},{11,1... | collective-permute-start | bytes 101384 | tf_op jit(solution)/shard_map/ppermute | solution.py:453
  130.4 0.8 collective-permute-done.9
  131.3 2.3 %collective-permute-start.12 = (f32[112,128]{1,0:T(8,128)S(1)}, f32[112,128]{1,0:T(8,128)S(1)}, u32[]{:S(2)}, u32[]{:S(2)}) collective-permute-start(f32[112,128]{1,0:T(8,128)S(1)} %add_add_fusion.near_ref), channel_id=1, source_target_pairs={{0,4},{1,5},{2,6},{3,7},{4,0},{5,1},{6,2},{7,3},{8,12},{9,13},{10,... | collective-permute-start | bytes 172040 | tf_op jit(solution)/shard_map/ppermute | solution.py:457
  133.6 0.2 collective-permute-done.11
  133.8 0.7 maximum_dynamic-update-slice_fusion
  134.5 5.6 %collective-permute-done.12.far_ref = f32[112,128]{1,0:T(8,128)S(1)} collective-permute-done((f32[112,128]{1,0:T(8,128)S(1)}, f32[112,128]{1,0:T(8,128)S(1)}, u32[]{:S(2)}, u32[]{:S(2)}) %collective-permute-start.12) | collective-permute-done | bytes 57376 | tf_op jit(solution)/shard_map/ppermute | solution.py:457
  140.1 0.7 shard_map.125
  (44 shorter events, 0.4 us)
Async XLA Ops:
  1.4 6.2 %collective-permute-start = (bf16[3,2816]{1,0:T(4,128)(2,1)S(1)}, bf16[3,2816]{1,0:T(4,128)(2,1)S(1)}, u32[]{:S(2)}, u32[]{:S(2)}) collective-permute-start(bf16[3,2816]{1,0:T(4,128)(2,1)S(1)} %slice_bitcast_fusion), channel_id=1, source_target_pairs={{0,1},{1,2},{2,3},{3,4},{4,5},{5,6},{6,7},{7,8},{8,9},{9,10},{10,1... | collective-permute-start | bytes 50696 | tf_op jit(solution)/shard_map/ppermute | solution.py:453
  7.7 3.7 %copy-start.3 = (bf16[3,2816]{1,0:T(4,128)(2,1)}, bf16[3,2816]{1,0:T(4,128)(2,1)S(1)}, u32[]{:S(2)}) copy-start(bf16[3,2816]{1,0:T(4,128)(2,1)S(1)} %collective-permute-done.halo_ref) | copy-start | bytes 50692
  11.4 46.0 %all-to-all-start = ((bf16[32,168,128]{2,1,0:T(8,128)(2,1)}), bf16[32,168,128]{2,1,0:T(8,128)(2,1)S(1)}, u32[]{:S(2)}, u32[]{:S(2)}) async-start(bf16[32,168,128]{2,1,0:T(8,128)(2,1)} %shard_map.119), calls=%async_computation | async-start | bytes 2752512 | tf_op jit(solution)/shard_map/all_to_all | solution.py:511
  58.8 38.7 %copy-start.1 = (f32[1,40,256]{2,1,0:T(8,128)S(1)}, f32[1,40,256]{2,1,0:T(8,128)}, u32[]{:S(2)}) copy-start(f32[1,40,256]{2,1,0:T(8,128)} %param.10) | copy-start | bytes 122884
  58.8 38.7 %copy-start.2 = (f32[256,256]{1,0:T(8,128)S(1)}, f32[256,256]{1,0:T(8,128)}, u32[]{:S(2)}) copy-start(f32[256,256]{1,0:T(8,128)} %get-tuple-element.60.slope_ref) | copy-start | bytes 786436
  58.8 38.7 %copy-start.4 = (bf16[3,2816]{1,0:T(4,128)(2,1)S(1)}, bf16[3,2816]{1,0:T(4,128)(2,1)}, u32[]{:S(2)}) copy-start(bf16[3,2816]{1,0:T(4,128)(2,1)} %copy-done.3) | copy-start | bytes 50692
  58.8 38.7 %copy-start.5 = (f32[40,256]{1,0:T(8,128)S(1)}, f32[40,256]{1,0:T(8,128)}, u32[]{:S(2)}) copy-start(f32[40,256]{1,0:T(8,128)} %get-tuple-element.63.colin_ref.col_ref) | copy-start | bytes 122884
  58.8 38.7 %copy-start.6 = (f32[40,256]{1,0:T(8,128)S(1)}, f32[40,256]{1,0:T(8,128)}, u32[]{:S(2)}) copy-start(f32[40,256]{1,0:T(8,128)} %get-tuple-element.64.row_ref) | copy-start | bytes 122884
  58.8 38.7 %copy-start.7 = (bf16[256,256]{1,0:T(8,128)(2,1)S(1)}, bf16[256,256]{1,0:T(8,128)(2,1)}, u32[]{:S(2)}) copy-start(bf16[256,256]{1,0:T(8,128)(2,1)} %get-tuple-element.58.bc_ref) | copy-start | bytes 393220
  58.8 38.7 %copy-start.8 = (bf16[256,256]{1,0:T(8,128)(2,1)S(1)}, bf16[256,256]{1,0:T(8,128)(2,1)}, u32[]{:S(2)}) copy-start(bf16[256,256]{1,0:T(8,128)(2,1)} %get-tuple-element.59.bct_ref) | copy-start | bytes 393220
  58.8 38.7 %copy-start.9 = (f32[128,256]{1,0:T(8,128)S(1)}, f32[128,256]{1,0:T(8,128)}, u32[]{:S(2)}) copy-start(f32[128,256]{1,0:T(8,128)} %get-tuple-element.61.gbin_ref) | copy-start | bytes 393220
  58.9 38.7 %copy-start.10 = (f32[128,256]{1,0:T(8,128)S(1)}, f32[128,256]{1,0:T(8,128)}, u32[]{:S(2)}) copy-start(f32[128,256]{1,0:T(8,128)} %get-tuple-element.62.gcin_ref) | copy-start | bytes 393220
  58.9 38.7 %copy-start.11 = (f32[40,256]{1,0:T(8,128)S(1)}, f32[40,256]{1,0:T(8,128)}, u32[]{:S(2)}) copy-start(f32[40,256]{1,0:T(8,128)} %get-tuple-element.65.skiprow_ref) | copy-start | bytes 122884
  58.9 38.7 %copy-start.12 = (f32[40,256]{1,0:T(8,128)S(1)}, f32[40,256]{1,0:T(8,128)}, u32[]{:S(2)}) copy-start(f32[40,256]{1,0:T(8,128)} %get-tuple-element.66.sofar_ref) | copy-start | bytes 122884
  58.9 38.7 %copy-start.13 = (f32[40,128]{1,0:T(8,128)S(1)}, f32[40,128]{1,0:T(8,128)}, u32[]{:S(2)}) copy-start(f32[40,128]{1,0:T(8,128)} %get-tuple-element.67.end_ref) | copy-start | bytes 61444
  97.6 12.9 %copy-start.14 = (f32[40]{0:T(128)S(1)}, f32[40]{0:T(128)}, u32[]{:S(2)}) copy-start(f32[40]{0:T(128)} %rate_ref.3) | copy-start | bytes 484
  97.6 22.6 %copy-start = (f32[4,2816]{1,0:T(4,128)S(1)}, f32[4,2816]{1,0:T(4,128)}, u32[]{:S(2)}) copy-start(f32[4,2816]{1,0:T(4,128)} %w_ref.3) | copy-start | bytes 135172
  104.3 1.3 collective-permute-start.1
  105.7 6.3 %collective-permute-start.2 = (f32[112,128]{1,0:T(8,128)S(1)}, f32[112,128]{1,0:T(8,128)S(1)}, u32[]{:S(2)}, u32[]{:S(2)}) collective-permute-start(f32[112,128]{1,0:T(8,128)S(1)} %add.41), channel_id=1, source_target_pairs={{0,64},{32,96},{64,0},{96,32},{128,192},{160,224},{192,128},{224,1... | collective-permute-start | bytes 172040 | tf_op jit(solution)/shard_map/ppermute | solution.py:457
  107.3 5.9 %collective-permute-start.3 = (f32[112,128]{1,0:T(8,128)S(1)}, f32[112,128]{1,0:T(8,128)S(1)}, u32[]{:S(2)}, u32[]{:S(2)}) collective-permute-start(f32[112,128]{1,0:T(8,128)S(1)} %add.41), channel_id=1, source_target_pairs={{0,128},{32,160},{64,192},{96,224},{128,0},{160,32},{192,64},{224,... | collective-permute-start | bytes 172040 | tf_op jit(solution)/shard_map/ppermute | solution.py:457
  110.0 5.4 %collective-permute-start.4 = (f32[112,128]{1,0:T(8,128)S(1)}, f32[112,128]{1,0:T(8,128)S(1)}, u32[]{:S(2)}, u32[]{:S(2)}) collective-permute-start(f32[112,128]{1,0:T(8,128)S(1)} %add.41), channel_id=1, source_target_pairs={{0,192},{32,224},{64,128},{96,160},{128,64},{160,96},{192,0},{224,... | collective-permute-start | bytes 172040 | tf_op jit(solution)/shard_map/ppermute | solution.py:457
  115.4 7.3 %collective-permute-start.5 = (f32[112,128]{1,0:T(8,128)S(1)}, f32[112,128]{1,0:T(8,128)S(1)}, u32[]{:S(2)}, u32[]{:S(2)}) collective-permute-start(f32[112,128]{1,0:T(8,128)S(1)} %add_add_fusion.2), channel_id=1, source_target_pairs={{0,8},{1,9},{2,10},{3,11},{4,12},{5,13},{6,14},{7,15},{8,0},{9,1},... | collective-permute-start | bytes 172040 | tf_op jit(solution)/shard_map/ppermute | solution.py:457
  116.1 6.6 %collective-permute-start.6 = (f32[112,128]{1,0:T(8,128)S(1)}, f32[112,128]{1,0:T(8,128)S(1)}, u32[]{:S(2)}, u32[]{:S(2)}) collective-permute-start(f32[112,128]{1,0:T(8,128)S(1)} %add_add_fusion.2), channel_id=1, source_target_pairs={{0,16},{1,17},{2,18},{3,19},{4,20},{5,21},{6,22},{7,23},{8,24},{9,... | collective-permute-start | bytes 172040 | tf_op jit(solution)/shard_map/ppermute | solution.py:457
  118.1 5.4 %collective-permute-start.7 = (f32[112,128]{1,0:T(8,128)S(1)}, f32[112,128]{1,0:T(8,128)S(1)}, u32[]{:S(2)}, u32[]{:S(2)}) collective-permute-start(f32[112,128]{1,0:T(8,128)S(1)} %add_add_fusion.2), channel_id=1, source_target_pairs={{0,24},{1,25},{2,26},{3,27},{4,28},{5,29},{6,30},{7,31},{8,16},{9,... | collective-permute-start | bytes 172040 | tf_op jit(solution)/shard_map/ppermute | solution.py:457
  123.5 6.9 %collective-permute-start.10 = (f32[112,128]{1,0:T(8,128)S(1)}, f32[112,128]{1,0:T(8,128)S(1)}, u32[]{:S(2)}, u32[]{:S(2)}) collective-permute-start(f32[112,128]{1,0:T(8,128)S(1)} %add_add_fusion.1), channel_id=1, source_target_pairs={{0,3},{1,2},{2,1},{3,0},{4,7},{5,6},{6,5},{7,4},{8,11},{9,10},{10,... | collective-permute-start | bytes 172040 | tf_op jit(solution)/shard_map/ppermute | solution.py:457
  124.4 6.0 %collective-permute-start.8 = (f32[112,128]{1,0:T(8,128)S(1)}, f32[112,128]{1,0:T(8,128)S(1)}, u32[]{:S(2)}, u32[]{:S(2)}) collective-permute-start(f32[112,128]{1,0:T(8,128)S(1)} %add_add_fusion.1), channel_id=1, source_target_pairs={{0,1},{1,0},{2,3},{3,2},{4,5},{5,4},{6,7},{7,6},{8,9},{9,8},{10,11... | collective-permute-start | bytes 172040 | tf_op jit(solution)/shard_map/ppermute | solution.py:457
  125.9 5.4 %collective-permute-start.9 = (f32[112,128]{1,0:T(8,128)S(1)}, f32[112,128]{1,0:T(8,128)S(1)}, u32[]{:S(2)}, u32[]{:S(2)}) collective-permute-start(f32[112,128]{1,0:T(8,128)S(1)} %add_add_fusion.1), channel_id=1, source_target_pairs={{0,2},{1,3},{2,0},{3,1},{4,6},{5,7},{6,4},{7,5},{8,10},{9,11},{10,... | collective-permute-start | bytes 172040 | tf_op jit(solution)/shard_map/ppermute | solution.py:457
  127.2 6.6 %collective-permute-start.11 = (f32[3,2816]{1,0:T(4,128)S(1)}, f32[3,2816]{1,0:T(4,128)S(1)}, u32[]{:S(2)}, u32[]{:S(2)}) collective-permute-start(f32[3,2816]{1,0:T(4,128)S(1)} %get-tuple-element.87), channel_id=1, source_target_pairs={{1,0},{2,1},{3,2},{4,3},{5,4},{6,5},{7,6},{8,7},{9,8},{10,9},{11,1... | collective-permute-start | bytes 101384 | tf_op jit(solution)/shard_map/ppermute | solution.py:453
  131.3 8.8 %collective-permute-start.12 = (f32[112,128]{1,0:T(8,128)S(1)}, f32[112,128]{1,0:T(8,128)S(1)}, u32[]{:S(2)}, u32[]{:S(2)}) collective-permute-start(f32[112,128]{1,0:T(8,128)S(1)} %add_add_fusion.near_ref), channel_id=1, source_target_pairs={{0,4},{1,5},{2,6},{3,7},{4,0},{5,1},{6,2},{7,3},{8,12},{9,13},{10,... | collective-permute-start | bytes 172040 | tf_op jit(solution)/shard_map/ppermute | solution.py:457

commit v10 on v9

--- a/solution.py
+++ b/solution.py
@@ -409,8 +409,10 @@
     gsteps_ref[...] = -head_column(rate_ref) * grad_log
 
 
-def unpack_kernel(near_ref, far_ref, weight_ref, bias_ref, rates_ref, skip_ref, sum_ref):
-    sum_ref[...] = near_ref[...] + far_ref[...]
+def unpack_kernel(
+    own_ref, near_ref, far_ref, both_ref, weight_ref, bias_ref, rates_ref, skip_ref, sum_ref
+):
+    sum_ref[...] = (own_ref[...] + near_ref[...]) + (far_ref[...] + both_ref[...])
     tiles = PAIRS + 2
     for c in range(tiles):
         at = slice(c * LANE, (c + 1) * LANE)
@@ -592,9 +594,9 @@
     sums = four_summed(sums, "seq", 8)
     sums, edge, grad_in = lax.optimization_barrier((sums, edge, grad_in))
     next_rows = shifted(edge, "seq", -1)
-    sums = four_summed(sums, "seq", 1)
+    sums = sums + flipped(sums, "seq", 1)
     sums, last = lax.optimization_barrier((sums, last))
-    far_sums = flipped(sums, "seq", 4)
+    others = [flipped(sums, "seq", bits) for bits in (2, 4, 6)]
     ahead = jnp.concatenate([jnp.zeros_like(next_rows), next_rows], axis=0)
     added = last[16 - rim :]
     for k in range(rim):
@@ -605,7 +607,7 @@
         unpack_kernel,
         [((KCONV, channels), F32), ((channels,), F32), ((HEADS,), F32), ((HEADS,), F32)],
         [(params.shape, F32)],
-        sums, far_sums, limit=SMALL_LIMIT,
+        sums, *others, limit=SMALL_LIMIT,
     )
     return (grad_in[None], gsteps[None], grad_weight, grad_bias, grad_rates, grad_skip)
 

time: 141 us -> 140 us (level)
  waiting for transfers between devices: 29.1 us -> 26.8 us
  starting transfers between devices: 34.6 us -> 36.1 us
    ppermute x11, waiting for transfers between devices: 11.9 us -> 9.75 us  [flipped(): lax.ppermute(array, axis, [(i, i ^ bits) for i in range(lax.axis_size(axi...]
where the time goes in v10:
time: 140 us
  blocking collectives  38.6 us (28%)
  starting transfers between devices  36.1 us (26%)
  Pallas kernels  35.7 us (26%)
  waiting for transfers between devices  26.8 us (19%)
    all_to_all x1, blocking collectives, shards(): back = lax.all_to_all(turned, 'seq', 0, 0, tiled=True)  38.6 us
    pallas_call x8, Pallas kernels, call(): pl.pallas_call(kernel, out_shape=[out_space(*out) if large_out or i in ke...  35.7 us
    all_to_all x1, waiting for transfers between devices, shards(): got = lax.all_to_all(msg, 'seq', 0, 0, tiled=True)  17.1 us
    ppermute x11, starting transfers between devices, flipped(): lax.ppermute(array, axis, [(i, i ^ bits) for i in range(lax.axis_size(axi...  16.8 us
    all_to_all x1, starting transfers between devices, shards(): got = lax.all_to_all(msg, 'seq', 0, 0, tiled=True)  12 us
    ppermute x11, waiting for transfers between devices, flipped(): lax.ppermute(array, axis, [(i, i ^ bits) for i in range(lax.axis_size(axi...  9.75 us
    ppermute x2, starting transfers between devices, shifted(): return lax.ppermute(array, axis, pairs)  7.33 us
  transfers between devices with their start and end apart: 14, of which 8 were waited for; matrix products, arithmetic and copies ran while one was open for 1% of the time, Pallas kernels for 17%

profile of v10, /device:TPU:32, one launch (start us, length us, event | category | flops | bytes accessed | tf_op | source)
XLA Modules:
  0.0 140.0 jit_solution(3586860524275646265)
XLA Ops:
  0.6 0.8 slice_bitcast_fusion
  1.4 3.8 %collective-permute-start = (bf16[3,2816]{1,0:T(4,128)(2,1)S(1)}, bf16[3,2816]{1,0:T(4,128)(2,1)S(1)}, u32[]{:S(2)}, u32[]{:S(2)}) collective-permute-start(bf16[3,2816]{1,0:T(4,128)(2,1)S(1)} %slice_bitcast_fusion), channel_id=1, source_target_pairs={{0,1},{1,2},{2,3},{3,4},{4,5},{5,6},{6,7},{7,8},{8,9},{9,10},{10,1... | collective-permute-start | bytes 50696 | tf_op jit(solution)/shard_map/ppermute | solution.py:455
  5.3 2.4 %shard_map.118 = (bf16[2560,256]{1,0:T(8,128)(2,1)S(1)}, bf16[256,2816]{1,0:T(8,128)(2,1)S(1)}, f32[4,2816]{1,0:T(4,128)S(1)}, f32[2816]{0:T(1024)S(1)}, f32[40,256]{1,0:T(8,128)S(1)}, /*index=5*/f32[40,256]{1,0:T(8,128)S(1)}) custom-call(f32[40,256]{1,0:T(8,128)} %bitcast.11, f32[40]{0:T(128)} %rate_ref.3, bf16[256,2560]{1,0:T(8,128)(2,1)} %bitcast.17, ...), custom_call_target="tpu_custom_call" | custom-call | tf_op jit(solution)/shard_map/pallas_call | solution.py:439
  7.7 3.7 %shard_map.119 = bf16[32,168,128]{2,1,0:T(8,128)(2,1)} custom-call(bf16[3,2816]{1,0:T(4,128)(2,1)S(1)} %collective-permute-done.halo_ref, bf16[2560,256]{1,0:T(8,128)(2,1)S(1)} %get-tuple-element.50.dywt_ref, f32[40,256]{1,0:T(8,128)S(1)} %get-tuple-element.51.tail_ref, f32[40,256]{1,0:T(8,128)S(1)} %get-tuple-element.52.head_ref, ...), custom_call_target="tpu_custom_call" | custom-call | tf_op jit(solution)/shard_map/pallas_call | solution.py:439
  11.4 12.0 %all-to-all-start = ((bf16[32,168,128]{2,1,0:T(8,128)(2,1)}), bf16[32,168,128]{2,1,0:T(8,128)(2,1)S(1)}, u32[]{:S(2)}, u32[]{:S(2)}) async-start(bf16[32,168,128]{2,1,0:T(8,128)(2,1)} %shard_map.119), calls=%async_computation | async-start | bytes 2752512 | tf_op jit(solution)/shard_map/all_to_all | solution.py:513
  23.4 16.8 %shard_map.120 = (f32[256,2560]{1,0:T(8,128)}, bf16[256,2560]{1,0:T(8,128)(2,1)}, bf16[2560,256]{1,0:T(8,128)(2,1)}, bf16[2560,256]{1,0:T(8,128)(2,1)}, bf16[256...) custom-call(bf16[256,2816]{1,0:T(8,128)(2,1)} %bitcast.15, ...), custom_call_target="tpu_custom_call" | custom-call | tf_op jit(solution)/shard_map/pallas_call | solution.py:439
  40.3 17.1 %all-to-all-done.got_ref = bf16[32,168,128]{2,1,0:T(8,128)(2,1)S(1)} async-done(((bf16[32,168,128]{2,1,0:T(8,128)(2,1)}), bf16[32,168,128]{2,1,0:T(8,128)(2,1)S(1)}, u32[]{:S(2)}, u32[]{:S(2)}) %all-to-all-start) | async-done | bytes 1376288 | tf_op jit(solution)/shard_map/all_to_all | solution.py:513
  57.4 1.4 shard_map.121
  58.9 38.6 %all_to_all.10.back_ref = bf16[32,160,128]{2,1,0:T(8,128)(2,1)S(1)} all-to-all(bf16[32,160,128]{2,1,0:T(8,128)(2,1)} %shard_map.121), channel_id=1, replica_groups=mesh['dp'=8,'seq'=32] {'seq'}, dimensions={0} | all-to-all | bytes 2621440 | tf_op jit(solution)/shard_map/all_to_all | solution.py:551
  97.6 6.7 %shard_map.122 = (f32[256,2816]{1,0:T(8,128)S(1)}, f32[3,2816]{1,0:T(4,128)S(1)}, f32[40,256]{1,0:T(8,128)S(1)}, f32[40,256]{1,0:T(8,128)S(1)}, f32[40,128]{1,0:T(8,128)S(1)}, /*index=5*/f32[112,128]{1,0:T(8,128)S(1)}) custom-call(bf16[32,160,128]{2,1,0:T(8,128)(2,1)S(1)} %all_to_all.10.back_ref, bf16[256,256]{1,0:T(8,128)(2,1)S(1)} %copy-done.7, ...), custom_call_target="tpu_custom_call" | custom-call | tf_op jit(solution)/shard_map/pallas_call | solution.py:439
  104.4 1.2 collective-permute-done.1
  105.7 1.6 %collective-permute-start.2 = (f32[112,128]{1,0:T(8,128)S(1)}, f32[112,128]{1,0:T(8,128)S(1)}, u32[]{:S(2)}, u32[]{:S(2)}) collective-permute-start(f32[112,128]{1,0:T(8,128)S(1)} %add.35), channel_id=1, source_target_pairs={{0,64},{32,96},{64,0},{96,32},{128,192},{160,224},{192,128},{224,1... | collective-permute-start | bytes 172040 | tf_op jit(solution)/shard_map/ppermute | solution.py:459
  107.3 2.7 %collective-permute-start.3 = (f32[112,128]{1,0:T(8,128)S(1)}, f32[112,128]{1,0:T(8,128)S(1)}, u32[]{:S(2)}, u32[]{:S(2)}) collective-permute-start(f32[112,128]{1,0:T(8,128)S(1)} %add.35), channel_id=1, source_target_pairs={{0,128},{32,160},{64,192},{96,224},{128,0},{160,32},{192,64},{224,... | collective-permute-start | bytes 172040 | tf_op jit(solution)/shard_map/ppermute | solution.py:459
  110.0 0.5 collective-permute-start.4
  110.5 1.5 %shard_map.123 = f32[40,256]{1,0:T(8,128)} custom-call(f32[40,256]{1,0:T(8,128)S(1)} %get-tuple-element.75.q_ref, f32[40,256]{1,0:T(8,128)S(1)} %get-tuple-element.76.r_ref, f32[40,128]{1,0:T(8,128)S(1)} %get-tuple-element.77.four_ref, f32[40,256]{1,0:T(8,128)S(1)} %copy-done.5, f32[40,256]{1,0:T(8,128)S(1)} %copy-done.6, f32[40]{0:T(128)S(1)} %copy-done.14), custom_call_target="tpu_custom_call" | custom-call | tf_op jit(solution)/shard_map/pallas_call | solution.py:439
  112.0 1.1 collective-permute-done.3
  113.1 2.3 %collective-permute-done.4 = f32[112,128]{1,0:T(8,128)S(1)} collective-permute-done((f32[112,128]{1,0:T(8,128)S(1)}, f32[112,128]{1,0:T(8,128)S(1)}, u32[]{:S(2)}, u32[]{:S(2)}) %collective-permute-start.4) | collective-permute-done | bytes 57376 | tf_op jit(solution)/shard_map/ppermute | solution.py:459
  115.4 0.7 collective-permute-start.5
  116.1 2.0 %collective-permute-start.6 = (f32[112,128]{1,0:T(8,128)S(1)}, f32[112,128]{1,0:T(8,128)S(1)}, u32[]{:S(2)}, u32[]{:S(2)}) collective-permute-start(f32[112,128]{1,0:T(8,128)S(1)} %add_add_fusion.1), channel_id=1, source_target_pairs={{0,16},{1,17},{2,18},{3,19},{4,20},{5,21},{6,22},{7,23},{8,24},{9,... | collective-permute-start | bytes 172040 | tf_op jit(solution)/shard_map/ppermute | solution.py:459
  118.1 2.1 %collective-permute-start.7 = (f32[112,128]{1,0:T(8,128)S(1)}, f32[112,128]{1,0:T(8,128)S(1)}, u32[]{:S(2)}, u32[]{:S(2)}) collective-permute-start(f32[112,128]{1,0:T(8,128)S(1)} %add_add_fusion.1), channel_id=1, source_target_pairs={{0,24},{1,25},{2,26},{3,27},{4,28},{5,29},{6,30},{7,31},{8,16},{9,... | collective-permute-start | bytes 172040 | tf_op jit(solution)/shard_map/ppermute | solution.py:459
  120.2 2.5 %shard_map.124 = (bf16[256,2816]{1,0:T(8,128)(2,1)}, f32[16,2816]{1,0:T(8,128)S(1)}) custom-call(f32[256,2816]{1,0:T(8,128)S(1)} %get-tuple-element.81.gpre_ref, f32[4,2816]{1,0:T(4,128)S(1)} %copy-done), custom_call_target="tpu_custom_call" | custom-call | tf_op jit(solution)/shard_map/pallas_call | solution.py:439
  122.7 0.8 collective-permute-done.7
  123.5 0.5 collective-permute-start.8
  124.1 3.5 %collective-permute-start.9 = (f32[3,2816]{1,0:T(4,128)S(1)}, f32[3,2816]{1,0:T(4,128)S(1)}, u32[]{:S(2)}, u32[]{:S(2)}) collective-permute-start(f32[3,2816]{1,0:T(4,128)S(1)} %get-tuple-element.87), channel_id=1, source_target_pairs={{1,0},{2,1},{3,2},{4,3},{5,4},{6,5},{7,6},{8,7},{9,8},{10,9},{11,1... | collective-permute-start | bytes 101384 | tf_op jit(solution)/shard_map/ppermute | solution.py:455
  127.6 0.1 collective-permute-done.8
  127.8 1.5 %collective-permute-start.10 = (f32[112,128]{1,0:T(8,128)S(1)}, f32[112,128]{1,0:T(8,128)S(1)}, u32[]{:S(2)}, u32[]{:S(2)}) collective-permute-start(f32[112,128]{1,0:T(8,128)S(1)} %add.42.own_ref), channel_id=1, source_target_pairs={{0,2},{1,3},{2,0},{3,1},{4,6},{5,7},{6,4},{7,5},{8,10},{9,11},{10,... | collective-permute-start | bytes 172040 | tf_op jit(solution)/shard_map/ppermute | solution.py:459
  129.3 2.5 %collective-permute-start.11 = (f32[112,128]{1,0:T(8,128)S(1)}, f32[112,128]{1,0:T(8,128)S(1)}, u32[]{:S(2)}, u32[]{:S(2)}) collective-permute-start(f32[112,128]{1,0:T(8,128)S(1)} %add.42.own_ref), channel_id=1, source_target_pairs={{0,4},{1,5},{2,6},{3,7},{4,0},{5,1},{6,2},{7,3},{8,12},{9,13},{10,... | collective-permute-start | bytes 172040 | tf_op jit(solution)/shard_map/ppermute | solution.py:459
  131.8 2.6 %collective-permute-start.12 = (f32[112,128]{1,0:T(8,128)S(1)}, f32[112,128]{1,0:T(8,128)S(1)}, u32[]{:S(2)}, u32[]{:S(2)}) collective-permute-start(f32[112,128]{1,0:T(8,128)S(1)} %add.42.own_ref), channel_id=1, source_target_pairs={{0,6},{1,7},{2,4},{3,5},{4,2},{5,3},{6,0},{7,1},{8,14},{9,15},{10,... | collective-permute-start | bytes 172040 | tf_op jit(solution)/shard_map/ppermute | solution.py:459
  134.4 0.7 maximum_dynamic-update-slice_fusion
  135.1 2.3 %collective-permute-done.11.far_ref = f32[112,128]{1,0:T(8,128)S(1)} collective-permute-done((f32[112,128]{1,0:T(8,128)S(1)}, f32[112,128]{1,0:T(8,128)S(1)}, u32[]{:S(2)}, u32[]{:S(2)}) %collective-permute-start.11) | collective-permute-done | bytes 57376 | tf_op jit(solution)/shard_map/ppermute | solution.py:459
  137.4 1.9 %collective-permute-done.12.both_ref = f32[112,128]{1,0:T(8,128)S(1)} collective-permute-done((f32[112,128]{1,0:T(8,128)S(1)}, f32[112,128]{1,0:T(8,128)S(1)}, u32[]{:S(2)}, u32[]{:S(2)}) %collective-permute-start.12) | collective-permute-done | bytes 57376 | tf_op jit(solution)/shard_map/ppermute | solution.py:459
  139.3 0.7 shard_map.125
  (44 shorter events, 0.4 us)
Async XLA Ops:
  1.4 6.2 %collective-permute-start = (bf16[3,2816]{1,0:T(4,128)(2,1)S(1)}, bf16[3,2816]{1,0:T(4,128)(2,1)S(1)}, u32[]{:S(2)}, u32[]{:S(2)}) collective-permute-start(bf16[3,2816]{1,0:T(4,128)(2,1)S(1)} %slice_bitcast_fusion), channel_id=1, source_target_pairs={{0,1},{1,2},{2,3},{3,4},{4,5},{5,6},{6,7},{7,8},{8,9},{9,10},{10,1... | collective-permute-start | bytes 50696 | tf_op jit(solution)/shard_map/ppermute | solution.py:455
  7.7 3.7 %copy-start.3 = (bf16[3,2816]{1,0:T(4,128)(2,1)}, bf16[3,2816]{1,0:T(4,128)(2,1)S(1)}, u32[]{:S(2)}) copy-start(bf16[3,2816]{1,0:T(4,128)(2,1)S(1)} %collective-permute-done.halo_ref) | copy-start | bytes 50692
  11.4 46.0 %all-to-all-start = ((bf16[32,168,128]{2,1,0:T(8,128)(2,1)}), bf16[32,168,128]{2,1,0:T(8,128)(2,1)S(1)}, u32[]{:S(2)}, u32[]{:S(2)}) async-start(bf16[32,168,128]{2,1,0:T(8,128)(2,1)} %shard_map.119), calls=%async_computation | async-start | bytes 2752512 | tf_op jit(solution)/shard_map/all_to_all | solution.py:513
  58.8 38.7 %copy-start.1 = (f32[1,40,256]{2,1,0:T(8,128)S(1)}, f32[1,40,256]{2,1,0:T(8,128)}, u32[]{:S(2)}) copy-start(f32[1,40,256]{2,1,0:T(8,128)} %param.10) | copy-start | bytes 122884
  58.8 38.7 %copy-start.2 = (f32[256,256]{1,0:T(8,128)S(1)}, f32[256,256]{1,0:T(8,128)}, u32[]{:S(2)}) copy-start(f32[256,256]{1,0:T(8,128)} %get-tuple-element.60.slope_ref) | copy-start | bytes 786436
  58.8 38.7 %copy-start.4 = (bf16[3,2816]{1,0:T(4,128)(2,1)S(1)}, bf16[3,2816]{1,0:T(4,128)(2,1)}, u32[]{:S(2)}) copy-start(bf16[3,2816]{1,0:T(4,128)(2,1)} %copy-done.3) | copy-start | bytes 50692
  58.8 38.7 %copy-start.5 = (f32[40,256]{1,0:T(8,128)S(1)}, f32[40,256]{1,0:T(8,128)}, u32[]{:S(2)}) copy-start(f32[40,256]{1,0:T(8,128)} %get-tuple-element.63.colin_ref.col_ref) | copy-start | bytes 122884
  58.8 38.7 %copy-start.6 = (f32[40,256]{1,0:T(8,128)S(1)}, f32[40,256]{1,0:T(8,128)}, u32[]{:S(2)}) copy-start(f32[40,256]{1,0:T(8,128)} %get-tuple-element.64.row_ref) | copy-start | bytes 122884
  58.8 38.7 %copy-start.7 = (bf16[256,256]{1,0:T(8,128)(2,1)S(1)}, bf16[256,256]{1,0:T(8,128)(2,1)}, u32[]{:S(2)}) copy-start(bf16[256,256]{1,0:T(8,128)(2,1)} %get-tuple-element.58.bc_ref) | copy-start | bytes 393220
  58.8 38.7 %copy-start.8 = (bf16[256,256]{1,0:T(8,128)(2,1)S(1)}, bf16[256,256]{1,0:T(8,128)(2,1)}, u32[]{:S(2)}) copy-start(bf16[256,256]{1,0:T(8,128)(2,1)} %get-tuple-element.59.bct_ref) | copy-start | bytes 393220
  58.8 38.7 %copy-start.9 = (f32[128,256]{1,0:T(8,128)S(1)}, f32[128,256]{1,0:T(8,128)}, u32[]{:S(2)}) copy-start(f32[128,256]{1,0:T(8,128)} %get-tuple-element.61.gbin_ref) | copy-start | bytes 393220
  58.9 38.7 %copy-start.10 = (f32[128,256]{1,0:T(8,128)S(1)}, f32[128,256]{1,0:T(8,128)}, u32[]{:S(2)}) copy-start(f32[128,256]{1,0:T(8,128)} %get-tuple-element.62.gcin_ref) | copy-start | bytes 393220
  58.9 38.7 %copy-start.11 = (f32[40,256]{1,0:T(8,128)S(1)}, f32[40,256]{1,0:T(8,128)}, u32[]{:S(2)}) copy-start(f32[40,256]{1,0:T(8,128)} %get-tuple-element.65.skiprow_ref) | copy-start | bytes 122884
  58.9 38.7 %copy-start.12 = (f32[40,256]{1,0:T(8,128)S(1)}, f32[40,256]{1,0:T(8,128)}, u32[]{:S(2)}) copy-start(f32[40,256]{1,0:T(8,128)} %get-tuple-element.66.sofar_ref) | copy-start | bytes 122884
  58.9 38.7 %copy-start.13 = (f32[40,128]{1,0:T(8,128)S(1)}, f32[40,128]{1,0:T(8,128)}, u32[]{:S(2)}) copy-start(f32[40,128]{1,0:T(8,128)} %get-tuple-element.67.end_ref) | copy-start | bytes 61444
  97.6 12.9 %copy-start.14 = (f32[40]{0:T(128)S(1)}, f32[40]{0:T(128)}, u32[]{:S(2)}) copy-start(f32[40]{0:T(128)} %rate_ref.3) | copy-start | bytes 484
  97.6 22.6 %copy-start = (f32[4,2816]{1,0:T(4,128)S(1)}, f32[4,2816]{1,0:T(4,128)}, u32[]{:S(2)}) copy-start(f32[4,2816]{1,0:T(4,128)} %w_ref.3) | copy-start | bytes 135172
  104.3 1.3 collective-permute-start.1
  105.7 6.3 %collective-permute-start.2 = (f32[112,128]{1,0:T(8,128)S(1)}, f32[112,128]{1,0:T(8,128)S(1)}, u32[]{:S(2)}, u32[]{:S(2)}) collective-permute-start(f32[112,128]{1,0:T(8,128)S(1)} %add.35), channel_id=1, source_target_pairs={{0,64},{32,96},{64,0},{96,32},{128,192},{160,224},{192,128},{224,1... | collective-permute-start | bytes 172040 | tf_op jit(solution)/shard_map/ppermute | solution.py:459
  107.3 5.9 %collective-permute-start.3 = (f32[112,128]{1,0:T(8,128)S(1)}, f32[112,128]{1,0:T(8,128)S(1)}, u32[]{:S(2)}, u32[]{:S(2)}) collective-permute-start(f32[112,128]{1,0:T(8,128)S(1)} %add.35), channel_id=1, source_target_pairs={{0,128},{32,160},{64,192},{96,224},{128,0},{160,32},{192,64},{224,... | collective-permute-start | bytes 172040 | tf_op jit(solution)/shard_map/ppermute | solution.py:459
  110.0 5.4 %collective-permute-start.4 = (f32[112,128]{1,0:T(8,128)S(1)}, f32[112,128]{1,0:T(8,128)S(1)}, u32[]{:S(2)}, u32[]{:S(2)}) collective-permute-start(f32[112,128]{1,0:T(8,128)S(1)} %add.35), channel_id=1, source_target_pairs={{0,192},{32,224},{64,128},{96,160},{128,64},{160,96},{192,0},{224,... | collective-permute-start | bytes 172040 | tf_op jit(solution)/shard_map/ppermute | solution.py:459
  115.4 7.3 %collective-permute-start.5 = (f32[112,128]{1,0:T(8,128)S(1)}, f32[112,128]{1,0:T(8,128)S(1)}, u32[]{:S(2)}, u32[]{:S(2)}) collective-permute-start(f32[112,128]{1,0:T(8,128)S(1)} %add_add_fusion.1), channel_id=1, source_target_pairs={{0,8},{1,9},{2,10},{3,11},{4,12},{5,13},{6,14},{7,15},{8,0},{9,1},... | collective-permute-start | bytes 172040 | tf_op jit(solution)/shard_map/ppermute | solution.py:459
  116.1 6.6 %collective-permute-start.6 = (f32[112,128]{1,0:T(8,128)S(1)}, f32[112,128]{1,0:T(8,128)S(1)}, u32[]{:S(2)}, u32[]{:S(2)}) collective-permute-start(f32[112,128]{1,0:T(8,128)S(1)} %add_add_fusion.1), channel_id=1, source_target_pairs={{0,16},{1,17},{2,18},{3,19},{4,20},{5,21},{6,22},{7,23},{8,24},{9,... | collective-permute-start | bytes 172040 | tf_op jit(solution)/shard_map/ppermute | solution.py:459
  118.1 5.4 %collective-permute-start.7 = (f32[112,128]{1,0:T(8,128)S(1)}, f32[112,128]{1,0:T(8,128)S(1)}, u32[]{:S(2)}, u32[]{:S(2)}) collective-permute-start(f32[112,128]{1,0:T(8,128)S(1)} %add_add_fusion.1), channel_id=1, source_target_pairs={{0,24},{1,25},{2,26},{3,27},{4,28},{5,29},{6,30},{7,31},{8,16},{9,... | collective-permute-start | bytes 172040 | tf_op jit(solution)/shard_map/ppermute | solution.py:459
  123.5 4.3 %collective-permute-start.8 = (f32[112,128]{1,0:T(8,128)S(1)}, f32[112,128]{1,0:T(8,128)S(1)}, u32[]{:S(2)}, u32[]{:S(2)}) collective-permute-start(f32[112,128]{1,0:T(8,128)S(1)} %add_add_fusion), channel_id=1, source_target_pairs={{0,1},{1,0},{2,3},{3,2},{4,5},{5,4},{6,7},{7,6},{8,9},{9,8},{10,11... | collective-permute-start | bytes 172040 | tf_op jit(solution)/shard_map/ppermute | solution.py:459
  124.1 10.3 %collective-permute-start.9 = (f32[3,2816]{1,0:T(4,128)S(1)}, f32[3,2816]{1,0:T(4,128)S(1)}, u32[]{:S(2)}, u32[]{:S(2)}) collective-permute-start(f32[3,2816]{1,0:T(4,128)S(1)} %get-tuple-element.87), channel_id=1, source_target_pairs={{1,0},{2,1},{3,2},{4,3},{5,4},{6,5},{7,6},{8,7},{9,8},{10,9},{11,1... | collective-permute-start | bytes 101384 | tf_op jit(solution)/shard_map/ppermute | solution.py:455
  127.8 7.3 %collective-permute-start.10 = (f32[112,128]{1,0:T(8,128)S(1)}, f32[112,128]{1,0:T(8,128)S(1)}, u32[]{:S(2)}, u32[]{:S(2)}) collective-permute-start(f32[112,128]{1,0:T(8,128)S(1)} %add.42.own_ref), channel_id=1, source_target_pairs={{0,2},{1,3},{2,0},{3,1},{4,6},{5,7},{6,4},{7,5},{8,10},{9,11},{10,... | collective-permute-start | bytes 172040 | tf_op jit(solution)/shard_map/ppermute | solution.py:459
  129.3 8.1 %collective-permute-start.11 = (f32[112,128]{1,0:T(8,128)S(1)}, f32[112,128]{1,0:T(8,128)S(1)}, u32[]{:S(2)}, u32[]{:S(2)}) collective-permute-start(f32[112,128]{1,0:T(8,128)S(1)} %add.42.own_ref), channel_id=1, source_target_pairs={{0,4},{1,5},{2,6},{3,7},{4,0},{5,1},{6,2},{7,3},{8,12},{9,13},{10,... | collective-permute-start | bytes 172040 | tf_op jit(solution)/shard_map/ppermute | solution.py:459
  131.8 7.5 %collective-permute-start.12 = (f32[112,128]{1,0:T(8,128)S(1)}, f32[112,128]{1,0:T(8,128)S(1)}, u32[]{:S(2)}, u32[]{:S(2)}) collective-permute-start(f32[112,128]{1,0:T(8,128)S(1)} %add.42.own_ref), channel_id=1, source_target_pairs={{0,6},{1,7},{2,4},{3,5},{4,2},{5,3},{6,0},{7,1},{8,14},{9,15},{10,... | collective-permute-start | bytes 172040 | tf_op jit(solution)/shard_map/ppermute | solution.py:459
